TPU v7x, 512 devices: a whole 4x8x8 slice. The times are simulated.
512 devices in a mesh: fsdp: 64 (over z, y), tp: 8 (over x, core).
Axes of the slice: x: 4, y: 8, z: 8, core: 2. Of those that a mesh axis runs over, the one named last changes fastest.
Arguments:
- momentum: bfloat16 [8192, 26624], P('fsdp', 'tp'), may hold values from -6 to 6
- gradient: bfloat16 [8192, 26624], P('fsdp', 'tp'), may hold values from -150 to 150
- right_factor: bfloat16 [256, 26624], P('fsdp', 'tp'), may hold values from -0.0390625 to 0.0390625
Outputs:
- momentum_next: bfloat16 [8192, 26624], P('fsdp', 'tp')
- factor_next: float32 [256, 26624], P('fsdp', 'tp')
- update: bfloat16 [8192, 26624], P('fsdp', 'tp')
All inputs are finite; a program needn't handle non-finite values.
Results may differ from a plain program's by a relative error of at most 0.012.
Values may be sent and summed in bfloat16 or wider, within the bound.
No kernel may reach another device: no remote copies, remote signals or barrier semaphores. Data moves between devices by JAX's collectives and lax.ppermute only.
A program may use at most 64 MiB of HBM per device.

v0:
```python
import math

import jax
import jax.numpy as jnp
from jax import lax
from jax.sharding import PartitionSpec as P

EPSILON = 1e-06
MOMENTUM_DECAY = 0.95


def orthonormal(raw_rows, gram_matrix):
    factor_lower = jnp.linalg.cholesky(gram_matrix)
    solved = lax.linalg.triangular_solve(
        factor_lower, raw_rows, left_side=False, lower=True, transpose_a=True
    )
    return solved.astype(jnp.bfloat16)


def local_gram(raw_rows):
    return jnp.dot(raw_rows.T, raw_rows, precision=lax.Precision.HIGHEST)


def body(momentum, gradient, right_factor):
    blended = (momentum.astype(jnp.float32) + gradient.astype(jnp.float32)).astype(jnp.bfloat16)
    share_rank = right_factor.shape[0]
    partial_basis = lax.dot_general(
        blended,
        lax.all_gather(right_factor, "fsdp", axis=0, tiled=True),
        (((1,), (1,)), ((), ())),
        preferred_element_type=jnp.float32,
    )
    raw_basis = lax.psum(partial_basis, "tp")
    gram_matrix = lax.psum(local_gram(raw_basis), "fsdp")
    ortho_basis = orthonormal(raw_basis, gram_matrix)
    partial_proj = lax.dot_general(
        ortho_basis, blended, (((0,), (0,)), ((), ())), preferred_element_type=jnp.float32
    )
    projection = lax.psum(partial_proj, "fsdp")
    squares = lax.psum(jnp.sum(projection * projection, axis=1), "tp")
    factor_full = projection / (jnp.sqrt(squares)[:, None] + EPSILON)
    proj_rounded = projection.astype(jnp.bfloat16)
    factor_rounded = factor_full.astype(jnp.bfloat16)
    factor_next = lax.dynamic_slice_in_dim(
        factor_full, lax.axis_index("fsdp") * share_rank, share_rank, 0
    )
    carried = jnp.dot(ortho_basis, proj_rounded, preferred_element_type=jnp.float32)
    momentum_next = (blended.astype(jnp.float32) - (1.0 - MOMENTUM_DECAY) * carried).astype(
        jnp.bfloat16
    )
    total_rows = blended.shape[0] * lax.axis_size("fsdp")
    total_cols = blended.shape[1] * lax.axis_size("tp")
    total_rank = ortho_basis.shape[1]
    scale_factor = math.sqrt(total_rows * total_cols / total_rank)
    direction = jnp.dot(ortho_basis, factor_rounded, preferred_element_type=jnp.float32)
    update = (scale_factor * direction).astype(jnp.bfloat16)
    return (momentum_next, factor_next, update)


def solution(mesh):
    placed = (P("fsdp", "tp"), P("fsdp", "tp"), P("fsdp", "tp"))
    return jax.shard_map(
        body,
        mesh=mesh,
        in_specs=placed,
        out_specs=(P("fsdp", "tp"), P("fsdp", "tp"), P("fsdp", "tp")),
        check_vma=False,
    )
```

profile of v0, /device:TPU:1, one launch (start us, length us, event | category | flops | bytes accessed | tf_op | source)
XLA Modules:
  0.0 580.9 jit_solution(5327222077035669731)
XLA Ops:
  7.2 0.0 all-gather.3.cloned.1.call-start
  7.2 0.7 all-gather.3.cloned.1.call-update
  7.9 0.0 copy-start.1
  7.9 0.0 copy-start.3
  7.9 0.0 all-reduce.5.cloned.1.call-start
  8.0 87.3 %all-gather.3.cloned.1.call-done = bf16[64,4,3328]{2,1,0:T(4,128)(2,1)} async-done(((bf16[1,4,3328]{2,1,0:T(4,128)(2,1)}), bf16[64,4,3328]{2,1,0:T(4,128)(2,1)}) %all-gather.3.cloned.1.call-update) | async-done | bytes 1703952 | tf_op jit(solution)/shard_map/all_gather | solution.py:29
  95.3 2.9 reshape.45
  98.1 0.0 copy-done.1
  98.2 0.0 copy-done.3
  98.2 1.4 fusion.16
  99.5 0.0 all-reduce.5.cloned.1.call-update
  99.6 0.0 all-reduce.7.cloned.1.call-start
  99.6 69.8 %all-reduce.5.cloned.1.call-done = f32[128,256]{1,0:T(8,128)} async-done(((f32[128,256]{1,0:T(8,128)}), f32[128,256]{1,0:T(8,128)}) %all-reduce.5.cloned.1.call-update) | async-done | bytes 131088 | tf_op jit(solution)/shard_map/psum | solution.py:33
  169.4 2.1 fusion.19
  171.5 0.0 all-reduce.7.cloned.1.call-update
  171.5 0.0 all-reduce.9.cloned.1.call-start
  171.6 150.4 %all-reduce.7.cloned.1.call-done = f32[256,256]{0,1:T(8,128)} async-done(((f32[256,256]{0,1:T(8,128)}), f32[256,256]{0,1:T(8,128)}) %all-reduce.7.cloned.1.call-update) | async-done | bytes 262160 | tf_op jit(solution)/shard_map/psum | solution.py:34
  321.9 1.1 copy.9
  323.0 0.0 copy-start.5
  323.0 1.0 fusion.5
  324.1 11.7 %cholesky.50 = f32[128,128]{1,0:T(8,128)S(1)} custom-call(f32[128,128]{1,0:T(8,128)S(1)} %cholesky.118), custom_call_target="Cholesky" | custom-call | tf_op jit(solution)/shard_map/jit(cholesky)/cholesky | solution.py:13
  335.8 9.8 %custom-call.14 = f32[1,128,128]{1,2,0:T(8,128)S(1)} custom-call(f32[1,128,128]{2,1,0:T(8,128)S(1)} %get-tuple-element.24), custom_call_target="InvertDiagBlocksLowerTriangular" | custom-call | tf_op jit(solution)/shard_map/jit(cholesky)/cholesky | solution.py:13
  345.7 0.2 constant_dynamic-update-slice_fusion
  345.9 0.3 convolution_subtract_fusion.1
  346.1 11.7 %cholesky.105 = f32[128,128]{1,0:T(8,128)S(1)} custom-call(f32[128,128]{1,0:T(8,128)S(1)} %convolution_subtract_fusion.1), custom_call_target="Cholesky" | custom-call | tf_op jit(solution)/shard_map/jit(cholesky)/cholesky | solution.py:13
  357.9 0.6 compare_reduce_fusion
  359.9 0.1 triangular_solve.58
  359.9 4.1 while.1
  360.1 0.6 fusion.28
  360.7 1.4 bitcast_dynamic-update-slice_fusion.2
  362.1 0.6 fusion.28
  362.7 1.4 bitcast_dynamic-update-slice_fusion.2
  364.1 19.7 %custom-call.15 = f32[2,128,128]{1,2,0:T(8,128)S(1)} custom-call(f32[2,128,128]{2,1,0:T(8,128)S(1)} %get-tuple-element.10), custom_call_target="InvertDiagBlocksLowerTriangular" | custom-call | tf_op jit(solution)/shard_map/triangular_solve | solution.py:14
  383.8 0.0 copy-done.5
  383.8 0.3 fusion.18
  384.1 0.3 convolution_subtract_fusion
  384.4 0.3 convolution_convert_fusion
  384.7 2.4 fusion.12
  387.0 0.0 all-reduce.9.cloned.1.call-update
  387.1 164.6 %all-reduce.9.cloned.1.call-done = f32[256,3328]{1,0:T(8,128)} async-done(((f32[256,3328]{1,0:T(8,128)}), f32[256,3328]{1,0:T(8,128)}) %all-reduce.9.cloned.1.call-update) | async-done | bytes 3407888 | tf_op jit(solution)/shard_map/psum | solution.py:39
  551.6 0.0 copy-start
  551.6 2.4 multiply_reduce_fusion
  554.1 16.5 %psum.31 = f32[256]{0:T(256)S(1)} all-reduce(f32[256]{0:T(256)S(1)} %multiply_reduce_fusion), channel_id=1, replica_groups=mesh['fsdp'=64,'tp'=8] {'tp'}, use_global_device_ids=true, to_apply=%region_8.9 | all-reduce | flops 256 | bytes 2048 | tf_op jit(solution)/shard_map/psum | solution.py:40
  570.5 0.0 copy-done
  570.5 0.3 broadcast_divide_fusion
  570.8 0.0 copy-start.2
  570.9 0.0 copy-start.4
  570.9 1.3 fusion.2
  572.2 0.6 constant_dynamic-slice_fusion.1
  572.8 0.0 copy-done.2
  572.8 0.0 copy-done.4
  572.8 1.6 fusion.1
  (10 shorter events, 0.2 us)
Async XLA Ops:
  7.2 88.1 %all-gather.3.cloned.1.call-start = ((), (), s32[]{:S(2)}) async-start(), calls=%async_computation.3 | async-start | bytes 1730560 | tf_op jit(solution)/shard_map/all_gather | solution.py:29
  7.9 90.2 %copy-start.1 = (bf16[128,3328]{1,0:T(8,128)(2,1)S(1)}, bf16[128,3328]{1,0:T(8,128)(2,1)}, u32[]{:S(2)}) copy-start(bf16[128,3328]{1,0:T(8,128)(2,1)} %param.4) | copy-start | bytes 2555908
  7.9 90.2 %copy-start.3 = (bf16[128,3328]{1,0:T(8,128)(2,1)S(1)}, bf16[128,3328]{1,0:T(8,128)(2,1)}, u32[]{:S(2)}) copy-start(bf16[128,3328]{1,0:T(8,128)(2,1)} %param.3) | copy-start | bytes 2555908
  7.9 161.5 %all-reduce.5.cloned.1.call-start = ((), (), s32[]{:S(2)}) async-start(), calls=%async_computation | async-start | bytes 262144 | tf_op jit(solution)/shard_map/psum | solution.py:33
  99.6 222.4 %all-reduce.7.cloned.1.call-start = ((), (), s32[]{:S(2)}) async-start(), calls=%async_computation.1 | async-start | bytes 524288 | tf_op jit(solution)/shard_map/psum | solution.py:34
  171.5 380.2 %all-reduce.9.cloned.1.call-start = ((), (), s32[]{:S(2)}) async-start(), calls=%async_computation.2 | async-start | bytes 6815744 | tf_op jit(solution)/shard_map/psum | solution.py:39
  323.0 60.7 %copy-start.5 = (f32[128,256]{1,0:T(8,128)S(1)}, f32[128,256]{1,0:T(8,128)}, u32[]{:S(2)}) copy-start(f32[128,256]{1,0:T(8,128)} %all-reduce.5.cloned.1.call-done) | copy-start | bytes 393220
  551.6 18.9 %copy-start = (f32[256,3328]{1,0:T(8,128)S(1)}, f32[256,3328]{1,0:T(8,128)}, u32[]{:S(2)}) copy-start(f32[256,3328]{1,0:T(8,128)} %all-reduce.9.cloned.1.call-done) | copy-start | bytes 10223620
  570.8 2.0 copy-start.2
  570.9 2.0 copy-start.4
Sparse Core Ops, SparseCore 0:
  11.0 84.2 all-gather.2
  99.7 69.6 all-reduce.4
  173.5 148.4 all-reduce.6
  387.2 164.4 all-reduce.8
where the time goes:
time: 581 us
  waiting for transfers between devices  473 us (81%)
  other arithmetic  57.4 us (10%)
  blocking collectives  16.5 us (3%)
  between operations  15.3 us (3%)
  matrix products  10.1 us (2%)
  local copies, waits for them, and re-layouts  8.64 us (1%)
    psum x1, waiting for transfers between devices, body(): projection = lax.psum(partial_proj, 'fsdp')  165 us
    psum x1, waiting for transfers between devices, body(): gram_matrix = lax.psum(local_gram(raw_basis), 'fsdp')  150 us
    all_gather x1, waiting for transfers between devices, body(): lax.all_gather(right_factor, 'fsdp', axis=0, tiled=True)  87.3 us
    psum x1, waiting for transfers between devices, body(): raw_basis = lax.psum(partial_basis, 'tp')  69.8 us
    another operation x6, other arithmetic, orthonormal(): factor_lower = jnp.linalg.cholesky(gram_matrix)  33.9 us
    another operation x3, other arithmetic, orthonormal(): lax.linalg.triangular_solve(factor_lower, raw_rows, left_side=False, lowe...  19.7 us
    psum x1, blocking collectives, body(): squares = lax.psum(jnp.sum(projection * projection, axis=1), 'tp')  16.5 us
  transfers between devices with their start and end apart: 4, of which 4 were waited for; matrix products, arithmetic and copies ran while one was open for 0% of the time, Pallas kernels for 0%

commit v1 on v0

v1 whole, which is shorter than its diff:
```python
import functools
import math

import jax
import jax.numpy as jnp
from jax import lax
from jax.experimental import pallas as pl
from jax.experimental.pallas import tpu as pltpu
from jax.sharding import Mesh, PartitionSpec as P

EPSILON = 1e-06
MOMENTUM_DECAY = 0.95
HIGHEST = lax.Precision.HIGHEST

ROWS_OVER = ("z", "y")
COLS_OVER = ("x", "core")
GRID = {"z": 8, "y": 8, "x": 4, "core": 2}
GROUPS = 64
CHUNK = 56

FACTOR_BLOCK = 64
FACTOR_GROUP = 8


def block_inverse(block, size):
    lane = lax.broadcasted_iota(jnp.int32, (size, 128), 1)
    sub = lax.broadcasted_iota(jnp.int32, (size, 128), 0)
    eye = (lane == sub + size).astype(jnp.float32)
    if 2 * size == 128:
        work = jnp.concatenate([block, jnp.zeros_like(block)], axis=1) + eye
    else:
        work = jnp.concatenate([block, jnp.zeros((size, 128 - size), jnp.float32)], axis=1) + eye
    pivots = jnp.ones((size, 128), jnp.float32)
    for start in range(0, size, FACTOR_GROUP):
        columns = [
            jnp.broadcast_to(work[:, j : j + 1], (size, 128))
            for j in range(start, start + FACTOR_GROUP)
        ]
        for c in range(FACTOR_GROUP):
            j = start + c
            pivot = jnp.broadcast_to(columns[c][j : j + 1, :], (size, 128))
            ratio = jnp.where(sub > j, columns[c] * (1.0 / pivot), 0.0)
            pivots = jnp.where(sub == j, pivot, pivots)
            work = work - ratio * jnp.broadcast_to(work[j : j + 1, :], (size, 128))
            for later in range(c + 1, FACTOR_GROUP):
                columns[later] = columns[later] - ratio * jnp.broadcast_to(
                    columns[later][j : j + 1, :], (size, 128)
                )
    work = work * lax.rsqrt(pivots)
    return work[:, size : 2 * size]


def factor_kernel(gram_ref, inverse_ref, *, size):
    inverse_ref[...] = gram_ref[...]
    step = FACTOR_BLOCK
    for k in range(0, size, step):
        after = k + step
        inverse = block_inverse(inverse_ref[k:after, k:after], step)
        panel = jnp.dot(
            inverse, inverse_ref[k:after, :], precision=HIGHEST, preferred_element_type=jnp.float32
        )
        pieces = [inverse]
        if k > 0:
            pieces = [panel[:, :k]] + pieces
        if after < size:
            pieces = pieces + [panel[:, after:]]
            lower = lax.dot_general(
                inverse_ref[after:, k:after],
                inverse,
                (((1,), (1,)), ((), ())),
                precision=HIGHEST,
                preferred_element_type=jnp.float32,
            )
        panel = jnp.concatenate(pieces, axis=1)
        inverse_ref[k:after, :] = panel
        if after < size:
            inverse_ref[after:, k:after] = jnp.zeros((size - after, step), jnp.float32)
            inverse_ref[after:, :] = inverse_ref[after:, :] - jnp.dot(
                lower, panel, precision=HIGHEST, preferred_element_type=jnp.float32
            )
    row = lax.broadcasted_iota(jnp.int32, (size, size), 0)
    col = lax.broadcasted_iota(jnp.int32, (size, size), 1)
    inverse_ref[...] = jnp.where(row >= col, inverse_ref[...], 0.0)


def inverse_factor(gram):
    size = gram.shape[0]
    return pl.pallas_call(
        functools.partial(factor_kernel, size=size),
        out_shape=jax.ShapeDtypeStruct((size, size), jnp.float32),
        in_specs=[pl.BlockSpec(memory_space=pltpu.VMEM)],
        out_specs=pl.BlockSpec(memory_space=pltpu.VMEM),
        compiler_params=pltpu.CompilerParams(vmem_limit_bytes=32 << 20),
        cost_estimate=pl.CostEstimate(flops=10**9, bytes_accessed=1 << 19, transcendentals=512),
        name="inverse_factor",
    )(gram)


def spread(block, axes, parts):
    copies = jnp.broadcast_to(block[None], (parts,) + block.shape)
    return lax.all_to_all(copies, axes, 0, 0, tiled=True)


def nt_dot(a, b, precision=None):
    return lax.dot_general(
        a, b, (((1,), (1,)), ((), ())), precision=precision, preferred_element_type=jnp.float32
    )


def body(momentum, gradient, right_factor):
    rows, cols = momentum.shape
    share_rank = right_factor.shape[0]
    rank = share_rank * GROUPS
    padded = GROUPS * CHUNK
    blended = (momentum.astype(jnp.float32) + gradient.astype(jnp.float32)).astype(jnp.bfloat16)
    with jax.named_scope("factor_gather"):
        whole_factor = spread(right_factor, ROWS_OVER, GROUPS).reshape(rank, cols)
    with jax.named_scope("basis"):
        basis = nt_dot(blended, whole_factor)
        basis = jnp.sum(spread(basis, "core", GRID["core"]), axis=0)
        basis = jnp.sum(spread(basis, "x", GRID["x"]), axis=0)
    with jax.named_scope("cross"):
        high = basis.astype(jnp.bfloat16)
        low = (basis - high.astype(jnp.float32)).astype(jnp.bfloat16)
        wide = jnp.pad(blended, ((0, 0), (0, padded - cols)))
        cross = lax.dot_general(
            jnp.concatenate([wide, wide], axis=0),
            jnp.concatenate([high, low], axis=0),
            (((0,), (0,)), ((), ())),
            preferred_element_type=jnp.float32,
        )
        cross = lax.psum_scatter(cross, "z", scatter_dimension=0, tiled=True)
    with jax.named_scope("gram"):
        gram = jnp.dot(basis.T, basis, precision=HIGHEST)
        gram = lax.all_to_all(
            gram.reshape(GROUPS, share_rank, rank), ROWS_OVER, 0, 0, tiled=True
        )
        gram = spread(jnp.sum(gram, axis=0), ROWS_OVER, GROUPS).reshape(rank, rank)
    with jax.named_scope("solve"):
        inverse = inverse_factor(gram)
        cross, inverse = lax.optimization_barrier((cross, inverse))
        ortho_basis = nt_dot(basis, inverse, HIGHEST).astype(jnp.bfloat16)
    with jax.named_scope("projection"):
        cross = lax.all_to_all(
            cross.reshape(GRID["y"], CHUNK, rank), "y", 0, 0, tiled=True
        )
        own = nt_dot(jnp.sum(cross, axis=0), inverse, HIGHEST).astype(jnp.bfloat16)
        projection = spread(own, ROWS_OVER, GROUPS).reshape(padded, rank)[:cols]
    with jax.named_scope("norms"):
        wide_proj = projection.astype(jnp.float32)
        squares = jnp.sum(wide_proj * wide_proj, axis=0)[None]
        squares = jnp.sum(spread(squares, COLS_OVER, GRID["x"] * GRID["core"]), axis=0)
        inverse_norms = 1.0 / (jnp.sqrt(squares) + EPSILON)
    with jax.named_scope("outputs"):
        carried = nt_dot(ortho_basis, projection)
        momentum_next = (blended.astype(jnp.float32) - (1.0 - MOMENTUM_DECAY) * carried).astype(
            jnp.bfloat16
        )
        scale_factor = math.sqrt(rows * GROUPS * cols * GRID["x"] * GRID["core"] / rank)
        scaled = (wide_proj * inverse_norms).astype(jnp.bfloat16)
        update = (scale_factor * nt_dot(ortho_basis, scaled)).astype(jnp.bfloat16)
        first = lax.axis_index(ROWS_OVER) * share_rank
        own_rank = first + lax.broadcasted_iota(jnp.int32, (share_rank, rank), 0)
        pick = own_rank == lax.broadcasted_iota(jnp.int32, (share_rank, rank), 1)
        own_norms = jnp.sum(jnp.where(pick, inverse_norms, 0.0), axis=1, keepdims=True)
        factor_next = nt_dot(pick.astype(jnp.bfloat16), projection) * own_norms
    return (momentum_next, factor_next, update)


def solution(mesh):
    chips = Mesh(mesh.devices.reshape(tuple(GRID.values())), tuple(GRID))
    placed = P(ROWS_OVER, COLS_OVER)
    return jax.shard_map(
        body,
        mesh=chips,
        in_specs=(placed, placed, placed),
        out_specs=(placed, placed, placed),
        check_vma=False,
    )
```

time: 581 us -> 250 us (0.43)
  waiting for transfers between devices: 473 us -> 107 us
  other arithmetic: 57.4 us -> 2.24 us
  blocking collectives: 16.5 us -> 65.4 us
  starting transfers between devices: 0.16 us -> 34 us
  Pallas kernels: 0 us -> 9.43 us
    psum x3 -> x0, waiting for transfers between devices: 385 us -> none  [the longest x1 165 us: body(): projection = lax.psum(partial_proj, 'fsdp')]
    all_to_all x0 -> x4, waiting for transfers between devices: none -> 95.9 us  [spread(): return lax.all_to_all(copies, axes, 0, 0, tiled=True)]
    all_gather x1 -> x0, waiting for transfers between devices: 87.3 us -> none  [body(): lax.all_gather(right_factor, 'fsdp', axis=0, tiled=True)]
    all_to_all x0 -> x4, blocking collectives: none -> 65.4 us  [the longest x2 25.3 us: spread(): return lax.all_to_all(copies, axes, 0, 0, tiled=True)]
    another operation x9 -> x0, other arithmetic: 53.7 us -> none  [the longest x6 33.9 us: orthonormal(): factor_lower = jnp.linalg.cholesky(gram_matrix)]
    all_to_all x0 -> x4, starting transfers between devices: none -> 34 us  [spread(): return lax.all_to_all(copies, axes, 0, 0, tiled=True)]
    psum x1 -> x0, blocking collectives: 16.5 us -> none  [body(): squares = lax.psum(jnp.sum(projection * projection, axis=1), 'tp')]
    reduce_scatter x0 -> x1, waiting for transfers between devices: none -> 11 us  [body(): cross = lax.psum_scatter(cross, 'z', scatter_dimension=0, tiled=True)]
  transfers between devices with their start and end apart: 4 -> 5, of which waited for: 4 -> 5; matrix products, arithmetic and copies ran while one was open for 0% -> 2% of each run, Pallas kernels for 0% -> 4%
where the time goes in v1:
time: 250 us; the launch traced here: 249 us
  waiting for transfers between devices  107 us (43%)
  blocking collectives  65.4 us (26%)
  starting transfers between devices  34 us (14%)
  between operations  14.2 us (6%)
  matrix products  10.2 us (4%)
  Pallas kernels  9.43 us (4%)
  local copies, waits for them, and re-layouts  7.04 us (3%)
    all_to_all x4, waiting for transfers between devices, spread(): return lax.all_to_all(copies, axes, 0, 0, tiled=True)  95.9 us
    all_to_all x4, starting transfers between devices, spread(): return lax.all_to_all(copies, axes, 0, 0, tiled=True)  34 us
    all_to_all x2, blocking collectives, spread(): return lax.all_to_all(copies, axes, 0, 0, tiled=True)  25.3 us
    all_to_all x1, blocking collectives, body(): lax.all_to_all(cross.reshape(GRID['y'], CHUNK, rank), 'y', 0, 0, tiled=True)  20.8 us
    all_to_all x1, blocking collectives, body(): lax.all_to_all(gram.reshape(GROUPS, share_rank, rank), ROWS_OVER, 0, 0, t...  19.3 us
    reduce_scatter x1, waiting for transfers between devices, body(): cross = lax.psum_scatter(cross, 'z', scatter_dimension=0, tiled=True)  11 us
    pallas_call x1, Pallas kernels, inverse_factor(): pl.pallas_call(functools.partial(factor_kernel, size=size), out_shape=jax...  9.43 us
    dot_general x6, matrix products, nt_dot(): lax.dot_general(a, b, (((1,), (1,)), ((), ())), precision=precision, pref...  7.36 us
  transfers between devices with their start and end apart: 5, of which 5 were waited for; matrix products, arithmetic and copies ran while one was open for 2% of the time, Pallas kernels for 4%

profile of v1, /device:TPU:1, one launch (start us, length us, event | category | flops | bytes accessed | tf_op | source)
XLA Modules:
  0.0 249.5 jit_solution(8219784346709863332)
XLA Ops:
  7.2 2.4 broadcast_in_dim.20
  9.5 0.0 copy-start
  9.5 17.3 %all-to-all-start = ((bf16[64,4,3328]{2,1,0:T(4,128)(2,1)}), bf16[64,4,3328]{2,1,0:T(4,128)(2,1)S(1)}, u32[]{:S(2)}, u32[]{:S(2)}) async-start(bf16[64,4,3328]{2,1,0:T(4,128)(2,1)} %broadcast_in_dim.20), calls=%async_computation | async-start | bytes 3407872 | tf_op jit(solution)/shard_map/factor_gather/all_to_all | solution.py:101
  26.8 0.0 copy-done
  26.8 1.4 add_convert_fusion
  28.2 40.8 %all-to-all-done = bf16[64,4,3328]{2,1,0:T(4,128)(2,1)S(1)} async-done(((bf16[64,4,3328]{2,1,0:T(4,128)(2,1)}), bf16[64,4,3328]{2,1,0:T(4,128)(2,1)S(1)}, u32[]{:S(2)}, u32[]{:S(2)}) %all-to-all-start) | async-done | bytes 1703968 | tf_op jit(solution)/shard_map/factor_gather/all_to_all | solution.py:101
  69.0 1.4 reshape.38
  70.3 2.1 fusion.22
  72.5 6.6 %all_to_all.40 = f32[2,128,256]{2,1,0:T(8,128)S(1)} all-to-all(f32[2,128,256]{2,1,0:T(8,128)S(1)} %broadcast_in_dim.21), channel_id=1, replica_groups=mesh['z'=8,'y'=8,'x'=4,'core'=2] {'core'}, dimensions={0} | all-to-all | bytes 524288 | tf_op jit(solution)/shard_map/basis/all_to_all | solution.py:101
  79.2 0.8 broadcast_in_dim.22
  80.0 4.0 %all-to-all-start.2 = ((f32[4,128,256]{2,1,0:T(8,128)}), f32[4,128,256]{2,1,0:T(8,128)S(1)}, u32[]{:S(2)}, u32[]{:S(2)}) async-start(f32[4,128,256]{2,1,0:T(8,128)} %broadcast_in_dim.22), calls=%async_computation.2 | async-start | bytes 1048576 | tf_op jit(solution)/shard_map/basis/all_to_all | solution.py:101
  84.0 0.0 reduce-scatter.2.cloned.1.call-start
  84.0 0.1 pad.4
  84.1 8.9 %all-to-all-done.2 = f32[4,128,256]{2,1,0:T(8,128)S(1)} async-done(((f32[4,128,256]{2,1,0:T(8,128)}), f32[4,128,256]{2,1,0:T(8,128)S(1)}, u32[]{:S(2)}, u32[]{:S(2)}) %all-to-all-start.2) | async-done | bytes 524320 | tf_op jit(solution)/shard_map/basis/all_to_all | solution.py:101
  93.0 2.5 fusion.5
  95.5 0.0 reduce-scatter.2.cloned.1.call-update
  95.5 0.1 copy.14
  95.6 0.4 fusion.17
  96.0 0.2 copy.16
  96.2 19.3 %all_to_all.41 = f32[64,4,256]{2,1,0:T(4,128)S(1)} all-to-all(f32[64,4,256]{2,1,0:T(4,128)S(1)} %copy.16), channel_id=1, replica_groups=mesh['z'=8,'y'=8,'x'=4,'core'=2] {'z','y'}, dimensions={0} | all-to-all | bytes 524288 | tf_op jit(solution)/shard_map/gram/all_to_all | solution.py:135
  115.5 0.1 reduce_sum.65
  115.6 18.6 %all_to_all.42 = f32[64,4,256]{2,1,0:T(4,128)S(1)} all-to-all(f32[64,4,256]{2,1,0:T(4,128)S(1)} %broadcast_in_dim.23), channel_id=1, replica_groups=mesh['z'=8,'y'=8,'x'=4,'core'=2] {'z','y'}, dimensions={0} | all-to-all | bytes 524288 | tf_op jit(solution)/shard_map/gram/all_to_all | solution.py:101
  134.3 0.1 reshape.39.gram_ref
  134.3 9.4 %inverse_factor.1 = f32[256,256]{1,0:T(8,128)S(1)} custom-call(f32[256,256]{1,0:T(8,128)S(1)} %reshape.39.gram_ref), custom_call_target="tpu_custom_call" | custom-call | flops 1000000000 | bytes 524288 | tf_op jit(solution)/shard_map/solve/inverse_factor/pallas_call | solution.py:88
  143.8 11.0 %reduce-scatter.2.cloned.1.call-done = f32[448,256]{1,0:T(8,128)} async-done(((f32[3584,256]{1,0:T(8,128)}), f32[448,256]{1,0:T(8,128)}) %reduce-scatter.2.cloned.1.call-update) | async-done | bytes 458768 | tf_op jit(solution)/shard_map/cross/reduce_scatter | solution.py:132
  154.8 20.8 %all_to_all.43 = f32[8,56,256]{2,1,0:T(8,128)S(1)} all-to-all(f32[8,56,256]{2,1,0:T(8,128)} %bitcast.21), channel_id=1, replica_groups=mesh['z'=8,'y'=8,'x'=4,'core'=2] {'y'}, dimensions={0} | all-to-all | bytes 917504 | tf_op jit(solution)/shard_map/projection/all_to_all | solution.py:144
  175.7 0.4 convolution_convert_fusion.1
  176.0 1.4 broadcast_in_dim.24
  177.4 5.2 %all-to-all-start.6 = ((bf16[64,56,256]{2,1,0:T(8,128)(2,1)}), bf16[64,56,256]{2,1,0:T(8,128)(2,1)S(1)}, u32[]{:S(2)}, u32[]{:S(2)}) async-start(bf16[64,56,256]{2,1,0:T(8,128)(2,1)} %broadcast_in_dim.24), calls=%async_computation.7 | async-start | bytes 3670016 | tf_op jit(solution)/shard_map/projection/all_to_all | solution.py:101
  182.6 0.4 convolution_convert_fusion
  183.0 43.3 %all-to-all-done.6 = bf16[64,56,256]{2,1,0:T(8,128)(2,1)S(1)} async-done(((bf16[64,56,256]{2,1,0:T(8,128)(2,1)}), bf16[64,56,256]{2,1,0:T(8,128)(2,1)S(1)}, u32[]{:S(2)}, u32[]{:S(2)}) %all-to-all-start.6) | async-done | bytes 1835040 | tf_op jit(solution)/shard_map/projection/all_to_all | solution.py:101
  226.3 0.5 fusion.3
  226.8 0.6 broadcast_in_dim.25
  227.4 7.6 %all-to-all-start.7 = ((f32[8,1,256]{2,1,0:T(1,128)}), f32[8,1,256]{2,1,0:T(1,128)S(1)}, u32[]{:S(2)}, u32[]{:S(2)}) async-start(f32[8,1,256]{2,1,0:T(1,128)} %broadcast_in_dim.25), calls=%async_computation.8 | async-start | bytes 16384 | tf_op jit(solution)/shard_map/norms/all_to_all | solution.py:101
  234.9 1.6 fusion.1
  236.6 3.0 %all-to-all-done.7 = f32[8,1,256]{2,1,0:T(1,128)S(1)} async-done(((f32[8,1,256]{2,1,0:T(1,128)}), f32[8,1,256]{2,1,0:T(1,128)S(1)}, u32[]{:S(2)}, u32[]{:S(2)}) %all-to-all-start.7) | async-done | bytes 8224 | tf_op jit(solution)/shard_map/norms/all_to_all | solution.py:101
  239.6 1.6 fusion.2
  241.3 0.2 select_reduce_fusion
  241.4 1.2 convolution_multiply_fusion.2
  (9 shorter events, 0.2 us)
Async XLA Ops:
  9.5 17.3 %copy-start = (bf16[128,3328]{1,0:T(8,128)(2,1)S(1)}, bf16[128,3328]{1,0:T(8,128)(2,1)}, u32[]{:S(2)}) copy-start(bf16[128,3328]{1,0:T(8,128)(2,1)} %param.4) | copy-start | bytes 2555908
  9.5 59.4 %all-to-all-start = ((bf16[64,4,3328]{2,1,0:T(4,128)(2,1)}), bf16[64,4,3328]{2,1,0:T(4,128)(2,1)S(1)}, u32[]{:S(2)}, u32[]{:S(2)}) async-start(bf16[64,4,3328]{2,1,0:T(4,128)(2,1)} %broadcast_in_dim.20), calls=%async_computation | async-start | bytes 3407872 | tf_op jit(solution)/shard_map/factor_gather/all_to_all | solution.py:101
  80.0 12.9 %all-to-all-start.2 = ((f32[4,128,256]{2,1,0:T(8,128)}), f32[4,128,256]{2,1,0:T(8,128)S(1)}, u32[]{:S(2)}, u32[]{:S(2)}) async-start(f32[4,128,256]{2,1,0:T(8,128)} %broadcast_in_dim.22), calls=%async_computation.2 | async-start | bytes 1048576 | tf_op jit(solution)/shard_map/basis/all_to_all | solution.py:101
  84.0 70.8 %reduce-scatter.2.cloned.1.call-start = ((), (), s32[]{:S(2)}) async-start(), calls=%async_computation.9 | async-start | bytes 4128768 | tf_op jit(solution)/shard_map/cross/reduce_scatter | solution.py:132
  177.4 48.9 %all-to-all-start.6 = ((bf16[64,56,256]{2,1,0:T(8,128)(2,1)}), bf16[64,56,256]{2,1,0:T(8,128)(2,1)S(1)}, u32[]{:S(2)}, u32[]{:S(2)}) async-start(bf16[64,56,256]{2,1,0:T(8,128)(2,1)} %broadcast_in_dim.24), calls=%async_computation.7 | async-start | bytes 3670016 | tf_op jit(solution)/shard_map/projection/all_to_all | solution.py:101
  227.4 12.2 %all-to-all-start.7 = ((f32[8,1,256]{2,1,0:T(1,128)}), f32[8,1,256]{2,1,0:T(1,128)S(1)}, u32[]{:S(2)}, u32[]{:S(2)}) async-start(f32[8,1,256]{2,1,0:T(1,128)} %broadcast_in_dim.25), calls=%async_computation.8 | async-start | bytes 16384 | tf_op jit(solution)/shard_map/norms/all_to_all | solution.py:101
Sparse Core Ops, SparseCore 0:
  95.6 59.1 reduce-scatter.1

commit v2 on v1

--- a/solution.py
+++ b/solution.py
@@ -6,17 +6,45 @@
 from jax import lax
 from jax.experimental import pallas as pl
 from jax.experimental.pallas import tpu as pltpu
-from jax.sharding import Mesh, PartitionSpec as P
+from jax.sharding import PartitionSpec as P
 
 EPSILON = 1e-06
 MOMENTUM_DECAY = 0.95
 HIGHEST = lax.Precision.HIGHEST
 
-ROWS_OVER = ("z", "y")
-COLS_OVER = ("x", "core")
-GRID = {"z": 8, "y": 8, "x": 4, "core": 2}
-GROUPS = 64
-CHUNK = 56
+AXES = ("fsdp", "tp")
+SIDE = 8
+LINE = 4
+CORES = 2
+
+
+def groups_of(key, order):
+    found = {}
+    for index in range(SIDE * SIDE * LINE * CORES):
+        fsdp, tp = divmod(index, LINE * CORES)
+        place = divmod(fsdp, SIDE) + divmod(tp, CORES)
+        found.setdefault(key(*place), []).append((order(*place), index))
+    return [[index for _, index in sorted(group)] for group in found.values()]
+
+
+def tile(place, core):
+    return (place - core) % SIDE // 2
+
+
+NEAR = groups_of(
+    lambda z, y, x, core: (tile(z, core), tile(y, core), x, core), lambda z, y, x, core: (z % 2, y % 2)
+)
+STRIDED = groups_of(
+    lambda z, y, x, core: (z % 2, y % 2, x, core), lambda z, y, x, core: (z // 2, y // 2)
+)
+MIDDLE = groups_of(
+    lambda z, y, x, core: (z // 4, z % 2, y // 4, y % 2, x, core),
+    lambda z, y, x, core: (z // 2, y // 2),
+)
+FAR = groups_of(lambda z, y, x, core: (z % 4, y % 4, x, core), lambda z, y, x, core: (z, y))
+CHIP = groups_of(lambda z, y, x, core: (z, y, x), lambda z, y, x, core: core)
+ROW = groups_of(lambda z, y, x, core: (z, y, core), lambda z, y, x, core: x)
+COLUMNS = groups_of(lambda z, y, x, core: (z, y), lambda z, y, x, core: (x, core))
 
 FACTOR_BLOCK = 64
 FACTOR_GROUP = 8
@@ -96,9 +124,40 @@
     )(gram)
 
 
-def spread(block, axes, parts):
-    copies = jnp.broadcast_to(block[None], (parts,) + block.shape)
-    return lax.all_to_all(copies, axes, 0, 0, tiled=True)
+def exchange(blocks, groups):
+    return lax.all_to_all(blocks, AXES, 0, 0, axis_index_groups=groups, tiled=True)
+
+
+def spread(block, groups):
+    return exchange(jnp.broadcast_to(block[None], (len(groups[0]),) + block.shape), groups)
+
+
+def spread_rows(block):
+    return spread(spread(block, STRIDED), NEAR)
+
+
+def add_up(blocks):
+    parts = [blocks[i].astype(jnp.float32) for i in range(blocks.shape[0])]
+    while len(parts) > 1:
+        parts = [a + b for a, b in zip(parts[::2], parts[1::2])]
+    return parts[0]
+
+
+def total(block, groups):
+    return add_up(spread(block, groups))
+
+
+def to_tiles(blocks):
+    rest = blocks.shape[1:]
+    split = blocks.reshape((SIDE // 2, 2, SIDE // 2, 2, -1) + rest)
+    return jnp.transpose(split, (1, 3, 0, 2, 4) + tuple(range(5, split.ndim))).reshape(blocks.shape)
+
+
+def from_tiles(blocks):
+    rest = blocks.shape[2:]
+    split = blocks.reshape((2, 2, SIDE // 2, SIDE // 2, -1) + rest)
+    order = (2, 0, 3, 1, 4) + tuple(range(5, split.ndim))
+    return jnp.transpose(split, order).reshape((-1,) + rest)
 
 
 def nt_dot(a, b, precision=None):
@@ -110,69 +169,59 @@
 def body(momentum, gradient, right_factor):
     rows, cols = momentum.shape
     share_rank = right_factor.shape[0]
-    rank = share_rank * GROUPS
-    padded = GROUPS * CHUNK
+    groups, columns = SIDE * SIDE, LINE * CORES
+    tiles = groups // 4
+    rank = share_rank * groups
     blended = (momentum.astype(jnp.float32) + gradient.astype(jnp.float32)).astype(jnp.bfloat16)
     with jax.named_scope("factor_gather"):
-        whole_factor = spread(right_factor, ROWS_OVER, GROUPS).reshape(rank, cols)
+        whole_factor = from_tiles(
+            spread_rows(right_factor).reshape(4, tiles * share_rank, cols)
+        )
     with jax.named_scope("basis"):
-        basis = nt_dot(blended, whole_factor)
-        basis = jnp.sum(spread(basis, "core", GRID["core"]), axis=0)
-        basis = jnp.sum(spread(basis, "x", GRID["x"]), axis=0)
-    with jax.named_scope("cross"):
-        high = basis.astype(jnp.bfloat16)
-        low = (basis - high.astype(jnp.float32)).astype(jnp.bfloat16)
-        wide = jnp.pad(blended, ((0, 0), (0, padded - cols)))
-        cross = lax.dot_general(
-            jnp.concatenate([wide, wide], axis=0),
-            jnp.concatenate([high, low], axis=0),
-            (((0,), (0,)), ((), ())),
-            preferred_element_type=jnp.float32,
-        )
-        cross = lax.psum_scatter(cross, "z", scatter_dimension=0, tiled=True)
+        basis = total(total(nt_dot(blended, whole_factor), CHIP), ROW)
     with jax.named_scope("gram"):
-        gram = jnp.dot(basis.T, basis, precision=HIGHEST)
-        gram = lax.all_to_all(
-            gram.reshape(GROUPS, share_rank, rank), ROWS_OVER, 0, 0, tiled=True
-        )
-        gram = spread(jnp.sum(gram, axis=0), ROWS_OVER, GROUPS).reshape(rank, rank)
+        share = rank // columns
+        part = lax.dynamic_slice_in_dim(basis.T, lax.axis_index("tp") * share, share, 0)
+        part = jnp.dot(part, basis, precision=HIGHEST)
+        part = total(total(total(part, FAR), MIDDLE), NEAR)
+        gram = spread(part, COLUMNS).reshape(rank, rank)
     with jax.named_scope("solve"):
-        inverse = inverse_factor(gram)
-        cross, inverse = lax.optimization_barrier((cross, inverse))
+        inverse = to_tiles(inverse_factor(gram))
         ortho_basis = nt_dot(basis, inverse, HIGHEST).astype(jnp.bfloat16)
     with jax.named_scope("projection"):
-        cross = lax.all_to_all(
-            cross.reshape(GRID["y"], CHUNK, rank), "y", 0, 0, tiled=True
-        )
-        own = nt_dot(jnp.sum(cross, axis=0), inverse, HIGHEST).astype(jnp.bfloat16)
-        projection = spread(own, ROWS_OVER, GROUPS).reshape(padded, rank)[:cols]
+        partial = lax.dot_general(
+            ortho_basis, blended, (((0,), (0,)), ((), ())), preferred_element_type=jnp.float32
+        ).astype(jnp.bfloat16)
+        partial = exchange(partial.reshape(4, tiles * share_rank, cols), NEAR)
+        partial = add_up(partial).astype(jnp.bfloat16)
+        partial = exchange(partial.reshape(tiles, share_rank, cols), STRIDED)
+        own = add_up(partial)
+        projection = spread_rows(own.astype(jnp.bfloat16)).reshape(rank, cols)
     with jax.named_scope("norms"):
-        wide_proj = projection.astype(jnp.float32)
-        squares = jnp.sum(wide_proj * wide_proj, axis=0)[None]
-        squares = jnp.sum(spread(squares, COLS_OVER, GRID["x"] * GRID["core"]), axis=0)
-        inverse_norms = 1.0 / (jnp.sqrt(squares) + EPSILON)
+        wide = projection.astype(jnp.float32)
+        squares = total(jnp.sum(wide * wide, axis=1)[None], COLUMNS)[0]
+        norms = jnp.sqrt(squares) + EPSILON
     with jax.named_scope("outputs"):
-        carried = nt_dot(ortho_basis, projection)
+        carried = jnp.dot(ortho_basis, projection, preferred_element_type=jnp.float32)
         momentum_next = (blended.astype(jnp.float32) - (1.0 - MOMENTUM_DECAY) * carried).astype(
             jnp.bfloat16
         )
-        scale_factor = math.sqrt(rows * GROUPS * cols * GRID["x"] * GRID["core"] / rank)
-        scaled = (wide_proj * inverse_norms).astype(jnp.bfloat16)
-        update = (scale_factor * nt_dot(ortho_basis, scaled)).astype(jnp.bfloat16)
-        first = lax.axis_index(ROWS_OVER) * share_rank
-        own_rank = first + lax.broadcasted_iota(jnp.int32, (share_rank, rank), 0)
-        pick = own_rank == lax.broadcasted_iota(jnp.int32, (share_rank, rank), 1)
-        own_norms = jnp.sum(jnp.where(pick, inverse_norms, 0.0), axis=1, keepdims=True)
-        factor_next = nt_dot(pick.astype(jnp.bfloat16), projection) * own_norms
+        scale_factor = math.sqrt(rows * groups * cols * columns / rank)
+        factor = (wide / norms[:, None]).astype(jnp.bfloat16)
+        direction = jnp.dot(ortho_basis, factor, preferred_element_type=jnp.float32)
+        update = (scale_factor * direction).astype(jnp.bfloat16)
+        z, y = lax.axis_index("fsdp") // SIDE, lax.axis_index("fsdp") % SIDE
+        place = ((z % 2 * 2 + y % 2) * tiles + z // 2 * (SIDE // 2) + y // 2) * share_rank
+        own_norms = lax.dynamic_slice_in_dim(norms, place, share_rank, 0)
+        factor_next = own / own_norms[:, None]
     return (momentum_next, factor_next, update)
 
 
 def solution(mesh):
-    chips = Mesh(mesh.devices.reshape(tuple(GRID.values())), tuple(GRID))
-    placed = P(ROWS_OVER, COLS_OVER)
+    placed = P(*AXES)
     return jax.shard_map(
         body,
-        mesh=chips,
+        mesh=mesh,
         in_specs=(placed, placed, placed),
         out_specs=(placed, placed, placed),
         check_vma=False,

time: 250 us -> 233 us (0.932)
  blocking collectives: 65.4 us -> 162 us
  waiting for transfers between devices: 107 us -> 23.3 us
  starting transfers between devices: 34 us -> 12.8 us
  between operations: 14.2 us -> 0.9 us
  local copies, waits for them, and re-layouts: 7.04 us -> 15.7 us
  matrix products: 10.2 us -> 6.54 us
    all_to_all x4 -> x10, blocking collectives: 65.4 us -> 162 us  [exchange(): lax.all_to_all(blocks, AXES, 0, 0, axis_index_groups=groups, tiled=True)]
    all_to_all x4 -> x3, waiting for transfers between devices: 95.9 us -> 23.3 us  [exchange(): lax.all_to_all(blocks, AXES, 0, 0, axis_index_groups=groups, tiled=True)]
    all_to_all x4 -> x3, starting transfers between devices: 34 us -> 12.8 us  [exchange(): lax.all_to_all(blocks, AXES, 0, 0, axis_index_groups=groups, tiled=True)]
    reduce_scatter x1 -> x0, waiting for transfers between devices: 11 us -> none  [body(): cross = lax.psum_scatter(cross, 'z', scatter_dimension=0, tiled=True)]
    dot_general x6 -> x2, matrix products: 7.36 us -> 1.1 us  [nt_dot(): lax.dot_general(a, b, (((1,), (1,)), ((), ())), precision=precision, pref...]
    reshape x2 -> x5, local copies, waits for them, and re-layouts: 1.47 us -> 7.03 us  [the longest x1 3.86 us: body(): projection = spread_rows(own.astype(jnp.bfloat16)).reshape(rank, cols)]
    dot_general x2 -> x4, matrix products: 2.86 us -> 5.45 us  [the longest x1 2.98 us: body(): jnp.dot(ortho_basis, projection, preferred_element_type=jnp.float32)]
    broadcast_in_dim x6 -> x12, local copies, waits for them, and re-layouts: 5.24 us -> 4.39 us  [spread(): jnp.broadcast_to(block[None], (len(groups[0]),) + block.shape)]
  transfers between devices with their start and end apart: 5 -> 3, of which waited for: 5 -> 3; matrix products, arithmetic and copies ran while one was open for 2% -> 1% of each run, Pallas kernels for 4% -> 0%
where the time goes in v2:
time: 233 us; the launch traced here: 232 us
  blocking collectives  162 us (70%)
  waiting for transfers between devices  23.3 us (10%)
  local copies, waits for them, and re-layouts  15.7 us (7%)
  starting transfers between devices  12.8 us (5%)
  Pallas kernels  9.43 us (4%)
  matrix products  6.54 us (3%)
    all_to_all x10, blocking collectives, exchange(): lax.all_to_all(blocks, AXES, 0, 0, axis_index_groups=groups, tiled=True)  162 us
    all_to_all x3, waiting for transfers between devices, exchange(): lax.all_to_all(blocks, AXES, 0, 0, axis_index_groups=groups, tiled=True)  23.3 us
    all_to_all x3, starting transfers between devices, exchange(): lax.all_to_all(blocks, AXES, 0, 0, axis_index_groups=groups, tiled=True)  12.8 us
    pallas_call x1, Pallas kernels, inverse_factor(): pl.pallas_call(functools.partial(factor_kernel, size=size), out_shape=jax...  9.43 us
  transfers between devices with their start and end apart: 3, of which 3 were waited for; matrix products, arithmetic and copies ran while one was open for 1% of the time, Pallas kernels for 0%

profile of v2, /device:TPU:1, one launch (start us, length us, event | category | flops | bytes accessed | tf_op | source)
XLA Modules:
  0.0 231.8 jit_solution(15496889097192622694)
XLA Ops:
  0.6 0.9 broadcast_in_dim.34
  1.5 32.5 %all_to_all.65 = bf16[16,4,3328]{2,1,0:T(4,128)(2,1)S(1)} all-to-all(bf16[16,4,3328]{2,1,0:T(4,128)(2,1)S(1)} %broadcast_in_dim.34), channel_id=1, replica_groups={{0,16,32,48,128,144,160,176,256,272,288,304,384,400,416,432},{1,17,33,4..., dimensions={0} | all-to-all | bytes 851968 | tf_op jit(solution)/shard_map/factor_gather/all_to_all | solution.py:128
  34.0 0.4 broadcast_in_dim.35
  34.4 17.8 %all_to_all.66 = bf16[4,16,4,3328]{3,2,1,0:T(4,128)(2,1)S(1)} all-to-all(bf16[4,16,4,3328]{3,2,1,0:T(4,128)(2,1)S(1)} %broadcast_in_dim.35), channel_id=1, replica_groups={{0,8,64,72},{1,57,449,505},{2,10,66,74},{3,59,451,507},{4,12,68,76},{5,..., dimensions={0} | all-to-all | bytes 3407872 | tf_op jit(solution)/shard_map/factor_gather/all_to_all | solution.py:128
  52.2 1.9 copy.20
  54.0 0.0 copy-start
  54.0 0.0 copy-start.1
  54.0 3.0 %reshape.169 = bf16[256,3328]{1,0:T(8,128)(2,1)S(1)} reshape(bf16[4,2,4,2,4,3328]{5,4,3,2,1,0:T(4,128)(2,1)} %copy.20) | data formatting | bytes 3407872 | tf_op jit(solution)/shard_map/factor_gather/reshape | solution.py:160
  57.0 0.0 copy-done
  57.0 0.0 copy-done.1
  57.0 0.7 fusion.20
  57.8 4.0 %all_to_all.67 = f32[2,128,256]{2,1,0:T(8,128)S(1)} all-to-all(f32[2,128,256]{2,1,0:T(8,128)S(1)} %broadcast_in_dim.36), channel_id=1, replica_groups={{0,1},{2,3},{4,5},{6,7},{8,9},{10,11},{12,13},{14,15},{16,17},{18,19},{..., dimensions={0} | all-to-all | bytes 524288 | tf_op jit(solution)/shard_map/basis/all_to_all | solution.py:128
  61.8 0.8 broadcast_in_dim.38
  62.6 4.0 %all-to-all-start.3 = ((f32[4,128,256]{2,1,0:T(8,128)}), f32[4,128,256]{2,1,0:T(8,128)S(1)}, u32[]{:S(2)}, u32[]{:S(2)}) async-start(f32[4,128,256]{2,1,0:T(8,128)} %broadcast_in_dim.38), calls=%async_computation.3 | async-start | bytes 1048576 | tf_op jit(solution)/shard_map/basis/all_to_all | solution.py:128
  66.7 8.9 %all-to-all-done.3 = f32[4,128,256]{2,1,0:T(8,128)S(1)} async-done(((f32[4,128,256]{2,1,0:T(8,128)}), f32[4,128,256]{2,1,0:T(8,128)S(1)}, u32[]{:S(2)}, u32[]{:S(2)}) %all-to-all-start.3) | async-done | bytes 524320 | tf_op jit(solution)/shard_map/basis/all_to_all | solution.py:128
  75.6 0.3 fusion.6
  76.0 18.8 %all_to_all.68 = f32[4,32,256]{2,1,0:T(8,128)S(1)} all-to-all(f32[4,32,256]{2,1,0:T(8,128)S(1)} %broadcast_in_dim.39), channel_id=1, replica_groups={{0,32,256,288},{1,33,257,289},{2,34,258,290},{3,35,259,291},{4,36,260,2..., dimensions={0} | all-to-all | bytes 262144 | tf_op jit(solution)/shard_map/gram/all_to_all | solution.py:128
  94.8 8.6 %all_to_all.69 = f32[4,32,256]{2,1,0:T(8,128)S(1)} all-to-all(f32[4,32,256]{2,1,0:T(8,128)S(1)} %broadcast_in_dim.41), channel_id=1, replica_groups={{0,16,128,144},{1,17,129,145},{2,18,130,146},{3,19,131,147},{4,20,132,1..., dimensions={0} | all-to-all | bytes 262144 | tf_op jit(solution)/shard_map/gram/all_to_all | solution.py:128
  103.4 8.7 %all_to_all.70 = f32[4,32,256]{2,1,0:T(8,128)S(1)} all-to-all(f32[4,32,256]{2,1,0:T(8,128)S(1)} %broadcast_in_dim.43), channel_id=1, replica_groups={{0,8,64,72},{1,57,449,505},{2,10,66,74},{3,59,451,507},{4,12,68,76},{5,..., dimensions={0} | all-to-all | bytes 262144 | tf_op jit(solution)/shard_map/gram/all_to_all | solution.py:128
  112.2 10.9 %all_to_all.71 = f32[8,32,256]{2,1,0:T(8,128)S(1)} all-to-all(f32[8,32,256]{2,1,0:T(8,128)S(1)} %broadcast_in_dim.45), channel_id=1, replica_groups={{0,1,2,3,4,5,6,7},{8,9,10,11,12,13,14,15},{16,17,18,19,20,21,22,23},{24..., dimensions={0} | all-to-all | bytes 524288 | tf_op jit(solution)/shard_map/gram/all_to_all | solution.py:128
  123.1 9.4 %inverse_factor.1 = f32[256,256]{1,0:T(8,128)S(1)} custom-call(f32[256,256]{1,0:T(8,128)S(1)} %bitcast.37), custom_call_target="tpu_custom_call" | custom-call | flops 1000000000 | bytes 524288 | tf_op jit(solution)/shard_map/solve/inverse_factor/pallas_call | solution.py:116
  132.5 0.1 reshape.172
  132.6 0.1 reshape.173
  132.7 0.4 convolution_convert_fusion.1
  133.1 0.6 convolution_convert_fusion
  133.8 17.2 %all_to_all.72 = bf16[4,64,3328]{2,1,0:T(8,128)(2,1)S(1)} all-to-all(bf16[4,64,3328]{2,1,0:T(8,128)(2,1)S(1)} %bitcast.39), channel_id=1, replica_groups={{0,8,64,72},{1,57,449,505},{2,10,66,74},{3,59,451,507},{4,12,68,76},{5,..., dimensions={0} | all-to-all | bytes 3407872 | tf_op jit(solution)/shard_map/projection/all_to_all | solution.py:128
  150.9 0.2 add_convert_fusion.1
  151.2 0.1 convert_element_type.155
  151.3 22.1 %all_to_all.73 = bf16[16,4,3328]{2,1,0:T(4,128)(2,1)S(1)} all-to-all(bf16[16,4,3328]{2,1,0:T(4,128)(2,1)S(1)} %convert_element_type.155), channel_id=1, replica_groups={{0,16,32,48,128,144,160,176,256,272,288,304,384,400,416,432},{1,17,33,4..., dimensions={0} | all-to-all | bytes 851968 | tf_op jit(solution)/shard_map/projection/all_to_all | solution.py:128
  173.4 0.1 convert_bitcast_fusion
  173.5 0.1 broadcast_in_dim.93
  173.6 21.1 %all_to_all.74 = bf16[16,4,3328]{2,1,0:T(4,128)(2,1)S(1)} all-to-all(bf16[16,4,3328]{2,1,0:T(4,128)(2,1)S(1)} %broadcast_in_dim.93), channel_id=1, replica_groups={{0,16,32,48,128,144,160,176,256,272,288,304,384,400,416,432},{1,17,33,4..., dimensions={0} | all-to-all | bytes 851968 | tf_op jit(solution)/shard_map/projection/all_to_all | solution.py:128
  194.7 1.3 broadcast_in_dim.94
  196.1 3.8 %all-to-all-start.11 = ((bf16[4,16,4,3328]{3,1,2,0:T(8,128)(2,1)}), bf16[4,16,4,3328]{3,1,2,0:T(8,128)(2,1)S(1)}, u32[]{:S(2)}, u32[]{:S(2)}) async-start(bf16[4,16,4,3328]{3,1,2,0:T(8,128)(2,1)} %broadcast_in_dim.94), calls=%async_computation.11 | async-start | bytes 3407872 | tf_op jit(solution)/shard_map/projection/all_to_all | solution.py:128
  199.9 12.7 %all-to-all-done.11 = bf16[4,16,4,3328]{3,1,2,0:T(8,128)(2,1)S(1)} async-done(((bf16[4,16,4,3328]{3,1,2,0:T(8,128)(2,1)}), bf16[4,16,4,3328]{3,1,2,0:T(8,128)(2,1)S(1)}, u32[]{:S(2)}, u32[]{:S(2)}) %all-to-all-start.11) | async-done | bytes 1703968 | tf_op jit(solution)/shard_map/projection/all_to_all | solution.py:128
  212.6 2.1 copy.23
  214.7 3.9 %reshape.175 = bf16[256,3328]{1,0:T(8,128)(2,1)} reshape(bf16[4,16,4,3328]{3,2,1,0:T(4,128)(2,1)} %copy.23) | data formatting | bytes 3407872 | tf_op jit(solution)/shard_map/projection/reshape | solution.py:199
  218.6 0.4 multiply_reduce_fusion
  219.0 0.1 copy.24
  219.1 0.1 broadcast_in_dim.95
  219.2 0.6 broadcast_in_dim.96
  219.8 5.1 %all-to-all-start.12 = ((f32[8,1,256]{2,1,0:T(1,128)}), f32[8,1,256]{2,1,0:T(1,128)S(1)}, u32[]{:S(2)}, u32[]{:S(2)}) async-start(f32[8,1,256]{2,1,0:T(1,128)} %broadcast_in_dim.96), calls=%async_computation.12 | async-start | bytes 16384 | tf_op jit(solution)/shard_map/norms/all_to_all | solution.py:128
  224.9 0.0 copy-start.2
  224.9 3.0 %fusion.1 = bf16[128,3328]{1,0:T(8,128)(2,1)} fusion(bf16[128,256]{1,0:T(8,128)(2,1)S(1)} %convolution_convert_fusion.1, bf16[256,3328]{1,0:T(8,128)(2,1)} %reshape.175, bf16[128,3328]{1,0:T(8,128)(2,1)S(1)} %copy-done, bf16[128,3328]{1,0:T(8,128)(2,1)S(1)} %copy-done.1), kind=kOutput, calls=%fused_computation.4 | convolution fusion | flops 221511680 | bytes 4325376 | tf_op jit(solution)/shard_map/outputs/dot_general | solution.py:205
  227.9 1.7 all-to-all-done.12
  229.5 0.1 dynamic-slice_bitcast_fusion
  229.6 0.0 copy-done.2
  229.6 1.5 fusion.2
  231.1 0.7 bitcast_divide_fusion
  (13 shorter events, 0.2 us)
Async XLA Ops:
  54.0 3.0 %copy-start = (bf16[128,3328]{1,0:T(8,128)(2,1)S(1)}, bf16[128,3328]{1,0:T(8,128)(2,1)}, u32[]{:S(2)}) copy-start(bf16[128,3328]{1,0:T(8,128)(2,1)} %param.4) | copy-start | bytes 2555908
  54.0 3.0 %copy-start.1 = (bf16[128,3328]{1,0:T(8,128)(2,1)S(1)}, bf16[128,3328]{1,0:T(8,128)(2,1)}, u32[]{:S(2)}) copy-start(bf16[128,3328]{1,0:T(8,128)(2,1)} %param.3) | copy-start | bytes 2555908
  62.6 12.9 %all-to-all-start.3 = ((f32[4,128,256]{2,1,0:T(8,128)}), f32[4,128,256]{2,1,0:T(8,128)S(1)}, u32[]{:S(2)}, u32[]{:S(2)}) async-start(f32[4,128,256]{2,1,0:T(8,128)} %broadcast_in_dim.38), calls=%async_computation.3 | async-start | bytes 1048576 | tf_op jit(solution)/shard_map/basis/all_to_all | solution.py:128
  196.1 16.5 %all-to-all-start.11 = ((bf16[4,16,4,3328]{3,1,2,0:T(8,128)(2,1)}), bf16[4,16,4,3328]{3,1,2,0:T(8,128)(2,1)S(1)}, u32[]{:S(2)}, u32[]{:S(2)}) async-start(bf16[4,16,4,3328]{3,1,2,0:T(8,128)(2,1)} %broadcast_in_dim.94), calls=%async_computation.11 | async-start | bytes 3407872 | tf_op jit(solution)/shard_map/projection/all_to_all | solution.py:128
  219.8 9.7 %all-to-all-start.12 = ((f32[8,1,256]{2,1,0:T(1,128)}), f32[8,1,256]{2,1,0:T(1,128)S(1)}, u32[]{:S(2)}, u32[]{:S(2)}) async-start(f32[8,1,256]{2,1,0:T(1,128)} %broadcast_in_dim.96), calls=%async_computation.12 | async-start | bytes 16384 | tf_op jit(solution)/shard_map/norms/all_to_all | solution.py:128
  224.9 4.7 %copy-start.2 = (bf16[256,3328]{1,0:T(8,128)(2,1)S(1)}, bf16[256,3328]{1,0:T(8,128)(2,1)}, u32[]{:S(2)}) copy-start(bf16[256,3328]{1,0:T(8,128)(2,1)} %reshape.175) | copy-start | bytes 5111812

commit v3 on v2

--- a/solution.py
+++ b/solution.py
@@ -37,11 +37,12 @@
 STRIDED = groups_of(
     lambda z, y, x, core: (z % 2, y % 2, x, core), lambda z, y, x, core: (z // 2, y // 2)
 )
-MIDDLE = groups_of(
-    lambda z, y, x, core: (z // 4, z % 2, y // 4, y % 2, x, core),
-    lambda z, y, x, core: (z // 2, y // 2),
+FIRST_LINE = groups_of(
+    lambda z, y, x, core: (z if core else y, x, core), lambda z, y, x, core: y if core else z
 )
-FAR = groups_of(lambda z, y, x, core: (z % 4, y % 4, x, core), lambda z, y, x, core: (z, y))
+SECOND_LINE = groups_of(
+    lambda z, y, x, core: (y if core else z, x, core), lambda z, y, x, core: z if core else y
+)
 CHIP = groups_of(lambda z, y, x, core: (z, y, x), lambda z, y, x, core: core)
 ROW = groups_of(lambda z, y, x, core: (z, y, core), lambda z, y, x, core: x)
 COLUMNS = groups_of(lambda z, y, x, core: (z, y), lambda z, y, x, core: (x, core))
@@ -153,37 +154,135 @@
     return jnp.transpose(split, (1, 3, 0, 2, 4) + tuple(range(5, split.ndim))).reshape(blocks.shape)
 
 
-def from_tiles(blocks):
-    rest = blocks.shape[2:]
-    split = blocks.reshape((2, 2, SIDE // 2, SIDE // 2, -1) + rest)
-    order = (2, 0, 3, 1, 4) + tuple(range(5, split.ndim))
-    return jnp.transpose(split, order).reshape((-1,) + rest)
-
-
 def nt_dot(a, b, precision=None):
     return lax.dot_general(
         a, b, (((1,), (1,)), ((), ())), precision=precision, preferred_element_type=jnp.float32
     )
 
 
+def halves(block):
+    middle = block.shape[1] // 2
+    return jnp.concatenate([block[:, :middle], block[:, middle:]], axis=0)
+
+
+def split_row(row, share):
+    return row // (2 * share), row // share % 2, row % share
+
+
+def exact_dot(a, selection):
+    high = a.astype(jnp.bfloat16)
+    rest = a - high.astype(jnp.float32)
+    middle = rest.astype(jnp.bfloat16)
+    low = (rest - middle.astype(jnp.float32)).astype(jnp.bfloat16)
+    dot = functools.partial(jnp.dot, preferred_element_type=jnp.float32)
+    return dot(high, selection) + (dot(middle, selection) + dot(low, selection))
+
+
+def basis_kernel(momentum_ref, gradient_ref, factor_ref, blended_ref, copies_ref, *, share):
+    blended = (
+        momentum_ref[...].astype(jnp.float32) + gradient_ref[...].astype(jnp.float32)
+    ).astype(jnp.bfloat16)
+    blended_ref[...] = blended
+    height, half = factor_ref.shape
+    rank = height // 2
+    place, part, low = split_row(lax.broadcasted_iota(jnp.int32, (height, rank), 0), share)
+    parity, tile_index = place // 16, place % 16
+    z = tile_index // 4 * 2 + parity // 2
+    y = tile_index % 4 * 2 + parity % 2
+    chosen = (z * SIDE + y) * share + low == lax.broadcasted_iota(jnp.int32, (height, rank), 1)
+    result = None
+    for h in range(2):
+        product = nt_dot(blended[:, h * half : (h + 1) * half], factor_ref[...])
+        selection = (chosen & (part == h)).astype(jnp.bfloat16)
+        picked = exact_dot(product, selection)
+        result = picked if result is None else result + picked
+    for copy in range(copies_ref.shape[0]):
+        copies_ref[copy] = result
+
+
+def basis_part(momentum, gradient, factor, share):
+    rows, cols = momentum.shape
+    vmem = pl.BlockSpec(memory_space=pltpu.VMEM)
+    return pl.pallas_call(
+        functools.partial(basis_kernel, share=share),
+        out_shape=(
+            jax.ShapeDtypeStruct((rows, cols), jnp.bfloat16),
+            jax.ShapeDtypeStruct((CORES, rows, factor.shape[0] // 2), jnp.float32),
+        ),
+        in_specs=[vmem] * 3,
+        out_specs=(vmem, vmem),
+        compiler_params=pltpu.CompilerParams(vmem_limit_bytes=32 << 20),
+        name="basis_part",
+    )(momentum, gradient, factor)
+
+
+def half_columns(ortho, height, share, h):
+    rank = ortho.shape[1]
+    place, part, low = split_row(lax.broadcasted_iota(jnp.int32, (rank, height), 1), share)
+    source = lax.broadcasted_iota(jnp.int32, (rank, height), 0)
+    selection = ((place * share + low == source) & (part == h)).astype(jnp.bfloat16)
+    return jnp.dot(ortho, selection, preferred_element_type=jnp.float32).astype(jnp.bfloat16)
+
+
+def momentum_kernel(ortho_ref, projection_ref, blended_ref, out_ref, *, share):
+    height, half = projection_ref.shape
+    for h in range(2):
+        columns = slice(h * half, (h + 1) * half)
+        left = half_columns(ortho_ref[...], height, share, h)
+        carried = jnp.dot(left, projection_ref[...], preferred_element_type=jnp.float32)
+        out_ref[:, columns] = (
+            blended_ref[:, columns].astype(jnp.float32) - (1.0 - MOMENTUM_DECAY) * carried
+        ).astype(jnp.bfloat16)
+
+
+def update_kernel(ortho_ref, projection_ref, squares_ref, out_ref, *, share, scale):
+    height, half = projection_ref.shape
+    rank = height // 2
+    squares = jnp.broadcast_to(jnp.sum(squares_ref[...], axis=0), (8, height))
+    place, _, low = split_row(lax.broadcasted_iota(jnp.int32, (height, rank), 0), share)
+    target = lax.broadcasted_iota(jnp.int32, (height, rank), 1)
+    fold = (place * share + low == target).astype(jnp.float32)
+    norms = jnp.sqrt(jnp.dot(squares, fold, precision=HIGHEST, preferred_element_type=jnp.float32))
+    inverse = 1.0 / (norms[0:1] + EPSILON)
+    scaled = (ortho_ref[...].astype(jnp.float32) * inverse).astype(jnp.bfloat16)
+    for h in range(2):
+        left = half_columns(scaled, height, share, h)
+        direction = jnp.dot(left, projection_ref[...], preferred_element_type=jnp.float32)
+        out_ref[:, h * half : (h + 1) * half] = (scale * direction).astype(jnp.bfloat16)
+
+
+def output_call(kernel, name, ortho, projection, extra):
+    rows, cols = ortho.shape[0], 2 * projection.shape[1]
+    vmem = pl.BlockSpec(memory_space=pltpu.VMEM)
+    return pl.pallas_call(
+        kernel,
+        out_shape=jax.ShapeDtypeStruct((rows, cols), jnp.bfloat16),
+        in_specs=[vmem] * 3,
+        out_specs=vmem,
+        compiler_params=pltpu.CompilerParams(vmem_limit_bytes=32 << 20),
+        cost_estimate=pl.CostEstimate(
+            flops=8 * rows * cols * ortho.shape[1], bytes_accessed=4 * rows * cols, transcendentals=0
+        ),
+        name=name,
+    )(ortho, projection, extra)
+
+
 def body(momentum, gradient, right_factor):
     rows, cols = momentum.shape
-    share_rank = right_factor.shape[0]
+    share = right_factor.shape[0]
     groups, columns = SIDE * SIDE, LINE * CORES
     tiles = groups // 4
-    rank = share_rank * groups
-    blended = (momentum.astype(jnp.float32) + gradient.astype(jnp.float32)).astype(jnp.bfloat16)
+    rank = share * groups
     with jax.named_scope("factor_gather"):
-        whole_factor = from_tiles(
-            spread_rows(right_factor).reshape(4, tiles * share_rank, cols)
-        )
+        whole_factor = spread_rows(halves(right_factor)).reshape(2 * rank, cols // 2)
     with jax.named_scope("basis"):
-        basis = total(total(nt_dot(blended, whole_factor), CHIP), ROW)
+        blended, copies = basis_part(momentum, gradient, whole_factor, share)
+        basis = total(add_up(exchange(copies, CHIP)), ROW)
     with jax.named_scope("gram"):
-        share = rank // columns
-        part = lax.dynamic_slice_in_dim(basis.T, lax.axis_index("tp") * share, share, 0)
+        width = rank // columns
+        part = lax.dynamic_slice_in_dim(basis.T, lax.axis_index("tp") * width, width, 0)
         part = jnp.dot(part, basis, precision=HIGHEST)
-        part = total(total(total(part, FAR), MIDDLE), NEAR)
+        part = total(total(part, FIRST_LINE), SECOND_LINE)
         gram = spread(part, COLUMNS).reshape(rank, rank)
     with jax.named_scope("solve"):
         inverse = to_tiles(inverse_factor(gram))
@@ -192,28 +291,31 @@
         partial = lax.dot_general(
             ortho_basis, blended, (((0,), (0,)), ((), ())), preferred_element_type=jnp.float32
         ).astype(jnp.bfloat16)
-        partial = exchange(partial.reshape(4, tiles * share_rank, cols), NEAR)
+        partial = exchange(partial.reshape(4, tiles * share, cols), NEAR)
         partial = add_up(partial).astype(jnp.bfloat16)
-        partial = exchange(partial.reshape(tiles, share_rank, cols), STRIDED)
+        partial = exchange(partial.reshape(tiles, share, cols), STRIDED)
         own = add_up(partial)
-        projection = spread_rows(own.astype(jnp.bfloat16)).reshape(rank, cols)
+        projection = spread_rows(halves(own.astype(jnp.bfloat16))).reshape(2 * rank, cols // 2)
     with jax.named_scope("norms"):
         wide = projection.astype(jnp.float32)
-        squares = total(jnp.sum(wide * wide, axis=1)[None], COLUMNS)[0]
-        norms = jnp.sqrt(squares) + EPSILON
+        squares = spread(jnp.sum(wide * wide, axis=1)[None], COLUMNS)
     with jax.named_scope("outputs"):
-        carried = jnp.dot(ortho_basis, projection, preferred_element_type=jnp.float32)
-        momentum_next = (blended.astype(jnp.float32) - (1.0 - MOMENTUM_DECAY) * carried).astype(
-            jnp.bfloat16
+        momentum_next = output_call(
+            functools.partial(momentum_kernel, share=share),
+            "momentum_next", ortho_basis, projection, blended,
         )
-        scale_factor = math.sqrt(rows * groups * cols * columns / rank)
-        factor = (wide / norms[:, None]).astype(jnp.bfloat16)
-        direction = jnp.dot(ortho_basis, factor, preferred_element_type=jnp.float32)
-        update = (scale_factor * direction).astype(jnp.bfloat16)
-        z, y = lax.axis_index("fsdp") // SIDE, lax.axis_index("fsdp") % SIDE
-        place = ((z % 2 * 2 + y % 2) * tiles + z // 2 * (SIDE // 2) + y // 2) * share_rank
-        own_norms = lax.dynamic_slice_in_dim(norms, place, share_rank, 0)
-        factor_next = own / own_norms[:, None]
+        scale = math.sqrt(rows * groups * cols * columns / rank)
+        update = output_call(
+            functools.partial(update_kernel, share=share, scale=scale),
+            "update", ortho_basis, projection, squares,
+        )
+        z, y = lax.div(lax.axis_index("fsdp"), SIDE), lax.rem(lax.axis_index("fsdp"), SIDE)
+        place = (lax.rem(z, 2) * 2 + lax.rem(y, 2)) * tiles + lax.div(z, 2) * (SIDE // 2) + lax.div(y, 2)
+        own_squares = lax.dynamic_slice(
+            squares, (0, 0, place * 2 * share), (columns, 1, 2 * share)
+        )
+        own_squares = jnp.sum(own_squares.reshape(2 * columns, share), axis=0)
+        factor_next = own / (jnp.sqrt(own_squares) + EPSILON)[:, None]
     return (momentum_next, factor_next, update)
 
 

time: 233 us -> 216 us (0.927)
  local copies, waits for them, and re-layouts: 15.7 us -> 4.32 us
  blocking collectives: 162 us -> 155 us
  Pallas kernels: 9.43 us -> 15.8 us
  matrix products: 6.54 us -> 1.36 us
    reshape x2 -> x1, local copies, waits for them, and re-layouts: 6.84 us -> 0.07 us  [body(): own_squares = jnp.sum(own_squares.reshape(2 * columns, share), axis=0)]
    all_to_all x10 -> x9, blocking collectives: 162 us -> 155 us  [exchange(): lax.all_to_all(blocks, AXES, 0, 0, axis_index_groups=groups, tiled=True)]
    pallas_call x0 -> x3, Pallas kernels: none -> 6.36 us  [the longest x2 4.4 us: output_call(): pl.pallas_call(kernel, out_shape=jax.ShapeDtypeStruct((rows, cols), jnp.b...]
    dot_general x2 -> x0, matrix products: 4.48 us -> none  [the longest x1 2.98 us: body(): jnp.dot(ortho_basis, projection, preferred_element_type=jnp.float32)]
  transfers between devices with their start and end apart: 3 -> 3, of which waited for: 3 -> 3; matrix products, arithmetic and copies ran while one was open for 1% -> 0% of each run, Pallas kernels for 0% -> 1%
where the time goes in v3:
time: 216 us; the launch traced here: 215 us
  blocking collectives  155 us (72%)
  waiting for transfers between devices  24.7 us (11%)
  Pallas kernels  15.8 us (7%)
  starting transfers between devices  11.5 us (5%)
  local copies, waits for them, and re-layouts  4.32 us (2%)
    all_to_all x9, blocking collectives, exchange(): lax.all_to_all(blocks, AXES, 0, 0, axis_index_groups=groups, tiled=True)  155 us
    all_to_all x3, waiting for transfers between devices, exchange(): lax.all_to_all(blocks, AXES, 0, 0, axis_index_groups=groups, tiled=True)  24.7 us
    all_to_all x3, starting transfers between devices, exchange(): lax.all_to_all(blocks, AXES, 0, 0, axis_index_groups=groups, tiled=True)  11.5 us
    pallas_call x1, Pallas kernels, inverse_factor(): pl.pallas_call(functools.partial(factor_kernel, size=size), out_shape=jax...  9.43 us
    pallas_call x2, Pallas kernels, output_call(): pl.pallas_call(kernel, out_shape=jax.ShapeDtypeStruct((rows, cols), jnp.b...  4.4 us
  transfers between devices with their start and end apart: 3, of which 3 were waited for; matrix products, arithmetic and copies ran while one was open for 0% of the time, Pallas kernels for 1%

profile of v3, /device:TPU:1, one launch (start us, length us, event | category | flops | bytes accessed | tf_op | source)
XLA Modules:
  0.0 215.0 jit_solution(15677480090933967687)
XLA Ops:
  0.6 0.7 fusion.17
  1.4 32.5 %all_to_all.60 = bf16[16,8,1664]{2,1,0:T(8,128)(2,1)S(1)} all-to-all(bf16[16,8,1664]{2,1,0:T(8,128)(2,1)S(1)} %broadcast_in_dim.26), channel_id=1, replica_groups={{0,16,32,48,128,144,160,176,256,272,288,304,384,400,416,432},{1,17,33,4..., dimensions={0} | all-to-all | bytes 851968 | tf_op jit(solution)/shard_map/factor_gather/all_to_all | solution.py:129
  33.9 0.1 broadcast_in_dim.27
  34.0 0.0 copy-start
  34.0 0.0 copy-start.1
  34.1 17.9 %all_to_all.61 = bf16[4,16,8,1664]{3,2,1,0:T(8,128)(2,1)S(1)} all-to-all(bf16[4,16,8,1664]{3,2,1,0:T(8,128)(2,1)S(1)} %broadcast_in_dim.27), channel_id=1, replica_groups={{0,8,64,72},{1,57,449,505},{2,10,66,74},{3,59,451,507},{4,12,68,76},{5,..., dimensions={0} | all-to-all | bytes 3407872 | tf_op jit(solution)/shard_map/factor_gather/all_to_all | solution.py:129
  52.0 0.0 copy-done
  52.0 0.0 copy-done.1
  52.0 2.0 basis_part.1
  53.9 4.0 %all_to_all.62 = f32[2,128,256]{2,1,0:T(8,128)S(1)} all-to-all(f32[2,128,256]{2,1,0:T(8,128)S(1)} %get-tuple-element.5), channel_id=1, replica_groups={{0,1},{2,3},{4,5},{6,7},{8,9},{10,11},{12,13},{14,15},{16,17},{18,19},{..., dimensions={0} | all-to-all | bytes 524288 | tf_op jit(solution)/shard_map/basis/all_to_all | solution.py:129
  57.9 0.8 broadcast_in_dim.29
  58.8 4.0 %all-to-all-start.3 = ((f32[4,128,256]{2,1,0:T(8,128)}), f32[4,128,256]{2,1,0:T(8,128)S(1)}, u32[]{:S(2)}, u32[]{:S(2)}) async-start(f32[4,128,256]{2,1,0:T(8,128)} %broadcast_in_dim.29), calls=%async_computation.3 | async-start | bytes 1048576 | tf_op jit(solution)/shard_map/basis/all_to_all | solution.py:129
  62.8 8.9 %all-to-all-done.3 = f32[4,128,256]{2,1,0:T(8,128)S(1)} async-done(((f32[4,128,256]{2,1,0:T(8,128)}), f32[4,128,256]{2,1,0:T(8,128)S(1)}, u32[]{:S(2)}, u32[]{:S(2)}) %all-to-all-start.3) | async-done | bytes 524320 | tf_op jit(solution)/shard_map/basis/all_to_all | solution.py:129
  71.8 0.3 fusion.3
  72.1 13.5 %all_to_all.63 = f32[8,32,256]{2,1,0:T(8,128)S(1)} all-to-all(f32[8,32,256]{2,1,0:T(8,128)S(1)} %broadcast_in_dim.30), channel_id=1, replica_groups={{0,64,128,192,256,320,384,448},{1,9,17,25,33,41,49,57},{2,66,130,194,25..., dimensions={0} | all-to-all | bytes 524288 | tf_op jit(solution)/shard_map/gram/all_to_all | solution.py:129
  85.7 13.3 %all_to_all.64 = f32[8,32,256]{2,1,0:T(8,128)S(1)} all-to-all(f32[8,32,256]{2,1,0:T(8,128)S(1)} %broadcast_in_dim.32), channel_id=1, replica_groups={{0,8,16,24,32,40,48,56},{1,65,129,193,257,321,385,449},{2,10,18,26,34,4..., dimensions={0} | all-to-all | bytes 524288 | tf_op jit(solution)/shard_map/gram/all_to_all | solution.py:129
  99.0 13.3 %all_to_all.65 = f32[8,32,256]{2,1,0:T(8,128)S(1)} all-to-all(f32[8,32,256]{2,1,0:T(8,128)S(1)} %broadcast_in_dim.34), channel_id=1, replica_groups={{0,1,2,3,4,5,6,7},{8,9,10,11,12,13,14,15},{16,17,18,19,20,21,22,23},{24..., dimensions={0} | all-to-all | bytes 524288 | tf_op jit(solution)/shard_map/gram/all_to_all | solution.py:129
  112.3 9.4 %inverse_factor.1 = f32[256,256]{1,0:T(8,128)S(1)} custom-call(f32[256,256]{1,0:T(8,128)S(1)} %bitcast.30), custom_call_target="tpu_custom_call" | custom-call | flops 1000000000 | bytes 524288 | tf_op jit(solution)/shard_map/solve/inverse_factor/pallas_call | solution.py:117
  121.7 0.1 reshape.94
  121.8 0.1 reshape.95
  122.0 0.4 convolution_convert_fusion.1.ortho_ref
  122.4 0.6 convolution_convert_fusion
  123.0 17.2 %all_to_all.66 = bf16[4,64,3328]{2,1,0:T(8,128)(2,1)S(1)} all-to-all(bf16[4,64,3328]{2,1,0:T(8,128)(2,1)S(1)} %bitcast.31), channel_id=1, replica_groups={{0,8,64,72},{1,57,449,505},{2,10,66,74},{3,59,451,507},{4,12,68,76},{5,..., dimensions={0} | all-to-all | bytes 3407872 | tf_op jit(solution)/shard_map/projection/all_to_all | solution.py:129
  140.2 0.2 add_convert_fusion
  140.4 0.1 convert_element_type.111
  140.5 20.9 %all_to_all.67 = bf16[16,4,3328]{2,1,0:T(4,128)(2,1)S(1)} all-to-all(bf16[16,4,3328]{2,1,0:T(4,128)(2,1)S(1)} %convert_element_type.111), channel_id=1, replica_groups={{0,16,32,48,128,144,160,176,256,272,288,304,384,400,416,432},{1,17,33,4..., dimensions={0} | all-to-all | bytes 851968 | tf_op jit(solution)/shard_map/projection/all_to_all | solution.py:129
  161.3 0.1 bitcast_convert_fusion
  161.6 22.5 %all_to_all.68 = bf16[16,8,1664]{2,1,0:T(8,128)(2,1)S(1)} all-to-all(bf16[16,8,1664]{2,1,0:T(8,128)(2,1)S(1)} %broadcast_in_dim.35), channel_id=1, replica_groups={{0,16,32,48,128,144,160,176,256,272,288,304,384,400,416,432},{1,17,33,4..., dimensions={0} | all-to-all | bytes 851968 | tf_op jit(solution)/shard_map/projection/all_to_all | solution.py:129
  184.0 1.3 broadcast_in_dim.36
  185.3 3.6 %all-to-all-start.10 = ((bf16[4,16,8,1664]{3,2,1,0:T(8,128)(2,1)}), bf16[4,16,8,1664]{3,2,1,0:T(8,128)(2,1)S(1)}, u32[]{:S(2)}, u32[]{:S(2)}) async-start(bf16[4,16,8,1664]{3,2,1,0:T(8,128)(2,1)} %broadcast_in_dim.36), calls=%async_computation.10 | async-start | bytes 3407872 | tf_op jit(solution)/shard_map/projection/all_to_all | solution.py:129
  189.0 12.9 %all-to-all-done.10 = bf16[4,16,8,1664]{3,2,1,0:T(8,128)(2,1)S(1)} async-done(((bf16[4,16,8,1664]{3,2,1,0:T(8,128)(2,1)}), bf16[4,16,8,1664]{3,2,1,0:T(8,128)(2,1)S(1)}, u32[]{:S(2)}, u32[]{:S(2)}) %all-to-all-start.10) | async-done | bytes 1703968 | tf_op jit(solution)/shard_map/projection/all_to_all | solution.py:129
  201.9 0.4 multiply_reduce_fusion
  202.3 0.1 broadcast_in_dim.74
  202.4 0.6 broadcast_in_dim.75
  203.0 3.9 %all-to-all-start.11 = ((f32[8,1,512]{2,1,0:T(1,128)}), f32[8,1,512]{2,1,0:T(1,128)S(1)}, u32[]{:S(2)}, u32[]{:S(2)}) async-start(f32[8,1,512]{2,1,0:T(1,128)} %broadcast_in_dim.75), calls=%async_computation.11 | async-start | bytes 32768 | tf_op jit(solution)/shard_map/norms/all_to_all | solution.py:129
  206.9 1.9 momentum_next.1
  208.7 2.8 %all-to-all-done.11.squares_ref = f32[8,1,512]{2,1,0:T(1,128)S(1)} async-done(((f32[8,1,512]{2,1,0:T(1,128)}), f32[8,1,512]{2,1,0:T(1,128)S(1)}, u32[]{:S(2)}, u32[]{:S(2)}) %all-to-all-start.11) | async-done | bytes 16416 | tf_op jit(solution)/shard_map/norms/all_to_all | solution.py:129
  211.5 0.1 dynamic-slice_reduce_fusion
  211.6 0.1 reshape.98
  211.7 0.7 bitcast_divide_fusion
  212.4 2.5 %update.1 = bf16[128,3328]{1,0:T(8,128)(2,1)} custom-call(bf16[128,256]{1,0:T(8,128)(2,1)S(1)} %convolution_convert_fusion.1.ortho_ref, bf16[512,1664]{1,0:T(8,128)(2,1)S(1)} %bitcast.28, f32[8,1,512]{2,1,0:T(1,128)S(1)} %all-to-all-done.11.squares_ref), custom_call_target="tpu_custom_call" | custom-call | flops 872415232 | bytes 1703936 | tf_op jit(solution)/shard_map/outputs/update/pallas_call | solution.py:257
  (15 shorter events, 0.3 us)
Async XLA Ops:
  34.0 17.9 %copy-start = (bf16[128,3328]{1,0:T(8,128)(2,1)S(1)}, bf16[128,3328]{1,0:T(8,128)(2,1)}, u32[]{:S(2)}) copy-start(bf16[128,3328]{1,0:T(8,128)(2,1)} %momentum_ref.1) | copy-start | bytes 2555908
  34.0 17.9 %copy-start.1 = (bf16[128,3328]{1,0:T(8,128)(2,1)S(1)}, bf16[128,3328]{1,0:T(8,128)(2,1)}, u32[]{:S(2)}) copy-start(bf16[128,3328]{1,0:T(8,128)(2,1)} %gradient_ref.1) | copy-start | bytes 2555908
  58.8 12.9 %all-to-all-start.3 = ((f32[4,128,256]{2,1,0:T(8,128)}), f32[4,128,256]{2,1,0:T(8,128)S(1)}, u32[]{:S(2)}, u32[]{:S(2)}) async-start(f32[4,128,256]{2,1,0:T(8,128)} %broadcast_in_dim.29), calls=%async_computation.3 | async-start | bytes 1048576 | tf_op jit(solution)/shard_map/basis/all_to_all | solution.py:129
  185.3 16.5 %all-to-all-start.10 = ((bf16[4,16,8,1664]{3,2,1,0:T(8,128)(2,1)}), bf16[4,16,8,1664]{3,2,1,0:T(8,128)(2,1)S(1)}, u32[]{:S(2)}, u32[]{:S(2)}) async-start(bf16[4,16,8,1664]{3,2,1,0:T(8,128)(2,1)} %broadcast_in_dim.36), calls=%async_computation.10 | async-start | bytes 3407872 | tf_op jit(solution)/shard_map/projection/all_to_all | solution.py:129
  203.0 8.5 %all-to-all-start.11 = ((f32[8,1,512]{2,1,0:T(1,128)}), f32[8,1,512]{2,1,0:T(1,128)S(1)}, u32[]{:S(2)}, u32[]{:S(2)}) async-start(f32[8,1,512]{2,1,0:T(1,128)} %broadcast_in_dim.75), calls=%async_computation.11 | async-start | bytes 32768 | tf_op jit(solution)/shard_map/norms/all_to_all | solution.py:129

commit v4 on v3

--- a/solution.py
+++ b/solution.py
@@ -37,18 +37,13 @@
 STRIDED = groups_of(
     lambda z, y, x, core: (z % 2, y % 2, x, core), lambda z, y, x, core: (z // 2, y // 2)
 )
-FIRST_LINE = groups_of(
-    lambda z, y, x, core: (z if core else y, x, core), lambda z, y, x, core: y if core else z
-)
-SECOND_LINE = groups_of(
-    lambda z, y, x, core: (y if core else z, x, core), lambda z, y, x, core: z if core else y
-)
+PLANE = groups_of(lambda z, y, x, core: (x, core), lambda z, y, x, core: (z, y))
 CHIP = groups_of(lambda z, y, x, core: (z, y, x), lambda z, y, x, core: core)
 ROW = groups_of(lambda z, y, x, core: (z, y, core), lambda z, y, x, core: x)
 COLUMNS = groups_of(lambda z, y, x, core: (z, y), lambda z, y, x, core: (x, core))
 
 FACTOR_BLOCK = 64
-FACTOR_GROUP = 8
+FACTOR_GROUP = 16
 
 
 def block_inverse(block, size):
@@ -79,8 +74,8 @@
     return work[:, size : 2 * size]
 
 
-def factor_kernel(gram_ref, inverse_ref, *, size):
-    inverse_ref[...] = gram_ref[...]
+def factor_in_place(inverse_ref):
+    size = inverse_ref.shape[0]
     step = FACTOR_BLOCK
     for k in range(0, size, step):
         after = k + step
@@ -93,13 +88,7 @@
             pieces = [panel[:, :k]] + pieces
         if after < size:
             pieces = pieces + [panel[:, after:]]
-            lower = lax.dot_general(
-                inverse_ref[after:, k:after],
-                inverse,
-                (((1,), (1,)), ((), ())),
-                precision=HIGHEST,
-                preferred_element_type=jnp.float32,
-            )
+            lower = nt_dot(inverse_ref[after:, k:after], inverse, HIGHEST)
         panel = jnp.concatenate(pieces, axis=1)
         inverse_ref[k:after, :] = panel
         if after < size:
@@ -107,22 +96,57 @@
             inverse_ref[after:, :] = inverse_ref[after:, :] - jnp.dot(
                 lower, panel, precision=HIGHEST, preferred_element_type=jnp.float32
             )
-    row = lax.broadcasted_iota(jnp.int32, (size, size), 0)
-    col = lax.broadcasted_iota(jnp.int32, (size, size), 1)
-    inverse_ref[...] = jnp.where(row >= col, inverse_ref[...], 0.0)
-
-
-def inverse_factor(gram):
-    size = gram.shape[0]
+
+
+def gram_kernel(parts_ref, basis_ref, blocks_ref):
+    basis = (parts_ref[0] + parts_ref[1]) + (parts_ref[2] + parts_ref[3])
+    basis_ref[...] = basis
+    gram = jnp.dot(basis.T, basis, precision=HIGHEST, preferred_element_type=jnp.float32)
+    halves_of_row = gram.shape[1] // 128
+    for block in range(blocks_ref.shape[0]):
+        row, col = 8 * (block // halves_of_row), 128 * (block % halves_of_row)
+        blocks_ref[block] = gram[row : row + 8, col : col + 128]
+
+
+def copies_kernel(parts_ref, copies_ref):
+    copies_ref[...] = jnp.broadcast_to(jnp.sum(parts_ref[...], axis=0)[None], copies_ref.shape)
+
+
+def solve_kernel(blocks_ref, basis_ref, ortho_ref, inverse_ref, *, share):
+    size = inverse_ref.shape[0]
+    for block in range(blocks_ref.shape[0]):
+        row, col = 8 * (block // (size // 128)), 128 * (block % (size // 128))
+        inverse_ref[row : row + 8, col : col + 128] = blocks_ref[block]
+    factor_in_place(inverse_ref)
+    source = lax.broadcasted_iota(jnp.int32, (size, size), 0)
+    target = lax.broadcasted_iota(jnp.int32, (size, size), 1)
+    inverse = jnp.where(source >= target, inverse_ref[...], 0.0)
+    ortho = nt_dot(basis_ref[...], inverse, HIGHEST).astype(jnp.bfloat16)
+    selection = (device_of(target // share) * share + target % share == source).astype(jnp.bfloat16)
+    ortho_ref[...] = jnp.dot(ortho, selection, preferred_element_type=jnp.float32).astype(
+        jnp.bfloat16
+    )
+
+
+VMEM = pl.BlockSpec(memory_space=pltpu.VMEM)
+
+
+def local_call(kernel, name, shapes, *operands, scratch=(), flops=0):
+    size = sum(math.prod(o.shape) * o.dtype.itemsize for o in operands)
     return pl.pallas_call(
-        functools.partial(factor_kernel, size=size),
-        out_shape=jax.ShapeDtypeStruct((size, size), jnp.float32),
-        in_specs=[pl.BlockSpec(memory_space=pltpu.VMEM)],
-        out_specs=pl.BlockSpec(memory_space=pltpu.VMEM),
+        kernel,
+        out_shape=shapes,
+        in_specs=[VMEM] * len(operands),
+        out_specs=jax.tree.map(lambda _: VMEM, shapes),
+        scratch_shapes=scratch,
         compiler_params=pltpu.CompilerParams(vmem_limit_bytes=32 << 20),
-        cost_estimate=pl.CostEstimate(flops=10**9, bytes_accessed=1 << 19, transcendentals=512),
-        name="inverse_factor",
-    )(gram)
+        cost_estimate=pl.CostEstimate(flops=flops, bytes_accessed=2 * size, transcendentals=0),
+        name=name,
+    )(*operands)
+
+
+def shaped(*shape, dtype=jnp.float32):
+    return jax.ShapeDtypeStruct(shape, dtype)
 
 
 def exchange(blocks, groups):
@@ -148,10 +172,11 @@
     return add_up(spread(block, groups))
 
 
-def to_tiles(blocks):
-    rest = blocks.shape[1:]
-    split = blocks.reshape((SIDE // 2, 2, SIDE // 2, 2, -1) + rest)
-    return jnp.transpose(split, (1, 3, 0, 2, 4) + tuple(range(5, split.ndim))).reshape(blocks.shape)
+def device_of(place):
+    parity, tile_index = place // 16, place % 16
+    z = tile_index // 4 * 2 + parity // 2
+    y = tile_index % 4 * 2 + parity % 2
+    return z * SIDE + y
 
 
 def nt_dot(a, b, precision=None):
@@ -186,10 +211,7 @@
     height, half = factor_ref.shape
     rank = height // 2
     place, part, low = split_row(lax.broadcasted_iota(jnp.int32, (height, rank), 0), share)
-    parity, tile_index = place // 16, place % 16
-    z = tile_index // 4 * 2 + parity // 2
-    y = tile_index % 4 * 2 + parity % 2
-    chosen = (z * SIDE + y) * share + low == lax.broadcasted_iota(jnp.int32, (height, rank), 1)
+    chosen = device_of(place) * share + low == lax.broadcasted_iota(jnp.int32, (height, rank), 1)
     result = None
     for h in range(2):
         product = nt_dot(blended[:, h * half : (h + 1) * half], factor_ref[...])
@@ -198,22 +220,6 @@
         result = picked if result is None else result + picked
     for copy in range(copies_ref.shape[0]):
         copies_ref[copy] = result
-
-
-def basis_part(momentum, gradient, factor, share):
-    rows, cols = momentum.shape
-    vmem = pl.BlockSpec(memory_space=pltpu.VMEM)
-    return pl.pallas_call(
-        functools.partial(basis_kernel, share=share),
-        out_shape=(
-            jax.ShapeDtypeStruct((rows, cols), jnp.bfloat16),
-            jax.ShapeDtypeStruct((CORES, rows, factor.shape[0] // 2), jnp.float32),
-        ),
-        in_specs=[vmem] * 3,
-        out_specs=(vmem, vmem),
-        compiler_params=pltpu.CompilerParams(vmem_limit_bytes=32 << 20),
-        name="basis_part",
-    )(momentum, gradient, factor)
 
 
 def half_columns(ortho, height, share, h):
@@ -235,36 +241,48 @@
         ).astype(jnp.bfloat16)
 
 
-def update_kernel(ortho_ref, projection_ref, squares_ref, out_ref, *, share, scale):
+def squares_kernel(projection_ref, copies_ref):
+    height, half = projection_ref.shape
+    wide = projection_ref[...].astype(jnp.float32)
+    squares = wide * wide
+    high = squares.astype(jnp.bfloat16)
+    low = (squares - high.astype(jnp.float32)).astype(jnp.bfloat16)
+    ones = jnp.ones((8, half), jnp.bfloat16)
+    sums = nt_dot(ones, high) + nt_dot(ones, low)
+    copies_ref[...] = jnp.zeros(copies_ref.shape, jnp.float32)
+    for copy in range(copies_ref.shape[0]):
+        for piece in range(height // 128):
+            copies_ref[copy, piece : piece + 1, :] = sums[0:1, piece * 128 : (piece + 1) * 128]
+
+
+def update_kernel(
+    ortho_ref, projection_ref, squares_ref, own_ref, out_ref, factor_ref, *, share, scale
+):
     height, half = projection_ref.shape
     rank = height // 2
-    squares = jnp.broadcast_to(jnp.sum(squares_ref[...], axis=0), (8, height))
+    pieces = jnp.sum(squares_ref[...], axis=0)
+    squares = jnp.concatenate([pieces[i : i + 1] for i in range(height // 128)], axis=1)
     place, _, low = split_row(lax.broadcasted_iota(jnp.int32, (height, rank), 0), share)
     target = lax.broadcasted_iota(jnp.int32, (height, rank), 1)
     fold = (place * share + low == target).astype(jnp.float32)
-    norms = jnp.sqrt(jnp.dot(squares, fold, precision=HIGHEST, preferred_element_type=jnp.float32))
-    inverse = 1.0 / (norms[0:1] + EPSILON)
-    scaled = (ortho_ref[...].astype(jnp.float32) * inverse).astype(jnp.bfloat16)
+    squares = jnp.dot(
+        jnp.broadcast_to(squares, (8, height)),
+        fold,
+        precision=HIGHEST,
+        preferred_element_type=jnp.float32,
+    )
+    inverse = 1.0 / (jnp.sqrt(squares) + EPSILON)
+    scaled = (ortho_ref[...].astype(jnp.float32) * inverse[0:1]).astype(jnp.bfloat16)
     for h in range(2):
         left = half_columns(scaled, height, share, h)
         direction = jnp.dot(left, projection_ref[...], preferred_element_type=jnp.float32)
         out_ref[:, h * half : (h + 1) * half] = (scale * direction).astype(jnp.bfloat16)
-
-
-def output_call(kernel, name, ortho, projection, extra):
-    rows, cols = ortho.shape[0], 2 * projection.shape[1]
-    vmem = pl.BlockSpec(memory_space=pltpu.VMEM)
-    return pl.pallas_call(
-        kernel,
-        out_shape=jax.ShapeDtypeStruct((rows, cols), jnp.bfloat16),
-        in_specs=[vmem] * 3,
-        out_specs=vmem,
-        compiler_params=pltpu.CompilerParams(vmem_limit_bytes=32 << 20),
-        cost_estimate=pl.CostEstimate(
-            flops=8 * rows * cols * ortho.shape[1], bytes_accessed=4 * rows * cols, transcendentals=0
-        ),
-        name=name,
-    )(ortho, projection, extra)
+    column = lax.broadcasted_iota(jnp.int32, (8, rank), 1)
+    natural = device_of(column // share) * share + column % share
+    first = lax.axis_index("fsdp") * share
+    mine = natural == first + lax.broadcasted_iota(jnp.int32, (8, rank), 0)
+    own_inverse = jnp.sum(jnp.where(mine, inverse, 0.0), axis=1, keepdims=True)
+    factor_ref[...] = own_ref[...] * own_inverse[0:share]
 
 
 def body(momentum, gradient, right_factor):
@@ -276,17 +294,32 @@
     with jax.named_scope("factor_gather"):
         whole_factor = spread_rows(halves(right_factor)).reshape(2 * rank, cols // 2)
     with jax.named_scope("basis"):
-        blended, copies = basis_part(momentum, gradient, whole_factor, share)
-        basis = total(add_up(exchange(copies, CHIP)), ROW)
+        blended, copies = local_call(
+            functools.partial(basis_kernel, share=share),
+            "basis_part",
+            (shaped(rows, cols, dtype=jnp.bfloat16), shaped(CORES, rows, rank)),
+            momentum, gradient, whole_factor,
+        )
+        parts = spread(add_up(exchange(copies, CHIP)), ROW)
     with jax.named_scope("gram"):
-        width = rank // columns
-        part = lax.dynamic_slice_in_dim(basis.T, lax.axis_index("tp") * width, width, 0)
-        part = jnp.dot(part, basis, precision=HIGHEST)
-        part = total(total(part, FIRST_LINE), SECOND_LINE)
-        gram = spread(part, COLUMNS).reshape(rank, rank)
+        basis, blocks = local_call(
+            gram_kernel,
+            "gram_part",
+            (shaped(rows, rank), shaped(groups, 8, rank * rank // groups // 8)),
+            parts,
+        )
+        parts = exchange(blocks, PLANE)
+        copies = local_call(copies_kernel, "gram_copies", shaped(*parts.shape), parts)
+        blocks = exchange(copies, PLANE)
     with jax.named_scope("solve"):
-        inverse = to_tiles(inverse_factor(gram))
-        ortho_basis = nt_dot(basis, inverse, HIGHEST).astype(jnp.bfloat16)
+        ortho_basis = local_call(
+            functools.partial(solve_kernel, share=share),
+            "ortho_basis",
+            shaped(rows, rank, dtype=jnp.bfloat16),
+            blocks, basis,
+            scratch=[pltpu.VMEM((rank, rank), jnp.float32)],
+            flops=10**9,
+        )
     with jax.named_scope("projection"):
         partial = lax.dot_general(
             ortho_basis, blended, (((0,), (0,)), ((), ())), preferred_element_type=jnp.float32
@@ -297,25 +330,24 @@
         own = add_up(partial)
         projection = spread_rows(halves(own.astype(jnp.bfloat16))).reshape(2 * rank, cols // 2)
     with jax.named_scope("norms"):
-        wide = projection.astype(jnp.float32)
-        squares = spread(jnp.sum(wide * wide, axis=1)[None], COLUMNS)
+        copies = local_call(squares_kernel, "squares", shaped(columns, 8, 128), projection)
+        squares = exchange(copies, COLUMNS)
     with jax.named_scope("outputs"):
-        momentum_next = output_call(
+        momentum_next = local_call(
             functools.partial(momentum_kernel, share=share),
-            "momentum_next", ortho_basis, projection, blended,
+            "momentum_next",
+            shaped(rows, cols, dtype=jnp.bfloat16),
+            ortho_basis, projection, blended,
+            flops=8 * rows * cols * rank,
         )
         scale = math.sqrt(rows * groups * cols * columns / rank)
-        update = output_call(
+        update, factor_next = local_call(
             functools.partial(update_kernel, share=share, scale=scale),
-            "update", ortho_basis, projection, squares,
-        )
-        z, y = lax.div(lax.axis_index("fsdp"), SIDE), lax.rem(lax.axis_index("fsdp"), SIDE)
-        place = (lax.rem(z, 2) * 2 + lax.rem(y, 2)) * tiles + lax.div(z, 2) * (SIDE // 2) + lax.div(y, 2)
-        own_squares = lax.dynamic_slice(
-            squares, (0, 0, place * 2 * share), (columns, 1, 2 * share)
-        )
-        own_squares = jnp.sum(own_squares.reshape(2 * columns, share), axis=0)
-        factor_next = own / (jnp.sqrt(own_squares) + EPSILON)[:, None]
+            "update",
+            (shaped(rows, cols, dtype=jnp.bfloat16), shaped(share, cols)),
+            ortho_basis, projection, squares, own,
+            flops=8 * rows * cols * rank,
+        )
     return (momentum_next, factor_next, update)
 
 

time: 216 us -> 210 us (0.972)
  blocking collectives: 155 us -> 181 us
  waiting for transfers between devices: 24.7 us -> 2.85 us
  starting transfers between devices: 11.5 us -> 4.46 us
  local copies, waits for them, and re-layouts: 4.32 us -> 1.2 us
    all_to_all x9 -> x10, blocking collectives: 155 us -> 181 us  [exchange(): lax.all_to_all(blocks, AXES, 0, 0, axis_index_groups=groups, tiled=True)]
    all_to_all x3 -> x1, waiting for transfers between devices: 24.7 us -> 2.85 us  [exchange(): lax.all_to_all(blocks, AXES, 0, 0, axis_index_groups=groups, tiled=True)]
    all_to_all x3 -> x1, starting transfers between devices: 11.5 us -> 4.46 us  [exchange(): lax.all_to_all(blocks, AXES, 0, 0, axis_index_groups=groups, tiled=True)]
    broadcast_in_dim x10 -> x5, local copies, waits for them, and re-layouts: 3.1 us -> 0.34 us  [spread(): jnp.broadcast_to(block[None], (len(groups[0]),) + block.shape)]
    pallas_call x4 -> x7, Pallas kernels: 15.8 us -> 17.5 us  [local_call(): pl.pallas_call(kernel, out_shape=shapes, in_specs=[VMEM] * len(operands),...]
  transfers between devices with their start and end apart: 3 -> 1, of which waited for: 3 -> 1; matrix products, arithmetic and copies ran while one was open for 0% -> 0% of each run, Pallas kernels for 1% -> 1%
where the time goes in v4:
time: 210 us; the launch traced here: 209 us
  blocking collectives  181 us (86%)
  Pallas kernels  17.5 us (8%)
  starting transfers between devices  4.46 us (2%)
  waiting for transfers between devices  2.85 us (1%)
    all_to_all x10, blocking collectives, exchange(): lax.all_to_all(blocks, AXES, 0, 0, axis_index_groups=groups, tiled=True)  181 us
    pallas_call x7, Pallas kernels, local_call(): pl.pallas_call(kernel, out_shape=shapes, in_specs=[VMEM] * len(operands),...  17.5 us
    all_to_all x1, starting transfers between devices, exchange(): lax.all_to_all(blocks, AXES, 0, 0, axis_index_groups=groups, tiled=True)  4.46 us
  transfers between devices with their start and end apart: 1, of which 1 were waited for; matrix products, arithmetic and copies ran while one was open for 0% of the time, Pallas kernels for 1%

profile of v4, /device:TPU:1, one launch (start us, length us, event | category | flops | bytes accessed | tf_op | source)
XLA Modules:
  0.0 208.8 jit_solution(10076108410806456089)
XLA Ops:
  0.6 0.7 fusion.3
  1.4 32.5 %all_to_all.55 = bf16[16,8,1664]{2,1,0:T(8,128)(2,1)S(1)} all-to-all(bf16[16,8,1664]{2,1,0:T(8,128)(2,1)S(1)} %broadcast_in_dim.12), channel_id=1, replica_groups={{0,16,32,48,128,144,160,176,256,272,288,304,384,400,416,432},{1,17,33,4..., dimensions={0} | all-to-all | bytes 851968 | tf_op jit(solution)/shard_map/factor_gather/all_to_all | solution.py:153
  33.9 0.1 broadcast_in_dim.13
  34.0 0.0 copy-start
  34.0 0.0 copy-start.1
  34.1 17.9 %all_to_all.56 = bf16[4,16,8,1664]{3,2,1,0:T(8,128)(2,1)S(1)} all-to-all(bf16[4,16,8,1664]{3,2,1,0:T(8,128)(2,1)S(1)} %broadcast_in_dim.13), channel_id=1, replica_groups={{0,8,64,72},{1,57,449,505},{2,10,66,74},{3,59,451,507},{4,12,68,76},{5,..., dimensions={0} | all-to-all | bytes 3407872 | tf_op jit(solution)/shard_map/factor_gather/all_to_all | solution.py:153
  52.0 0.0 copy-done
  52.0 0.0 copy-done.1
  52.0 1.9 basis_part.1
  53.9 4.0 %all_to_all.57 = f32[2,128,256]{2,1,0:T(8,128)S(1)} all-to-all(f32[2,128,256]{2,1,0:T(8,128)S(1)} %get-tuple-element.9), channel_id=1, replica_groups={{0,1},{2,3},{4,5},{6,7},{8,9},{10,11},{12,13},{14,15},{16,17},{18,19},{..., dimensions={0} | all-to-all | bytes 524288 | tf_op jit(solution)/shard_map/basis/all_to_all | solution.py:153
  58.0 12.4 %all_to_all.58.parts_ref = f32[4,128,256]{2,1,0:T(8,128)S(1)} all-to-all(f32[4,128,256]{2,1,0:T(8,128)S(1)} %broadcast_in_dim.15), channel_id=1, replica_groups={{0,2,4,6},{1,3,5,7},{8,10,12,14},{9,11,13,15},{16,18,20,22},{17,19,21,2..., dimensions={0} | all-to-all | bytes 1048576 | tf_op jit(solution)/shard_map/basis/all_to_all | solution.py:153
  70.4 0.4 gram_part.1
  70.9 20.3 %all_to_all.59.parts_ref = f32[64,8,128]{2,1,0:T(8,128)S(1)} all-to-all(f32[64,8,128]{2,1,0:T(8,128)S(1)} %get-tuple-element.10), channel_id=1, replica_groups={{0,8,16,24,32,40,48,56,64,72,80,88,96,104,112,120,128,136,144,152,160,1..., dimensions={0} | all-to-all | bytes 524288 | tf_op jit(solution)/shard_map/gram/all_to_all | solution.py:153
  91.2 0.1 gram_copies.1
  91.3 16.4 %all_to_all.60.blocks_ref = f32[64,8,128]{2,1,0:T(8,128)S(1)} all-to-all(f32[64,8,128]{2,1,0:T(8,128)S(1)} %gram_copies.1), channel_id=1, replica_groups={{0,8,16,24,32,40,48,56,64,72,80,88,96,104,112,120,128,136,144,152,160,1..., dimensions={0} | all-to-all | bytes 524288 | tf_op jit(solution)/shard_map/gram/all_to_all | solution.py:153
  107.7 9.0 %ortho_basis.1.ortho_ref = bf16[128,256]{1,0:T(8,128)(2,1)S(1)} custom-call(f32[64,8,128]{2,1,0:T(8,128)S(1)} %all_to_all.60.blocks_ref, f32[128,256]{1,0:T(8,128)S(1)} %get-tuple-element.11.basis_ref), custom_call_target="tpu_custom_call" | custom-call | flops 1000000000 | bytes 786432 | tf_op jit(solution)/shard_map/solve/ortho_basis/pallas_call | solution.py:136
  116.7 0.6 convolution_convert_fusion
  117.3 17.2 %all_to_all.61 = bf16[4,64,3328]{2,1,0:T(8,128)(2,1)S(1)} all-to-all(bf16[4,64,3328]{2,1,0:T(8,128)(2,1)S(1)} %bitcast.14), channel_id=1, replica_groups={{0,8,64,72},{1,57,449,505},{2,10,66,74},{3,59,451,507},{4,12,68,76},{5,..., dimensions={0} | all-to-all | bytes 3407872 | tf_op jit(solution)/shard_map/projection/all_to_all | solution.py:153
  134.5 0.2 add_convert_fusion
  134.7 0.1 convert_element_type.103
  134.8 21.9 %all_to_all.62 = bf16[16,4,3328]{2,1,0:T(4,128)(2,1)S(1)} all-to-all(bf16[16,4,3328]{2,1,0:T(4,128)(2,1)S(1)} %convert_element_type.103), channel_id=1, replica_groups={{0,16,32,48,128,144,160,176,256,272,288,304,384,400,416,432},{1,17,33,4..., dimensions={0} | all-to-all | bytes 851968 | tf_op jit(solution)/shard_map/projection/all_to_all | solution.py:153
  156.7 0.1 fusion.1
  156.9 21.2 %all_to_all.63 = bf16[16,8,1664]{2,1,0:T(8,128)(2,1)S(1)} all-to-all(bf16[16,8,1664]{2,1,0:T(8,128)(2,1)S(1)} %broadcast_in_dim.16), channel_id=1, replica_groups={{0,16,32,48,128,144,160,176,256,272,288,304,384,400,416,432},{1,17,33,4..., dimensions={0} | all-to-all | bytes 851968 | tf_op jit(solution)/shard_map/projection/all_to_all | solution.py:153
  178.1 0.1 broadcast_in_dim.17
  178.2 17.2 %all_to_all.64 = bf16[4,16,8,1664]{3,2,1,0:T(8,128)(2,1)S(1)} all-to-all(bf16[4,16,8,1664]{3,2,1,0:T(8,128)(2,1)S(1)} %broadcast_in_dim.17), channel_id=1, replica_groups={{0,8,64,72},{1,57,449,505},{2,10,66,74},{3,59,451,507},{4,12,68,76},{5,..., dimensions={0} | all-to-all | bytes 3407872 | tf_op jit(solution)/shard_map/projection/all_to_all | solution.py:153
  195.4 1.7 squares.1
  197.1 4.5 %all-to-all-start.10 = ((f32[8,8,128]{2,1,0:T(8,128)}), f32[8,8,128]{2,1,0:T(8,128)S(1)}, u32[]{:S(2)}, u32[]{:S(2)}) async-start(f32[8,8,128]{2,1,0:T(8,128)} %squares.1), calls=%async_computation.10 | async-start | bytes 65536 | tf_op jit(solution)/shard_map/norms/all_to_all | solution.py:153
  201.6 1.9 momentum_next.1
  203.5 2.9 %all-to-all-done.10.squares_ref = f32[8,8,128]{2,1,0:T(8,128)S(1)} async-done(((f32[8,8,128]{2,1,0:T(8,128)}), f32[8,8,128]{2,1,0:T(8,128)S(1)}, u32[]{:S(2)}, u32[]{:S(2)}) %all-to-all-start.10) | async-done | bytes 32800 | tf_op jit(solution)/shard_map/norms/all_to_all | solution.py:153
  206.3 2.5 %update.1 = (bf16[128,3328]{1,0:T(8,128)(2,1)}, f32[4,3328]{1,0:T(4,128)}) custom-call(bf16[128,256]{1,0:T(8,128)(2,1)S(1)} %ortho_basis.1.ortho_ref, bf16[512,1664]{1,0:T(8,128)(2,1)S(1)} %bitcast.12, f32[8,8,128]{2,1,0:T(8,128)S(1)} %all-to-all-done.10.squares_ref, f32[4,3328]{1,0:T(4,128)S(1)} %get-tuple-element.16.own_ref), custom_call_target="tpu_custom_call" | custom-call | flops 872415232 | bytes 3710976 | tf_op jit(solution)/shard_map/outputs/update/pallas_call | solution.py:136
  (7 shorter events, 0.2 us)
Async XLA Ops:
  34.0 17.9 %copy-start = (bf16[128,3328]{1,0:T(8,128)(2,1)S(1)}, bf16[128,3328]{1,0:T(8,128)(2,1)}, u32[]{:S(2)}) copy-start(bf16[128,3328]{1,0:T(8,128)(2,1)} %momentum_ref.1) | copy-start | bytes 2555908
  34.0 17.9 %copy-start.1 = (bf16[128,3328]{1,0:T(8,128)(2,1)S(1)}, bf16[128,3328]{1,0:T(8,128)(2,1)}, u32[]{:S(2)}) copy-start(bf16[128,3328]{1,0:T(8,128)(2,1)} %gradient_ref.1) | copy-start | bytes 2555908
  197.1 9.2 %all-to-all-start.10 = ((f32[8,8,128]{2,1,0:T(8,128)}), f32[8,8,128]{2,1,0:T(8,128)S(1)}, u32[]{:S(2)}, u32[]{:S(2)}) async-start(f32[8,8,128]{2,1,0:T(8,128)} %squares.1), calls=%async_computation.10 | async-start | bytes 65536 | tf_op jit(solution)/shard_map/norms/all_to_all | solution.py:153

commit v5 on v4

--- a/solution.py
+++ b/solution.py
@@ -38,7 +38,6 @@
     lambda z, y, x, core: (z % 2, y % 2, x, core), lambda z, y, x, core: (z // 2, y // 2)
 )
 PLANE = groups_of(lambda z, y, x, core: (x, core), lambda z, y, x, core: (z, y))
-CHIP = groups_of(lambda z, y, x, core: (z, y, x), lambda z, y, x, core: core)
 ROW = groups_of(lambda z, y, x, core: (z, y, core), lambda z, y, x, core: x)
 COLUMNS = groups_of(lambda z, y, x, core: (z, y), lambda z, y, x, core: (x, core))
 
@@ -47,29 +46,33 @@
 
 
 def block_inverse(block, size):
-    lane = lax.broadcasted_iota(jnp.int32, (size, 128), 1)
     sub = lax.broadcasted_iota(jnp.int32, (size, 128), 0)
-    eye = (lane == sub + size).astype(jnp.float32)
-    if 2 * size == 128:
-        work = jnp.concatenate([block, jnp.zeros_like(block)], axis=1) + eye
-    else:
-        work = jnp.concatenate([block, jnp.zeros((size, 128 - size), jnp.float32)], axis=1) + eye
+    eye = (lax.broadcasted_iota(jnp.int32, (size, 128), 1) == sub + size).astype(jnp.float32)
+    work = jnp.concatenate([block, jnp.zeros((size, 128 - size), jnp.float32)], axis=1) + eye
     pivots = jnp.ones((size, 128), jnp.float32)
+
+    def row(array, index):
+        return jnp.broadcast_to(array[index : index + 1, :], (size, 128))
+
     for start in range(0, size, FACTOR_GROUP):
         columns = [
             jnp.broadcast_to(work[:, j : j + 1], (size, 128))
             for j in range(start, start + FACTOR_GROUP)
         ]
-        for c in range(FACTOR_GROUP):
+        for c in range(0, FACTOR_GROUP, 2):
             j = start + c
-            pivot = jnp.broadcast_to(columns[c][j : j + 1, :], (size, 128))
-            ratio = jnp.where(sub > j, columns[c] * (1.0 / pivot), 0.0)
-            pivots = jnp.where(sub == j, pivot, pivots)
-            work = work - ratio * jnp.broadcast_to(work[j : j + 1, :], (size, 128))
-            for later in range(c + 1, FACTOR_GROUP):
-                columns[later] = columns[later] - ratio * jnp.broadcast_to(
-                    columns[later][j : j + 1, :], (size, 128)
-                )
+            first, second = columns[c], columns[c + 1]
+            a, e, b = row(first, j), row(first, j + 1), row(second, j + 1)
+            det = a * b - e * e
+            inverse_det, inverse_a = 1.0 / det, 1.0 / a
+            ratio = jnp.where(sub > j + 1, (first * b - second * e) * inverse_det, 0.0)
+            ratio = jnp.where(sub == j + 1, e * inverse_a, ratio)
+            other = jnp.where(sub > j + 1, (second * a - first * e) * inverse_det, 0.0)
+            pivots = jnp.where(sub == j, a, jnp.where(sub == j + 1, det * inverse_a, pivots))
+            for later in range(c + 2, FACTOR_GROUP):
+                column = columns[later]
+                columns[later] = column - ratio * row(column, j) - other * row(column, j + 1)
+            work = work - ratio * row(work, j) - other * row(work, j + 1)
     work = work * lax.rsqrt(pivots)
     return work[:, size : 2 * size]
 
@@ -117,10 +120,14 @@
     for block in range(blocks_ref.shape[0]):
         row, col = 8 * (block // (size // 128)), 128 * (block % (size // 128))
         inverse_ref[row : row + 8, col : col + 128] = blocks_ref[block]
-    factor_in_place(inverse_ref)
     source = lax.broadcasted_iota(jnp.int32, (size, size), 0)
     target = lax.broadcasted_iota(jnp.int32, (size, size), 1)
-    inverse = jnp.where(source >= target, inverse_ref[...], 0.0)
+    diagonal = jnp.where(source == target, inverse_ref[...], 0.0)
+    scale_row = lax.rsqrt(jnp.sum(diagonal, axis=0, keepdims=True))
+    scale_column = lax.rsqrt(jnp.sum(diagonal, axis=1, keepdims=True))
+    inverse_ref[...] = inverse_ref[...] * scale_column * scale_row
+    factor_in_place(inverse_ref)
+    inverse = jnp.where(source >= target, inverse_ref[...] * scale_row, 0.0)
     ortho = nt_dot(basis_ref[...], inverse, HIGHEST).astype(jnp.bfloat16)
     selection = (device_of(target // share) * share + target % share == source).astype(jnp.bfloat16)
     ortho_ref[...] = jnp.dot(ortho, selection, preferred_element_type=jnp.float32).astype(
@@ -168,10 +175,6 @@
     return parts[0]
 
 
-def total(block, groups):
-    return add_up(spread(block, groups))
-
-
 def device_of(place):
     parity, tile_index = place // 16, place % 16
     z = tile_index // 4 * 2 + parity // 2
@@ -203,38 +206,33 @@
     return dot(high, selection) + (dot(middle, selection) + dot(low, selection))
 
 
-def basis_kernel(momentum_ref, gradient_ref, factor_ref, blended_ref, copies_ref, *, share):
+def basis_kernel(momentum_ref, gradient_ref, factor_ref, blended_ref, basis_ref, *, share):
     blended = (
         momentum_ref[...].astype(jnp.float32) + gradient_ref[...].astype(jnp.float32)
     ).astype(jnp.bfloat16)
     blended_ref[...] = blended
     height, half = factor_ref.shape
     rank = height // 2
-    place, part, low = split_row(lax.broadcasted_iota(jnp.int32, (height, rank), 0), share)
-    chosen = device_of(place) * share + low == lax.broadcasted_iota(jnp.int32, (height, rank), 1)
-    result = None
-    for h in range(2):
-        product = nt_dot(blended[:, h * half : (h + 1) * half], factor_ref[...])
-        selection = (chosen & (part == h)).astype(jnp.bfloat16)
-        picked = exact_dot(product, selection)
-        result = picked if result is None else result + picked
-    for copy in range(copies_ref.shape[0]):
-        copies_ref[copy] = result
-
-
-def half_columns(ortho, height, share, h):
-    rank = ortho.shape[1]
+    place, _, low = split_row(lax.broadcasted_iota(jnp.int32, (height, rank), 0), share)
+    target = lax.broadcasted_iota(jnp.int32, (height, rank), 1)
+    selection = (device_of(place) * share + low == target).astype(jnp.bfloat16)
+    _, part, _ = split_row(lax.broadcasted_iota(jnp.int32, (blended.shape[0], height), 1), share)
+    left = nt_dot(blended[:, :half], factor_ref[...])
+    right = nt_dot(blended[:, half:], factor_ref[...])
+    basis_ref[...] = exact_dot(jnp.where(part == 0, left, right), selection)
+
+
+def momentum_kernel(ortho_ref, projection_ref, blended_ref, out_ref, left_ref, *, share):
+    height, half = projection_ref.shape
+    rank = height // 2
     place, part, low = split_row(lax.broadcasted_iota(jnp.int32, (rank, height), 1), share)
     source = lax.broadcasted_iota(jnp.int32, (rank, height), 0)
-    selection = ((place * share + low == source) & (part == h)).astype(jnp.bfloat16)
-    return jnp.dot(ortho, selection, preferred_element_type=jnp.float32).astype(jnp.bfloat16)
-
-
-def momentum_kernel(ortho_ref, projection_ref, blended_ref, out_ref, *, share):
-    height, half = projection_ref.shape
     for h in range(2):
         columns = slice(h * half, (h + 1) * half)
-        left = half_columns(ortho_ref[...], height, share, h)
+        selection = ((place * share + low == source) & (part == h)).astype(jnp.bfloat16)
+        left = jnp.dot(ortho_ref[...], selection, preferred_element_type=jnp.float32)
+        left = left.astype(jnp.bfloat16)
+        left_ref[h] = left
         carried = jnp.dot(left, projection_ref[...], preferred_element_type=jnp.float32)
         out_ref[:, columns] = (
             blended_ref[:, columns].astype(jnp.float32) - (1.0 - MOMENTUM_DECAY) * carried
@@ -243,44 +241,33 @@
 
 def squares_kernel(projection_ref, copies_ref):
     height, half = projection_ref.shape
-    wide = projection_ref[...].astype(jnp.float32)
-    squares = wide * wide
-    high = squares.astype(jnp.bfloat16)
-    low = (squares - high.astype(jnp.float32)).astype(jnp.bfloat16)
-    ones = jnp.ones((8, half), jnp.bfloat16)
-    sums = nt_dot(ones, high) + nt_dot(ones, low)
+    sums = jnp.zeros((height, 128), jnp.float32)
+    for column in range(0, half, 128):
+        piece = projection_ref[:, column : column + 128].astype(jnp.float32)
+        sums = sums + piece * piece
+    totals = nt_dot(jnp.ones((8, 128), jnp.float32), sums, HIGHEST)
     copies_ref[...] = jnp.zeros(copies_ref.shape, jnp.float32)
     for copy in range(copies_ref.shape[0]):
         for piece in range(height // 128):
-            copies_ref[copy, piece : piece + 1, :] = sums[0:1, piece * 128 : (piece + 1) * 128]
-
-
-def update_kernel(
-    ortho_ref, projection_ref, squares_ref, own_ref, out_ref, factor_ref, *, share, scale
-):
+            copies_ref[copy, piece : piece + 1, :] = totals[0:1, piece * 128 : (piece + 1) * 128]
+
+
+def update_kernel(left_ref, projection_ref, squares_ref, own_ref, out_ref, factor_ref, *, share, scale):
     height, half = projection_ref.shape
-    rank = height // 2
     pieces = jnp.sum(squares_ref[...], axis=0)
     squares = jnp.concatenate([pieces[i : i + 1] for i in range(height // 128)], axis=1)
-    place, _, low = split_row(lax.broadcasted_iota(jnp.int32, (height, rank), 0), share)
-    target = lax.broadcasted_iota(jnp.int32, (height, rank), 1)
-    fold = (place * share + low == target).astype(jnp.float32)
-    squares = jnp.dot(
-        jnp.broadcast_to(squares, (8, height)),
-        fold,
-        precision=HIGHEST,
-        preferred_element_type=jnp.float32,
+    squares = jnp.broadcast_to(squares, (8, height))
+    place, part, low = split_row(lax.broadcasted_iota(jnp.int32, (8, height), 1), share)
+    other = jnp.where(
+        part == 0, pltpu.roll(squares, height - share, 1), pltpu.roll(squares, share, 1)
     )
-    inverse = 1.0 / (jnp.sqrt(squares) + EPSILON)
-    scaled = (ortho_ref[...].astype(jnp.float32) * inverse[0:1]).astype(jnp.bfloat16)
+    inverse = 1.0 / (jnp.sqrt(squares + other) + EPSILON)
     for h in range(2):
-        left = half_columns(scaled, height, share, h)
+        left = (left_ref[h].astype(jnp.float32) * inverse[0:1]).astype(jnp.bfloat16)
         direction = jnp.dot(left, projection_ref[...], preferred_element_type=jnp.float32)
         out_ref[:, h * half : (h + 1) * half] = (scale * direction).astype(jnp.bfloat16)
-    column = lax.broadcasted_iota(jnp.int32, (8, rank), 1)
-    natural = device_of(column // share) * share + column % share
-    first = lax.axis_index("fsdp") * share
-    mine = natural == first + lax.broadcasted_iota(jnp.int32, (8, rank), 0)
+    mine = (device_of(place) == lax.axis_index("fsdp")) & (part == 0)
+    mine = mine & (low == lax.broadcasted_iota(jnp.int32, (8, height), 0))
     own_inverse = jnp.sum(jnp.where(mine, inverse, 0.0), axis=1, keepdims=True)
     factor_ref[...] = own_ref[...] * own_inverse[0:share]
 
@@ -294,13 +281,14 @@
     with jax.named_scope("factor_gather"):
         whole_factor = spread_rows(halves(right_factor)).reshape(2 * rank, cols // 2)
     with jax.named_scope("basis"):
-        blended, copies = local_call(
+        blended, part = local_call(
             functools.partial(basis_kernel, share=share),
             "basis_part",
-            (shaped(rows, cols, dtype=jnp.bfloat16), shaped(CORES, rows, rank)),
+            (shaped(rows, cols, dtype=jnp.bfloat16), shaped(rows, rank)),
             momentum, gradient, whole_factor,
         )
-        parts = spread(add_up(exchange(copies, CHIP)), ROW)
+        other_core = [(i, i ^ 1) for i in range(columns)]
+        parts = spread(part + lax.ppermute(part, "tp", other_core), ROW)
     with jax.named_scope("gram"):
         basis, blocks = local_call(
             gram_kernel,
@@ -333,10 +321,10 @@
         copies = local_call(squares_kernel, "squares", shaped(columns, 8, 128), projection)
         squares = exchange(copies, COLUMNS)
     with jax.named_scope("outputs"):
-        momentum_next = local_call(
+        momentum_next, left = local_call(
             functools.partial(momentum_kernel, share=share),
             "momentum_next",
-            shaped(rows, cols, dtype=jnp.bfloat16),
+            (shaped(rows, cols, dtype=jnp.bfloat16), shaped(2, rows, 2 * rank, dtype=jnp.bfloat16)),
             ortho_basis, projection, blended,
             flops=8 * rows * cols * rank,
         )
@@ -345,7 +333,7 @@
             functools.partial(update_kernel, share=share, scale=scale),
             "update",
             (shaped(rows, cols, dtype=jnp.bfloat16), shaped(share, cols)),
-            ortho_basis, projection, squares, own,
+            left, projection, squares, own,
             flops=8 * rows * cols * rank,
         )
     return (momentum_next, factor_next, update)

time: 210 us -> 210 us (level)
    ppermute x0 -> x1, starting transfers between devices: none -> 2.34 us  [body(): parts = spread(part + lax.ppermute(part, 'tp', other_core), ROW)]
    all_to_all x10 -> x9, blocking collectives: 181 us -> 181 us  [exchange(): lax.all_to_all(blocks, AXES, 0, 0, axis_index_groups=groups, tiled=True)]
  transfers between devices with their start and end apart: 1 -> 2, of which waited for: 1 -> 2; matrix products, arithmetic and copies ran while one was open for 0% -> 0% of each run, Pallas kernels for 1% -> 1%
where the time goes in v5:
time: 210 us; the launch traced here: 209 us
  blocking collectives  181 us (86%)
  Pallas kernels  15.8 us (8%)
  starting transfers between devices  5.63 us (3%)
  waiting for transfers between devices  3.78 us (2%)
    all_to_all x9, blocking collectives, exchange(): lax.all_to_all(blocks, AXES, 0, 0, axis_index_groups=groups, tiled=True)  181 us
    pallas_call x7, Pallas kernels, local_call(): pl.pallas_call(kernel, out_shape=shapes, in_specs=[VMEM] * len(operands),...  15.8 us
  transfers between devices with their start and end apart: 2, of which 2 were waited for; matrix products, arithmetic and copies ran while one was open for 0% of the time, Pallas kernels for 1%

profile of v5, /device:TPU:1, one launch (start us, length us, event | category | flops | bytes accessed | tf_op | source)
XLA Modules:
  0.0 208.8 jit_solution(2421161609025901700)
XLA Ops:
  0.6 0.7 fusion.2
  1.4 32.5 %all_to_all.50 = bf16[16,8,1664]{2,1,0:T(8,128)(2,1)S(1)} all-to-all(bf16[16,8,1664]{2,1,0:T(8,128)(2,1)S(1)} %broadcast_in_dim.10), channel_id=1, replica_groups={{0,16,32,48,128,144,160,176,256,272,288,304,384,400,416,432},{1,17,33,4..., dimensions={0} | all-to-all | bytes 851968 | tf_op jit(solution)/shard_map/factor_gather/all_to_all | solution.py:160
  33.9 0.1 broadcast_in_dim.11
  34.0 0.0 copy-start
  34.0 0.0 copy-start.1
  34.1 17.9 %all_to_all.51 = bf16[4,16,8,1664]{3,2,1,0:T(8,128)(2,1)S(1)} all-to-all(bf16[4,16,8,1664]{3,2,1,0:T(8,128)(2,1)S(1)} %broadcast_in_dim.11), channel_id=1, replica_groups={{0,8,64,72},{1,57,449,505},{2,10,66,74},{3,59,451,507},{4,12,68,76},{5,..., dimensions={0} | all-to-all | bytes 3407872 | tf_op jit(solution)/shard_map/factor_gather/all_to_all | solution.py:160
  52.0 0.0 copy-done
  52.0 0.0 copy-done.1
  52.0 1.5 basis_part.1
  53.4 2.3 %collective-permute-start = (f32[128,256]{1,0:T(8,128)S(1)}, f32[128,256]{1,0:T(8,128)S(1)}, u32[]{:S(2)}, u32[]{:S(2)}) collective-permute-start(f32[128,256]{1,0:T(8,128)S(1)} %get-tuple-element.11), channel_id=1, source_target_pairs={{0,1},{1,0},{2,3},{3,2},{4,5},{5,4},{6,7},{7,6},{8,9},{9,8},{10,11... | collective-permute-start | bytes 393224 | tf_op jit(solution)/shard_map/basis/ppermute | solution.py:291
  55.8 1.0 collective-permute-done
  56.8 12.4 %all_to_all.52.parts_ref = f32[4,128,256]{2,1,0:T(8,128)S(1)} all-to-all(f32[4,128,256]{2,1,0:T(8,128)S(1)} %broadcast_in_dim.12), channel_id=1, replica_groups={{0,2,4,6},{1,3,5,7},{8,10,12,14},{9,11,13,15},{16,18,20,22},{17,19,21,2..., dimensions={0} | all-to-all | bytes 1048576 | tf_op jit(solution)/shard_map/basis/all_to_all | solution.py:160
  69.3 0.4 gram_part.1
  69.7 21.1 %all_to_all.53.parts_ref = f32[64,8,128]{2,1,0:T(8,128)S(1)} all-to-all(f32[64,8,128]{2,1,0:T(8,128)S(1)} %get-tuple-element.12), channel_id=1, replica_groups={{0,8,16,24,32,40,48,56,64,72,80,88,96,104,112,120,128,136,144,152,160,1..., dimensions={0} | all-to-all | bytes 524288 | tf_op jit(solution)/shard_map/gram/all_to_all | solution.py:160
  90.8 0.1 gram_copies.1
  90.9 18.0 %all_to_all.54.blocks_ref = f32[64,8,128]{2,1,0:T(8,128)S(1)} all-to-all(f32[64,8,128]{2,1,0:T(8,128)S(1)} %gram_copies.1), channel_id=1, replica_groups={{0,8,16,24,32,40,48,56,64,72,80,88,96,104,112,120,128,136,144,152,160,1..., dimensions={0} | all-to-all | bytes 524288 | tf_op jit(solution)/shard_map/gram/all_to_all | solution.py:160
  108.9 9.0 %ortho_basis.1.ortho_ref = bf16[128,256]{1,0:T(8,128)(2,1)S(1)} custom-call(f32[64,8,128]{2,1,0:T(8,128)S(1)} %all_to_all.54.blocks_ref, f32[128,256]{1,0:T(8,128)S(1)} %get-tuple-element.13.basis_ref), custom_call_target="tpu_custom_call" | custom-call | flops 1000000000 | bytes 786432 | tf_op jit(solution)/shard_map/solve/ortho_basis/pallas_call | solution.py:143
  118.0 0.6 convolution_convert_fusion
  118.6 17.2 %all_to_all.55 = bf16[4,64,3328]{2,1,0:T(8,128)(2,1)S(1)} all-to-all(bf16[4,64,3328]{2,1,0:T(8,128)(2,1)S(1)} %bitcast.12), channel_id=1, replica_groups={{0,8,64,72},{1,57,449,505},{2,10,66,74},{3,59,451,507},{4,12,68,76},{5,..., dimensions={0} | all-to-all | bytes 3407872 | tf_op jit(solution)/shard_map/projection/all_to_all | solution.py:160
  135.8 0.2 add_convert_fusion
  136.0 0.1 convert_element_type.103
  136.1 23.6 %all_to_all.56 = bf16[16,4,3328]{2,1,0:T(4,128)(2,1)S(1)} all-to-all(bf16[16,4,3328]{2,1,0:T(4,128)(2,1)S(1)} %convert_element_type.103), channel_id=1, replica_groups={{0,16,32,48,128,144,160,176,256,272,288,304,384,400,416,432},{1,17,33,4..., dimensions={0} | all-to-all | bytes 851968 | tf_op jit(solution)/shard_map/projection/all_to_all | solution.py:160
  159.7 0.1 fusion
  159.9 20.7 %all_to_all.57 = bf16[16,8,1664]{2,1,0:T(8,128)(2,1)S(1)} all-to-all(bf16[16,8,1664]{2,1,0:T(8,128)(2,1)S(1)} %broadcast_in_dim.13), channel_id=1, replica_groups={{0,16,32,48,128,144,160,176,256,272,288,304,384,400,416,432},{1,17,33,4..., dimensions={0} | all-to-all | bytes 851968 | tf_op jit(solution)/shard_map/projection/all_to_all | solution.py:160
  180.6 0.1 broadcast_in_dim.14
  180.8 17.2 %all_to_all.58 = bf16[4,16,8,1664]{3,2,1,0:T(8,128)(2,1)S(1)} all-to-all(bf16[4,16,8,1664]{3,2,1,0:T(8,128)(2,1)S(1)} %broadcast_in_dim.14), channel_id=1, replica_groups={{0,8,64,72},{1,57,449,505},{2,10,66,74},{3,59,451,507},{4,12,68,76},{5,..., dimensions={0} | all-to-all | bytes 3407872 | tf_op jit(solution)/shard_map/projection/all_to_all | solution.py:160
  197.9 1.2 squares.1
  199.2 3.3 %all-to-all-start.9 = ((f32[8,8,128]{2,1,0:T(8,128)}), f32[8,8,128]{2,1,0:T(8,128)S(1)}, u32[]{:S(2)}, u32[]{:S(2)}) async-start(f32[8,8,128]{2,1,0:T(8,128)} %squares.1), calls=%async_computation.9 | async-start | bytes 65536 | tf_op jit(solution)/shard_map/norms/all_to_all | solution.py:160
  202.5 1.9 momentum_next.1
  204.4 2.8 %all-to-all-done.9.squares_ref = f32[8,8,128]{2,1,0:T(8,128)S(1)} async-done(((f32[8,8,128]{2,1,0:T(8,128)}), f32[8,8,128]{2,1,0:T(8,128)S(1)}, u32[]{:S(2)}, u32[]{:S(2)}) %all-to-all-start.9) | async-done | bytes 32800 | tf_op jit(solution)/shard_map/norms/all_to_all | solution.py:160
  207.2 1.6 update.1
  (7 shorter events, 0.2 us)
Async XLA Ops:
  34.0 17.9 %copy-start = (bf16[128,3328]{1,0:T(8,128)(2,1)S(1)}, bf16[128,3328]{1,0:T(8,128)(2,1)}, u32[]{:S(2)}) copy-start(bf16[128,3328]{1,0:T(8,128)(2,1)} %momentum_ref.1) | copy-start | bytes 2555908
  34.0 17.9 %copy-start.1 = (bf16[128,3328]{1,0:T(8,128)(2,1)S(1)}, bf16[128,3328]{1,0:T(8,128)(2,1)}, u32[]{:S(2)}) copy-start(bf16[128,3328]{1,0:T(8,128)(2,1)} %gradient_ref.1) | copy-start | bytes 2555908
  53.4 3.3 %collective-permute-start = (f32[128,256]{1,0:T(8,128)S(1)}, f32[128,256]{1,0:T(8,128)S(1)}, u32[]{:S(2)}, u32[]{:S(2)}) collective-permute-start(f32[128,256]{1,0:T(8,128)S(1)} %get-tuple-element.11), channel_id=1, source_target_pairs={{0,1},{1,0},{2,3},{3,2},{4,5},{5,4},{6,7},{7,6},{8,9},{9,8},{10,11... | collective-permute-start | bytes 393224 | tf_op jit(solution)/shard_map/basis/ppermute | solution.py:291
  199.2 8.0 %all-to-all-start.9 = ((f32[8,8,128]{2,1,0:T(8,128)}), f32[8,8,128]{2,1,0:T(8,128)S(1)}, u32[]{:S(2)}, u32[]{:S(2)}) async-start(f32[8,8,128]{2,1,0:T(8,128)} %squares.1), calls=%async_computation.9 | async-start | bytes 65536 | tf_op jit(solution)/shard_map/norms/all_to_all | solution.py:160

commit v6 on v5

--- a/solution.py
+++ b/solution.py
@@ -49,19 +49,21 @@
     sub = lax.broadcasted_iota(jnp.int32, (size, 128), 0)
     eye = (lax.broadcasted_iota(jnp.int32, (size, 128), 1) == sub + size).astype(jnp.float32)
     work = jnp.concatenate([block, jnp.zeros((size, 128 - size), jnp.float32)], axis=1) + eye
-    pivots = jnp.ones((size, 128), jnp.float32)
-
-    def row(array, index):
-        return jnp.broadcast_to(array[index : index + 1, :], (size, 128))
-
+    done = []
     for start in range(0, size, FACTOR_GROUP):
+        height = size - start
+        sub = lax.broadcasted_iota(jnp.int32, (height, 128), 0)
+
+        def row(array, index):
+            return jnp.broadcast_to(array[index : index + 1, :], (height, 128))
+
+        pivots = jnp.ones((height, 128), jnp.float32)
         columns = [
-            jnp.broadcast_to(work[:, j : j + 1], (size, 128))
-            for j in range(start, start + FACTOR_GROUP)
+            jnp.broadcast_to(work[:, start + j : start + j + 1], (height, 128))
+            for j in range(FACTOR_GROUP)
         ]
-        for c in range(0, FACTOR_GROUP, 2):
-            j = start + c
-            first, second = columns[c], columns[c + 1]
+        for j in range(0, FACTOR_GROUP, 2):
+            first, second = columns[j], columns[j + 1]
             a, e, b = row(first, j), row(first, j + 1), row(second, j + 1)
             det = a * b - e * e
             inverse_det, inverse_a = 1.0 / det, 1.0 / a
@@ -69,36 +71,34 @@
             ratio = jnp.where(sub == j + 1, e * inverse_a, ratio)
             other = jnp.where(sub > j + 1, (second * a - first * e) * inverse_det, 0.0)
             pivots = jnp.where(sub == j, a, jnp.where(sub == j + 1, det * inverse_a, pivots))
-            for later in range(c + 2, FACTOR_GROUP):
+            for later in range(j + 2, FACTOR_GROUP):
                 column = columns[later]
                 columns[later] = column - ratio * row(column, j) - other * row(column, j + 1)
             work = work - ratio * row(work, j) - other * row(work, j + 1)
-    work = work * lax.rsqrt(pivots)
-    return work[:, size : 2 * size]
-
-
-def factor_in_place(inverse_ref):
-    size = inverse_ref.shape[0]
+        done.append(work[:FACTOR_GROUP] * lax.rsqrt(pivots[:FACTOR_GROUP]))
+        work = work[FACTOR_GROUP:]
+    return jnp.concatenate(done, axis=0)[:, size : 2 * size]
+
+
+def inverse_factor(rows):
     step = FACTOR_BLOCK
-    for k in range(0, size, step):
-        after = k + step
-        inverse = block_inverse(inverse_ref[k:after, k:after], step)
-        panel = jnp.dot(
-            inverse, inverse_ref[k:after, :], precision=HIGHEST, preferred_element_type=jnp.float32
-        )
-        pieces = [inverse]
-        if k > 0:
-            pieces = [panel[:, :k]] + pieces
-        if after < size:
-            pieces = pieces + [panel[:, after:]]
-            lower = nt_dot(inverse_ref[after:, k:after], inverse, HIGHEST)
-        panel = jnp.concatenate(pieces, axis=1)
-        inverse_ref[k:after, :] = panel
-        if after < size:
-            inverse_ref[after:, k:after] = jnp.zeros((size - after, step), jnp.float32)
-            inverse_ref[after:, :] = inverse_ref[after:, :] - jnp.dot(
-                lower, panel, precision=HIGHEST, preferred_element_type=jnp.float32
+    rows = list(rows)
+    count = len(rows)
+
+    def with_column(row, k, block):
+        pieces = [row[:, q * step : (q + 1) * step] for q in range(count)]
+        return jnp.concatenate(pieces[:k] + [block] + pieces[k + 1 :], axis=1)
+
+    for k in range(count):
+        inverse = block_inverse(rows[k][:, k * step : (k + 1) * step], step)
+        panel = jnp.dot(inverse, rows[k], precision=HIGHEST, preferred_element_type=jnp.float32)
+        rows[k] = with_column(panel, k, inverse)
+        for i in range(k + 1, count):
+            lower = nt_dot(rows[i][:, k * step : (k + 1) * step], inverse, HIGHEST)
+            rows[i] = with_column(rows[i], k, jnp.zeros((step, step), jnp.float32)) - jnp.dot(
+                lower, rows[k], precision=HIGHEST, preferred_element_type=jnp.float32
             )
+    return jnp.concatenate(rows, axis=0)
 
 
 def gram_kernel(parts_ref, basis_ref, blocks_ref):
@@ -115,19 +115,26 @@
     copies_ref[...] = jnp.broadcast_to(jnp.sum(parts_ref[...], axis=0)[None], copies_ref.shape)
 
 
-def solve_kernel(blocks_ref, basis_ref, ortho_ref, inverse_ref, *, share):
-    size = inverse_ref.shape[0]
-    for block in range(blocks_ref.shape[0]):
-        row, col = 8 * (block // (size // 128)), 128 * (block % (size // 128))
-        inverse_ref[row : row + 8, col : col + 128] = blocks_ref[block]
+def solve_kernel(blocks_ref, basis_ref, ortho_ref, *, share):
+    size = basis_ref.shape[1]
+    wide = size // 128
+    gram = jnp.concatenate(
+        [
+            jnp.concatenate([blocks_ref[row * wide + part] for part in range(wide)], axis=1)
+            for row in range(size // 8)
+        ],
+        axis=0,
+    )
     source = lax.broadcasted_iota(jnp.int32, (size, size), 0)
     target = lax.broadcasted_iota(jnp.int32, (size, size), 1)
-    diagonal = jnp.where(source == target, inverse_ref[...], 0.0)
+    diagonal = jnp.where(source == target, gram, 0.0)
     scale_row = lax.rsqrt(jnp.sum(diagonal, axis=0, keepdims=True))
     scale_column = lax.rsqrt(jnp.sum(diagonal, axis=1, keepdims=True))
-    inverse_ref[...] = inverse_ref[...] * scale_column * scale_row
-    factor_in_place(inverse_ref)
-    inverse = jnp.where(source >= target, inverse_ref[...] * scale_row, 0.0)
+    gram = gram * scale_column * scale_row
+    inverse = inverse_factor(
+        [gram[k : k + FACTOR_BLOCK] for k in range(0, size, FACTOR_BLOCK)]
+    )
+    inverse = jnp.where(source >= target, inverse * scale_row, 0.0)
     ortho = nt_dot(basis_ref[...], inverse, HIGHEST).astype(jnp.bfloat16)
     selection = (device_of(target // share) * share + target % share == source).astype(jnp.bfloat16)
     ortho_ref[...] = jnp.dot(ortho, selection, preferred_element_type=jnp.float32).astype(
@@ -206,36 +213,43 @@
     return dot(high, selection) + (dot(middle, selection) + dot(low, selection))
 
 
-def basis_kernel(momentum_ref, gradient_ref, factor_ref, blended_ref, basis_ref, *, share):
-    blended = (
+def blend_kernel(momentum_ref, gradient_ref, blended_ref):
+    blended_ref[...] = (
         momentum_ref[...].astype(jnp.float32) + gradient_ref[...].astype(jnp.float32)
     ).astype(jnp.bfloat16)
-    blended_ref[...] = blended
+
+
+def basis_kernel(blended_ref, factor_ref, basis_ref, *, share):
+    rows = blended_ref.shape[0]
     height, half = factor_ref.shape
     rank = height // 2
     place, _, low = split_row(lax.broadcasted_iota(jnp.int32, (height, rank), 0), share)
     target = lax.broadcasted_iota(jnp.int32, (height, rank), 1)
     selection = (device_of(place) * share + low == target).astype(jnp.bfloat16)
-    _, part, _ = split_row(lax.broadcasted_iota(jnp.int32, (blended.shape[0], height), 1), share)
-    left = nt_dot(blended[:, :half], factor_ref[...])
-    right = nt_dot(blended[:, half:], factor_ref[...])
-    basis_ref[...] = exact_dot(jnp.where(part == 0, left, right), selection)
+    _, part, _ = split_row(lax.broadcasted_iota(jnp.int32, (rows, height), 1), share)
+    stacked = jnp.concatenate([blended_ref[:, :half], blended_ref[:, half:]], axis=0)
+    products = nt_dot(stacked, factor_ref[...])
+    basis_ref[...] = exact_dot(jnp.where(part == 0, products[:rows], products[rows:]), selection)
 
 
 def momentum_kernel(ortho_ref, projection_ref, blended_ref, out_ref, left_ref, *, share):
+    rows = ortho_ref.shape[0]
     height, half = projection_ref.shape
     rank = height // 2
     place, part, low = split_row(lax.broadcasted_iota(jnp.int32, (rank, height), 1), share)
     source = lax.broadcasted_iota(jnp.int32, (rank, height), 0)
+    selection = (place * share + low == source).astype(jnp.bfloat16)
+    left = jnp.dot(ortho_ref[...], selection, preferred_element_type=jnp.float32)
+    part = part[0:1]
+    left = jnp.concatenate([jnp.where(part == h, left, 0.0) for h in range(2)], axis=0)
+    left = left.astype(jnp.bfloat16)
+    left_ref[...] = left
+    carried = jnp.dot(left, projection_ref[...], preferred_element_type=jnp.float32)
     for h in range(2):
         columns = slice(h * half, (h + 1) * half)
-        selection = ((place * share + low == source) & (part == h)).astype(jnp.bfloat16)
-        left = jnp.dot(ortho_ref[...], selection, preferred_element_type=jnp.float32)
-        left = left.astype(jnp.bfloat16)
-        left_ref[h] = left
-        carried = jnp.dot(left, projection_ref[...], preferred_element_type=jnp.float32)
         out_ref[:, columns] = (
-            blended_ref[:, columns].astype(jnp.float32) - (1.0 - MOMENTUM_DECAY) * carried
+            blended_ref[:, columns].astype(jnp.float32)
+            - (1.0 - MOMENTUM_DECAY) * carried[h * rows : (h + 1) * rows]
         ).astype(jnp.bfloat16)
 
 
@@ -262,10 +276,13 @@
         part == 0, pltpu.roll(squares, height - share, 1), pltpu.roll(squares, share, 1)
     )
     inverse = 1.0 / (jnp.sqrt(squares + other) + EPSILON)
+    left = (left_ref[...].astype(jnp.float32) * inverse[0:1]).astype(jnp.bfloat16)
+    direction = jnp.dot(left, projection_ref[...], preferred_element_type=jnp.float32)
+    rows = out_ref.shape[0]
     for h in range(2):
-        left = (left_ref[h].astype(jnp.float32) * inverse[0:1]).astype(jnp.bfloat16)
-        direction = jnp.dot(left, projection_ref[...], preferred_element_type=jnp.float32)
-        out_ref[:, h * half : (h + 1) * half] = (scale * direction).astype(jnp.bfloat16)
+        out_ref[:, h * half : (h + 1) * half] = (
+            scale * direction[h * rows : (h + 1) * rows]
+        ).astype(jnp.bfloat16)
     mine = (device_of(place) == lax.axis_index("fsdp")) & (part == 0)
     mine = mine & (low == lax.broadcasted_iota(jnp.int32, (8, height), 0))
     own_inverse = jnp.sum(jnp.where(mine, inverse, 0.0), axis=1, keepdims=True)
@@ -279,13 +296,18 @@
     tiles = groups // 4
     rank = share * groups
     with jax.named_scope("factor_gather"):
-        whole_factor = spread_rows(halves(right_factor)).reshape(2 * rank, cols // 2)
+        blended = local_call(
+            blend_kernel, "blended", shaped(rows, cols, dtype=jnp.bfloat16), momentum, gradient
+        )
+        strided = spread(halves(right_factor), STRIDED)
+        strided, blended = lax.optimization_barrier((strided, blended))
+        whole_factor = spread(strided, NEAR).reshape(2 * rank, cols // 2)
     with jax.named_scope("basis"):
-        blended, part = local_call(
+        part = local_call(
             functools.partial(basis_kernel, share=share),
             "basis_part",
-            (shaped(rows, cols, dtype=jnp.bfloat16), shaped(rows, rank)),
-            momentum, gradient, whole_factor,
+            shaped(rows, rank),
+            blended, whole_factor,
         )
         other_core = [(i, i ^ 1) for i in range(columns)]
         parts = spread(part + lax.ppermute(part, "tp", other_core), ROW)
@@ -305,7 +327,6 @@
             "ortho_basis",
             shaped(rows, rank, dtype=jnp.bfloat16),
             blocks, basis,
-            scratch=[pltpu.VMEM((rank, rank), jnp.float32)],
             flops=10**9,
         )
     with jax.named_scope("projection"):
@@ -324,7 +345,7 @@
         momentum_next, left = local_call(
             functools.partial(momentum_kernel, share=share),
             "momentum_next",
-            (shaped(rows, cols, dtype=jnp.bfloat16), shaped(2, rows, 2 * rank, dtype=jnp.bfloat16)),
+            (shaped(rows, cols, dtype=jnp.bfloat16), shaped(2 * rows, 2 * rank, dtype=jnp.bfloat16)),
             ortho_basis, projection, blended,
             flops=8 * rows * cols * rank,
         )

time: 210 us -> 210 us (level)
  blocking collectives: 181 us -> 148 us
  starting transfers between devices: 5.63 us -> 22.1 us
  waiting for transfers between devices: 3.78 us -> 19.1 us
    all_to_all x9 -> x8, blocking collectives: 181 us -> 148 us  [exchange(): lax.all_to_all(blocks, AXES, 0, 0, axis_index_groups=groups, tiled=True)]
    all_to_all x1 -> x2, starting transfers between devices: 3.29 us -> 19.8 us  [exchange(): lax.all_to_all(blocks, AXES, 0, 0, axis_index_groups=groups, tiled=True)]
    all_to_all x1 -> x2, waiting for transfers between devices: 2.81 us -> 18.1 us  [exchange(): lax.all_to_all(blocks, AXES, 0, 0, axis_index_groups=groups, tiled=True)]
    pallas_call x7 -> x8, Pallas kernels: 15.8 us -> 14.8 us  [local_call(): pl.pallas_call(kernel, out_shape=shapes, in_specs=[VMEM] * len(operands),...]
  transfers between devices with their start and end apart: 2 -> 3, of which waited for: 2 -> 3; matrix products, arithmetic and copies ran while one was open for 0% -> 0% of each run, Pallas kernels for 1% -> 1%
where the time goes in v6:
time: 210 us; the launch traced here: 209 us
  blocking collectives  148 us (70%)
  starting transfers between devices  22.1 us (11%)
  waiting for transfers between devices  19.1 us (9%)
  Pallas kernels  14.8 us (7%)
  local copies, waits for them, and re-layouts  3.18 us (2%)
    all_to_all x8, blocking collectives, exchange(): lax.all_to_all(blocks, AXES, 0, 0, axis_index_groups=groups, tiled=True)  148 us
    all_to_all x2, starting transfers between devices, exchange(): lax.all_to_all(blocks, AXES, 0, 0, axis_index_groups=groups, tiled=True)  19.8 us
    all_to_all x2, waiting for transfers between devices, exchange(): lax.all_to_all(blocks, AXES, 0, 0, axis_index_groups=groups, tiled=True)  18.1 us
    pallas_call x8, Pallas kernels, local_call(): pl.pallas_call(kernel, out_shape=shapes, in_specs=[VMEM] * len(operands),...  14.8 us
  transfers between devices with their start and end apart: 3, of which 3 were waited for; matrix products, arithmetic and copies ran while one was open for 0% of the time, Pallas kernels for 1%

profile of v6, /device:TPU:1, one launch (start us, length us, event | category | flops | bytes accessed | tf_op | source)
XLA Modules:
  0.0 209.1 jit_solution(11334437792888634553)
XLA Ops:
  0.6 0.0 copy-start
  0.6 0.8 fusion.2
  1.5 0.8 broadcast_in_dim.10
  2.3 16.2 %all-to-all-start = ((bf16[16,8,1664]{2,1,0:T(8,128)(2,1)}), bf16[16,8,1664]{2,1,0:T(8,128)(2,1)S(1)}, u32[]{:S(2)}, u32[]{:S(2)}) async-start(bf16[16,8,1664]{2,1,0:T(8,128)(2,1)} %broadcast_in_dim.10), calls=%async_computation | async-start | bytes 851968 | tf_op jit(solution)/shard_map/factor_gather/all_to_all | solution.py:167
  18.5 0.0 copy-done
  18.5 0.0 copy-start.1
  18.5 1.1 copy-done.1
  19.7 0.2 blended.1.blended_ref
  19.9 15.1 %all-to-all-done = bf16[16,8,1664]{2,1,0:T(8,128)(2,1)S(1)} async-done(((bf16[16,8,1664]{2,1,0:T(8,128)(2,1)}), bf16[16,8,1664]{2,1,0:T(8,128)(2,1)S(1)}, u32[]{:S(2)}, u32[]{:S(2)}) %all-to-all-start) | async-done | bytes 426016 | tf_op jit(solution)/shard_map/factor_gather/all_to_all | solution.py:167
  35.0 0.1 broadcast_in_dim.11
  35.1 17.8 %all_to_all.50 = bf16[4,16,8,1664]{3,2,1,0:T(8,128)(2,1)S(1)} all-to-all(bf16[4,16,8,1664]{3,2,1,0:T(8,128)(2,1)S(1)} %broadcast_in_dim.11), channel_id=1, replica_groups={{0,8,64,72},{1,57,449,505},{2,10,66,74},{3,59,451,507},{4,12,68,76},{5,..., dimensions={0} | all-to-all | bytes 3407872 | tf_op jit(solution)/shard_map/factor_gather/all_to_all | solution.py:167
  52.8 1.1 basis_part.1
  54.0 2.3 %collective-permute-start = (f32[128,256]{1,0:T(8,128)S(1)}, f32[128,256]{1,0:T(8,128)S(1)}, u32[]{:S(2)}, u32[]{:S(2)}) collective-permute-start(f32[128,256]{1,0:T(8,128)S(1)} %basis_part.1), channel_id=1, source_target_pairs={{0,1},{1,0},{2,3},{3,2},{4,5},{5,4},{6,7},{7,6},{8,9},{9,8},{10,11... | collective-permute-start | bytes 393224 | tf_op jit(solution)/shard_map/basis/ppermute | solution.py:313
  56.3 1.0 collective-permute-done
  57.3 12.4 %all_to_all.51.parts_ref = f32[4,128,256]{2,1,0:T(8,128)S(1)} all-to-all(f32[4,128,256]{2,1,0:T(8,128)S(1)} %broadcast_in_dim.12), channel_id=1, replica_groups={{0,2,4,6},{1,3,5,7},{8,10,12,14},{9,11,13,15},{16,18,20,22},{17,19,21,2..., dimensions={0} | all-to-all | bytes 1048576 | tf_op jit(solution)/shard_map/basis/all_to_all | solution.py:167
  69.8 0.4 gram_part.1
  70.2 21.1 %all_to_all.52.parts_ref = f32[64,8,128]{2,1,0:T(8,128)S(1)} all-to-all(f32[64,8,128]{2,1,0:T(8,128)S(1)} %get-tuple-element.13), channel_id=1, replica_groups={{0,8,16,24,32,40,48,56,64,72,80,88,96,104,112,120,128,136,144,152,160,1..., dimensions={0} | all-to-all | bytes 524288 | tf_op jit(solution)/shard_map/gram/all_to_all | solution.py:167
  91.4 0.1 gram_copies.1
  91.4 18.0 %all_to_all.53.blocks_ref = f32[64,8,128]{2,1,0:T(8,128)S(1)} all-to-all(f32[64,8,128]{2,1,0:T(8,128)S(1)} %gram_copies.1), channel_id=1, replica_groups={{0,8,16,24,32,40,48,56,64,72,80,88,96,104,112,120,128,136,144,152,160,1..., dimensions={0} | all-to-all | bytes 524288 | tf_op jit(solution)/shard_map/gram/all_to_all | solution.py:167
  109.5 8.4 %ortho_basis.1.ortho_ref = bf16[128,256]{1,0:T(8,128)(2,1)S(1)} custom-call(f32[64,8,128]{2,1,0:T(8,128)S(1)} %all_to_all.53.blocks_ref, f32[128,256]{1,0:T(8,128)S(1)} %get-tuple-element.14.basis_ref), custom_call_target="tpu_custom_call" | custom-call | flops 1000000000 | bytes 786432 | tf_op jit(solution)/shard_map/solve/ortho_basis/pallas_call | solution.py:150
  117.9 0.6 convolution_convert_fusion
  118.5 17.2 %all_to_all.54 = bf16[4,64,3328]{2,1,0:T(8,128)(2,1)S(1)} all-to-all(bf16[4,64,3328]{2,1,0:T(8,128)(2,1)S(1)} %bitcast.12), channel_id=1, replica_groups={{0,8,64,72},{1,57,449,505},{2,10,66,74},{3,59,451,507},{4,12,68,76},{5,..., dimensions={0} | all-to-all | bytes 3407872 | tf_op jit(solution)/shard_map/projection/all_to_all | solution.py:167
  135.7 0.2 add_convert_fusion
  135.9 0.1 convert_element_type.103
  136.0 23.6 %all_to_all.55 = bf16[16,4,3328]{2,1,0:T(4,128)(2,1)S(1)} all-to-all(bf16[16,4,3328]{2,1,0:T(4,128)(2,1)S(1)} %convert_element_type.103), channel_id=1, replica_groups={{0,16,32,48,128,144,160,176,256,272,288,304,384,400,416,432},{1,17,33,4..., dimensions={0} | all-to-all | bytes 851968 | tf_op jit(solution)/shard_map/projection/all_to_all | solution.py:167
  159.6 0.1 fusion
  159.8 20.8 %all_to_all.56 = bf16[16,8,1664]{2,1,0:T(8,128)(2,1)S(1)} all-to-all(bf16[16,8,1664]{2,1,0:T(8,128)(2,1)S(1)} %broadcast_in_dim.13), channel_id=1, replica_groups={{0,16,32,48,128,144,160,176,256,272,288,304,384,400,416,432},{1,17,33,4..., dimensions={0} | all-to-all | bytes 851968 | tf_op jit(solution)/shard_map/projection/all_to_all | solution.py:167
  180.6 0.1 broadcast_in_dim.14
  180.7 17.2 %all_to_all.57 = bf16[4,16,8,1664]{3,2,1,0:T(8,128)(2,1)S(1)} all-to-all(bf16[4,16,8,1664]{3,2,1,0:T(8,128)(2,1)S(1)} %broadcast_in_dim.14), channel_id=1, replica_groups={{0,8,64,72},{1,57,449,505},{2,10,66,74},{3,59,451,507},{4,12,68,76},{5,..., dimensions={0} | all-to-all | bytes 3407872 | tf_op jit(solution)/shard_map/projection/all_to_all | solution.py:167
  197.9 1.2 squares.1
  199.2 3.6 %all-to-all-start.9 = ((f32[8,8,128]{2,1,0:T(8,128)}), f32[8,8,128]{2,1,0:T(8,128)S(1)}, u32[]{:S(2)}, u32[]{:S(2)}) async-start(f32[8,8,128]{2,1,0:T(8,128)} %squares.1), calls=%async_computation.9 | async-start | bytes 65536 | tf_op jit(solution)/shard_map/norms/all_to_all | solution.py:167
  202.7 1.7 momentum_next.1
  204.4 3.1 %all-to-all-done.9.squares_ref = f32[8,8,128]{2,1,0:T(8,128)S(1)} async-done(((f32[8,8,128]{2,1,0:T(8,128)}), f32[8,8,128]{2,1,0:T(8,128)S(1)}, u32[]{:S(2)}, u32[]{:S(2)}) %all-to-all-start.9) | async-done | bytes 32800 | tf_op jit(solution)/shard_map/norms/all_to_all | solution.py:167
  207.5 1.6 update.1
  (6 shorter events, 0.1 us)
Async XLA Ops:
  0.6 17.9 %copy-start = (bf16[128,3328]{1,0:T(8,128)(2,1)S(1)}, bf16[128,3328]{1,0:T(8,128)(2,1)}, u32[]{:S(2)}) copy-start(bf16[128,3328]{1,0:T(8,128)(2,1)} %momentum_ref.1) | copy-start | bytes 2555908
  2.3 32.7 %all-to-all-start = ((bf16[16,8,1664]{2,1,0:T(8,128)(2,1)}), bf16[16,8,1664]{2,1,0:T(8,128)(2,1)S(1)}, u32[]{:S(2)}, u32[]{:S(2)}) async-start(bf16[16,8,1664]{2,1,0:T(8,128)(2,1)} %broadcast_in_dim.10), calls=%async_computation | async-start | bytes 851968 | tf_op jit(solution)/shard_map/factor_gather/all_to_all | solution.py:167
  18.5 1.2 copy-start.1
  54.0 3.3 %collective-permute-start = (f32[128,256]{1,0:T(8,128)S(1)}, f32[128,256]{1,0:T(8,128)S(1)}, u32[]{:S(2)}, u32[]{:S(2)}) collective-permute-start(f32[128,256]{1,0:T(8,128)S(1)} %basis_part.1), channel_id=1, source_target_pairs={{0,1},{1,0},{2,3},{3,2},{4,5},{5,4},{6,7},{7,6},{8,9},{9,8},{10,11... | collective-permute-start | bytes 393224 | tf_op jit(solution)/shard_map/basis/ppermute | solution.py:313
  199.2 8.3 %all-to-all-start.9 = ((f32[8,8,128]{2,1,0:T(8,128)}), f32[8,8,128]{2,1,0:T(8,128)S(1)}, u32[]{:S(2)}, u32[]{:S(2)}) async-start(f32[8,8,128]{2,1,0:T(8,128)} %squares.1), calls=%async_computation.9 | async-start | bytes 65536 | tf_op jit(solution)/shard_map/norms/all_to_all | solution.py:167

commit v7 on v6

--- a/solution.py
+++ b/solution.py
@@ -37,9 +37,14 @@
 STRIDED = groups_of(
     lambda z, y, x, core: (z % 2, y % 2, x, core), lambda z, y, x, core: (z // 2, y // 2)
 )
-PLANE = groups_of(lambda z, y, x, core: (x, core), lambda z, y, x, core: (z, y))
+FIRST_LINE = groups_of(
+    lambda z, y, x, core: (z if core else y, x, core), lambda z, y, x, core: y if core else z
+)
+SECOND_LINE = groups_of(
+    lambda z, y, x, core: (y if core else z, x, core), lambda z, y, x, core: z if core else y
+)
+COLUMNS = groups_of(lambda z, y, x, core: (z, y), lambda z, y, x, core: (x, core))
 ROW = groups_of(lambda z, y, x, core: (z, y, core), lambda z, y, x, core: x)
-COLUMNS = groups_of(lambda z, y, x, core: (z, y), lambda z, y, x, core: (x, core))
 
 FACTOR_BLOCK = 64
 FACTOR_GROUP = 16
@@ -101,14 +106,26 @@
     return jnp.concatenate(rows, axis=0)
 
 
-def gram_kernel(parts_ref, basis_ref, blocks_ref):
+def gram_kernel(parts_ref, basis_ref, copies_ref, gram_ref):
     basis = (parts_ref[0] + parts_ref[1]) + (parts_ref[2] + parts_ref[3])
     basis_ref[...] = basis
-    gram = jnp.dot(basis.T, basis, precision=HIGHEST, preferred_element_type=jnp.float32)
-    halves_of_row = gram.shape[1] // 128
-    for block in range(blocks_ref.shape[0]):
-        row, col = 8 * (block // halves_of_row), 128 * (block % halves_of_row)
-        blocks_ref[block] = gram[row : row + 8, col : col + 128]
+    half = basis.shape[1] // 2
+    turned = basis.T
+    left = jnp.dot(
+        turned, basis[:, :half], precision=HIGHEST, preferred_element_type=jnp.float32
+    )
+    right = jnp.dot(
+        turned[half:], basis[:, half:], precision=HIGHEST, preferred_element_type=jnp.float32
+    )
+    gram_ref[0 : 2 * half, :] = left
+    gram_ref[2 * half :, :] = right
+    share = half // copies_ref.shape[0]
+    first = pl.multiple_of(lax.axis_index("tp") * share, share)
+    for quarter in range(3):
+        piece = gram_ref[pl.ds(quarter * half + first, share), :]
+        copies_ref[:, quarter * share : (quarter + 1) * share, :] = jnp.broadcast_to(
+            piece[None], (copies_ref.shape[0],) + piece.shape
+        )
 
 
 def copies_kernel(parts_ref, copies_ref):
@@ -117,13 +134,15 @@
 
 def solve_kernel(blocks_ref, basis_ref, ortho_ref, *, share):
     size = basis_ref.shape[1]
-    wide = size // 128
+    height = blocks_ref.shape[1] // 3
+    upper, lower, corner = [
+        jnp.concatenate(
+            [blocks_ref[t, q * height : (q + 1) * height] for t in range(blocks_ref.shape[0])], axis=0
+        )
+        for q in range(3)
+    ]
     gram = jnp.concatenate(
-        [
-            jnp.concatenate([blocks_ref[row * wide + part] for part in range(wide)], axis=1)
-            for row in range(size // 8)
-        ],
-        axis=0,
+        [jnp.concatenate([upper, lower.T], axis=1), jnp.concatenate([lower, corner], axis=1)], axis=0
     )
     source = lax.broadcasted_iota(jnp.int32, (size, size), 0)
     target = lax.broadcasted_iota(jnp.int32, (size, size), 1)
@@ -171,10 +190,6 @@
     return exchange(jnp.broadcast_to(block[None], (len(groups[0]),) + block.shape), groups)
 
 
-def spread_rows(block):
-    return spread(spread(block, STRIDED), NEAR)
-
-
 def add_up(blocks):
     parts = [blocks[i].astype(jnp.float32) for i in range(blocks.shape[0])]
     while len(parts) > 1:
@@ -213,13 +228,10 @@
     return dot(high, selection) + (dot(middle, selection) + dot(low, selection))
 
 
-def blend_kernel(momentum_ref, gradient_ref, blended_ref):
+def basis_kernel(momentum_ref, gradient_ref, factor_ref, blended_ref, basis_ref, *, share):
     blended_ref[...] = (
         momentum_ref[...].astype(jnp.float32) + gradient_ref[...].astype(jnp.float32)
     ).astype(jnp.bfloat16)
-
-
-def basis_kernel(blended_ref, factor_ref, basis_ref, *, share):
     rows = blended_ref.shape[0]
     height, half = factor_ref.shape
     rank = height // 2
@@ -259,7 +271,7 @@
     for column in range(0, half, 128):
         piece = projection_ref[:, column : column + 128].astype(jnp.float32)
         sums = sums + piece * piece
-    totals = nt_dot(jnp.ones((8, 128), jnp.float32), sums, HIGHEST)
+    totals = jnp.sum(sums.T, axis=0, keepdims=True)
     copies_ref[...] = jnp.zeros(copies_ref.shape, jnp.float32)
     for copy in range(copies_ref.shape[0]):
         for piece in range(height // 128):
@@ -296,31 +308,29 @@
     tiles = groups // 4
     rank = share * groups
     with jax.named_scope("factor_gather"):
-        blended = local_call(
-            blend_kernel, "blended", shaped(rows, cols, dtype=jnp.bfloat16), momentum, gradient
-        )
-        strided = spread(halves(right_factor), STRIDED)
-        strided, blended = lax.optimization_barrier((strided, blended))
-        whole_factor = spread(strided, NEAR).reshape(2 * rank, cols // 2)
+        whole_factor = spread(spread(halves(right_factor), STRIDED), NEAR)
+        whole_factor = whole_factor.reshape(2 * rank, cols // 2)
     with jax.named_scope("basis"):
-        part = local_call(
+        blended, part = local_call(
             functools.partial(basis_kernel, share=share),
             "basis_part",
-            shaped(rows, rank),
-            blended, whole_factor,
+            (shaped(rows, cols, dtype=jnp.bfloat16), shaped(rows, rank)),
+            momentum, gradient, whole_factor,
         )
         other_core = [(i, i ^ 1) for i in range(columns)]
         parts = spread(part + lax.ppermute(part, "tp", other_core), ROW)
     with jax.named_scope("gram"):
-        basis, blocks = local_call(
+        shape = (columns, 3 * rank // 2 // columns, rank // 2)
+        basis, copies = local_call(
             gram_kernel,
             "gram_part",
-            (shaped(rows, rank), shaped(groups, 8, rank * rank // groups // 8)),
+            (shaped(rows, rank), shaped(*shape)),
             parts,
-        )
-        parts = exchange(blocks, PLANE)
-        copies = local_call(copies_kernel, "gram_copies", shaped(*parts.shape), parts)
-        blocks = exchange(copies, PLANE)
+            scratch=[pltpu.VMEM((3 * rank // 2, rank // 2), jnp.float32)],
+        )
+        copies = local_call(copies_kernel, "gram_first", shaped(*shape), exchange(copies, FIRST_LINE))
+        copies = local_call(copies_kernel, "gram_second", shaped(*shape), exchange(copies, SECOND_LINE))
+        blocks = exchange(copies, COLUMNS)
     with jax.named_scope("solve"):
         ortho_basis = local_call(
             functools.partial(solve_kernel, share=share),
@@ -337,7 +347,8 @@
         partial = add_up(partial).astype(jnp.bfloat16)
         partial = exchange(partial.reshape(tiles, share, cols), STRIDED)
         own = add_up(partial)
-        projection = spread_rows(halves(own.astype(jnp.bfloat16))).reshape(2 * rank, cols // 2)
+        projection = spread(spread(halves(own.astype(jnp.bfloat16)), STRIDED), NEAR)
+        projection = projection.reshape(2 * rank, cols // 2)
     with jax.named_scope("norms"):
         copies = local_call(squares_kernel, "squares", shaped(columns, 8, 128), projection)
         squares = exchange(copies, COLUMNS)

time: 210 us -> 206 us (0.981)
  blocking collectives: 148 us -> 179 us
  starting transfers between devices: 22.1 us -> 5.63 us
  waiting for transfers between devices: 19.1 us -> 3.65 us
    all_to_all x8 -> x10, blocking collectives: 148 us -> 179 us  [exchange(): lax.all_to_all(blocks, AXES, 0, 0, axis_index_groups=groups, tiled=True)]
    all_to_all x2 -> x1, starting transfers between devices: 19.8 us -> 3.29 us  [exchange(): lax.all_to_all(blocks, AXES, 0, 0, axis_index_groups=groups, tiled=True)]
    all_to_all x2 -> x1, waiting for transfers between devices: 18.1 us -> 2.68 us  [exchange(): lax.all_to_all(blocks, AXES, 0, 0, axis_index_groups=groups, tiled=True)]
  transfers between devices with their start and end apart: 3 -> 2, of which waited for: 3 -> 2; matrix products, arithmetic and copies ran while one was open for 0% -> 0% of each run, Pallas kernels for 1% -> 1%
where the time goes in v7:
time: 206 us; the launch traced here: 205 us
  blocking collectives  179 us (87%)
  Pallas kernels  14.3 us (7%)
  starting transfers between devices  5.63 us (3%)
  waiting for transfers between devices  3.65 us (2%)
    all_to_all x10, blocking collectives, exchange(): lax.all_to_all(blocks, AXES, 0, 0, axis_index_groups=groups, tiled=True)  179 us
    pallas_call x8, Pallas kernels, local_call(): pl.pallas_call(kernel, out_shape=shapes, in_specs=[VMEM] * len(operands),...  14.3 us
  transfers between devices with their start and end apart: 2, of which 2 were waited for; matrix products, arithmetic and copies ran while one was open for 0% of the time, Pallas kernels for 1%

profile of v7, /device:TPU:1, one launch (start us, length us, event | category | flops | bytes accessed | tf_op | source)
XLA Modules:
  0.0 205.4 jit_solution(6399248505846706582)
XLA Ops:
  0.6 0.7 fusion.2
  1.4 32.5 %all_to_all.55 = bf16[16,8,1664]{2,1,0:T(8,128)(2,1)S(1)} all-to-all(bf16[16,8,1664]{2,1,0:T(8,128)(2,1)S(1)} %broadcast_in_dim.10), channel_id=1, replica_groups={{0,16,32,48,128,144,160,176,256,272,288,304,384,400,416,432},{1,17,33,4..., dimensions={0} | all-to-all | bytes 851968 | tf_op jit(solution)/shard_map/factor_gather/all_to_all | solution.py:186
  33.9 0.1 broadcast_in_dim.11
  34.0 0.0 copy-start
  34.0 0.0 copy-start.1
  34.1 17.9 %all_to_all.56 = bf16[4,16,8,1664]{3,2,1,0:T(8,128)(2,1)S(1)} all-to-all(bf16[4,16,8,1664]{3,2,1,0:T(8,128)(2,1)S(1)} %broadcast_in_dim.11), channel_id=1, replica_groups={{0,8,64,72},{1,57,449,505},{2,10,66,74},{3,59,451,507},{4,12,68,76},{5,..., dimensions={0} | all-to-all | bytes 3407872 | tf_op jit(solution)/shard_map/factor_gather/all_to_all | solution.py:186
  52.0 0.0 copy-done
  52.0 0.0 copy-done.1
  52.0 1.2 basis_part.1
  53.1 2.3 %collective-permute-start = (f32[128,256]{1,0:T(8,128)S(1)}, f32[128,256]{1,0:T(8,128)S(1)}, u32[]{:S(2)}, u32[]{:S(2)}) collective-permute-start(f32[128,256]{1,0:T(8,128)S(1)} %get-tuple-element.11), channel_id=1, source_target_pairs={{0,1},{1,0},{2,3},{3,2},{4,5},{5,4},{6,7},{7,6},{8,9},{9,8},{10,11... | collective-permute-start | bytes 393224 | tf_op jit(solution)/shard_map/basis/ppermute | solution.py:321
  55.5 1.0 collective-permute-done
  56.5 12.4 %all_to_all.57.parts_ref = f32[4,128,256]{2,1,0:T(8,128)S(1)} all-to-all(f32[4,128,256]{2,1,0:T(8,128)S(1)} %broadcast_in_dim.12), channel_id=1, replica_groups={{0,2,4,6},{1,3,5,7},{8,10,12,14},{9,11,13,15},{16,18,20,22},{17,19,21,2..., dimensions={0} | all-to-all | bytes 1048576 | tf_op jit(solution)/shard_map/basis/all_to_all | solution.py:186
  68.9 0.4 gram_part.1
  69.3 12.8 %all_to_all.58.parts_ref = f32[8,48,128]{2,1,0:T(8,128)S(1)} all-to-all(f32[8,48,128]{2,1,0:T(8,128)S(1)} %get-tuple-element.12), channel_id=1, replica_groups={{0,64,128,192,256,320,384,448},{1,9,17,25,33,41,49,57},{2,66,130,194,25..., dimensions={0} | all-to-all | bytes 393216 | tf_op jit(solution)/shard_map/gram/all_to_all | solution.py:186
  82.1 13.5 %all_to_all.59.parts_ref = f32[8,48,128]{2,1,0:T(8,128)S(1)} all-to-all(f32[8,48,128]{2,1,0:T(8,128)S(1)} %gram_first.1), channel_id=1, replica_groups={{0,8,16,24,32,40,48,56},{1,65,129,193,257,321,385,449},{2,10,18,26,34,4..., dimensions={0} | all-to-all | bytes 393216 | tf_op jit(solution)/shard_map/gram/all_to_all | solution.py:186
  95.6 12.4 %all_to_all.60.blocks_ref = f32[8,48,128]{2,1,0:T(8,128)S(1)} all-to-all(f32[8,48,128]{2,1,0:T(8,128)S(1)} %gram_second.1), channel_id=1, replica_groups={{0,1,2,3,4,5,6,7},{8,9,10,11,12,13,14,15},{16,17,18,19,20,21,22,23},{24..., dimensions={0} | all-to-all | bytes 393216 | tf_op jit(solution)/shard_map/gram/all_to_all | solution.py:186
  108.1 8.4 %ortho_basis.1.ortho_ref = bf16[128,256]{1,0:T(8,128)(2,1)S(1)} custom-call(f32[8,48,128]{2,1,0:T(8,128)S(1)} %all_to_all.60.blocks_ref, f32[128,256]{1,0:T(8,128)S(1)} %get-tuple-element.13.basis_ref), custom_call_target="tpu_custom_call" | custom-call | flops 1000000000 | bytes 655360 | tf_op jit(solution)/shard_map/solve/ortho_basis/pallas_call | solution.py:169
  116.5 0.6 convolution_convert_fusion
  117.1 17.2 %all_to_all.61 = bf16[4,64,3328]{2,1,0:T(8,128)(2,1)S(1)} all-to-all(bf16[4,64,3328]{2,1,0:T(8,128)(2,1)S(1)} %bitcast.12), channel_id=1, replica_groups={{0,8,64,72},{1,57,449,505},{2,10,66,74},{3,59,451,507},{4,12,68,76},{5,..., dimensions={0} | all-to-all | bytes 3407872 | tf_op jit(solution)/shard_map/projection/all_to_all | solution.py:186
  134.3 0.2 add_convert_fusion
  134.5 0.1 convert_element_type.103
  134.6 20.8 %all_to_all.62 = bf16[16,4,3328]{2,1,0:T(4,128)(2,1)S(1)} all-to-all(bf16[16,4,3328]{2,1,0:T(4,128)(2,1)S(1)} %convert_element_type.103), channel_id=1, replica_groups={{0,16,32,48,128,144,160,176,256,272,288,304,384,400,416,432},{1,17,33,4..., dimensions={0} | all-to-all | bytes 851968 | tf_op jit(solution)/shard_map/projection/all_to_all | solution.py:186
  155.4 0.1 fusion
  155.6 22.2 %all_to_all.63 = bf16[16,8,1664]{2,1,0:T(8,128)(2,1)S(1)} all-to-all(bf16[16,8,1664]{2,1,0:T(8,128)(2,1)S(1)} %broadcast_in_dim.13), channel_id=1, replica_groups={{0,16,32,48,128,144,160,176,256,272,288,304,384,400,416,432},{1,17,33,4..., dimensions={0} | all-to-all | bytes 851968 | tf_op jit(solution)/shard_map/projection/all_to_all | solution.py:186
  177.8 0.1 broadcast_in_dim.14
  177.9 17.2 %all_to_all.64 = bf16[4,16,8,1664]{3,2,1,0:T(8,128)(2,1)S(1)} all-to-all(bf16[4,16,8,1664]{3,2,1,0:T(8,128)(2,1)S(1)} %broadcast_in_dim.14), channel_id=1, replica_groups={{0,8,64,72},{1,57,449,505},{2,10,66,74},{3,59,451,507},{4,12,68,76},{5,..., dimensions={0} | all-to-all | bytes 3407872 | tf_op jit(solution)/shard_map/projection/all_to_all | solution.py:186
  195.1 1.0 squares.1
  196.1 3.3 %all-to-all-start.10 = ((f32[8,8,128]{2,1,0:T(8,128)}), f32[8,8,128]{2,1,0:T(8,128)S(1)}, u32[]{:S(2)}, u32[]{:S(2)}) async-start(f32[8,8,128]{2,1,0:T(8,128)} %squares.1), calls=%async_computation.10 | async-start | bytes 65536 | tf_op jit(solution)/shard_map/norms/all_to_all | solution.py:186
  199.4 1.7 momentum_next.1
  201.1 2.7 %all-to-all-done.10.squares_ref = f32[8,8,128]{2,1,0:T(8,128)S(1)} async-done(((f32[8,8,128]{2,1,0:T(8,128)}), f32[8,8,128]{2,1,0:T(8,128)S(1)}, u32[]{:S(2)}, u32[]{:S(2)}) %all-to-all-start.10) | async-done | bytes 32800 | tf_op jit(solution)/shard_map/norms/all_to_all | solution.py:186
  203.8 1.6 update.1
  (9 shorter events, 0.2 us)
Async XLA Ops:
  34.0 17.9 %copy-start = (bf16[128,3328]{1,0:T(8,128)(2,1)S(1)}, bf16[128,3328]{1,0:T(8,128)(2,1)}, u32[]{:S(2)}) copy-start(bf16[128,3328]{1,0:T(8,128)(2,1)} %momentum_ref.1) | copy-start | bytes 2555908
  34.0 17.9 %copy-start.1 = (bf16[128,3328]{1,0:T(8,128)(2,1)S(1)}, bf16[128,3328]{1,0:T(8,128)(2,1)}, u32[]{:S(2)}) copy-start(bf16[128,3328]{1,0:T(8,128)(2,1)} %gradient_ref.1) | copy-start | bytes 2555908
  53.1 3.3 %collective-permute-start = (f32[128,256]{1,0:T(8,128)S(1)}, f32[128,256]{1,0:T(8,128)S(1)}, u32[]{:S(2)}, u32[]{:S(2)}) collective-permute-start(f32[128,256]{1,0:T(8,128)S(1)} %get-tuple-element.11), channel_id=1, source_target_pairs={{0,1},{1,0},{2,3},{3,2},{4,5},{5,4},{6,7},{7,6},{8,9},{9,8},{10,11... | collective-permute-start | bytes 393224 | tf_op jit(solution)/shard_map/basis/ppermute | solution.py:321
  196.1 7.7 %all-to-all-start.10 = ((f32[8,8,128]{2,1,0:T(8,128)}), f32[8,8,128]{2,1,0:T(8,128)S(1)}, u32[]{:S(2)}, u32[]{:S(2)}) async-start(f32[8,8,128]{2,1,0:T(8,128)} %squares.1), calls=%async_computation.10 | async-start | bytes 65536 | tf_op jit(solution)/shard_map/norms/all_to_all | solution.py:186

commit v8 on v7

--- a/solution.py
+++ b/solution.py
@@ -36,6 +36,14 @@
 )
 STRIDED = groups_of(
     lambda z, y, x, core: (z % 2, y % 2, x, core), lambda z, y, x, core: (z // 2, y // 2)
+)
+SPARSE_FIRST = groups_of(
+    lambda z, y, x, core: (z, y % 2, x, core) if core else (z % 2, y, x, core),
+    lambda z, y, x, core: y if core else z,
+)
+SPARSE_SECOND = groups_of(
+    lambda z, y, x, core: (z % 2, y, x, core) if core else (z, y % 2, x, core),
+    lambda z, y, x, core: z if core else y,
 )
 FIRST_LINE = groups_of(
     lambda z, y, x, core: (z if core else y, x, core), lambda z, y, x, core: y if core else z
@@ -155,7 +163,8 @@
     )
     inverse = jnp.where(source >= target, inverse * scale_row, 0.0)
     ortho = nt_dot(basis_ref[...], inverse, HIGHEST).astype(jnp.bfloat16)
-    selection = (device_of(target // share) * share + target % share == source).astype(jnp.bfloat16)
+    rank_of = device_of(target // share, second_core()) * share + target % share
+    selection = (rank_of == source).astype(jnp.bfloat16)
     ortho_ref[...] = jnp.dot(ortho, selection, preferred_element_type=jnp.float32).astype(
         jnp.bfloat16
     )
@@ -197,11 +206,15 @@
     return parts[0]
 
 
-def device_of(place):
-    parity, tile_index = place // 16, place % 16
-    z = tile_index // 4 * 2 + parity // 2
-    y = tile_index % 4 * 2 + parity % 2
+def device_of(place, swapped=False):
+    parity, first, second = place // 16, place // 4 % 4, place % 4
+    z = jnp.where(swapped, second, first) * 2 + parity // 2
+    y = jnp.where(swapped, first, second) * 2 + parity % 2
     return z * SIDE + y
+
+
+def second_core():
+    return lax.rem(lax.axis_index("tp"), CORES) == 1
 
 
 def nt_dot(a, b, precision=None):
@@ -278,9 +291,29 @@
             copies_ref[copy, piece : piece + 1, :] = totals[0:1, piece * 128 : (piece + 1) * 128]
 
 
-def update_kernel(left_ref, projection_ref, squares_ref, own_ref, out_ref, factor_ref, *, share, scale):
+def swap_lines(pieces, share):
+    lane = lax.broadcasted_iota(jnp.int32, pieces.shape, 1)
+    count = SIDE // 2
+    outer = 2 * count * share
+    distance = lane // outer - lane // share % count
+    result = jnp.where(distance == 0, pieces, 0.0)
+    for step in range(1 - count, count):
+        if step:
+            moved = pltpu.roll(pieces, step * (outer - share) % 128, 1)
+            result = jnp.where(distance == step, moved, result)
+    return result
+
+
+def update_kernel(
+    left_ref, projection_ref, squares_ref, sums_ref, out_ref, factor_ref, *, share, scale
+):
     height, half = projection_ref.shape
-    pieces = jnp.sum(squares_ref[...], axis=0)
+    swapped = second_core()
+    first = jnp.sum(jnp.stack([squares_ref[t] for t in range(0, LINE * CORES, 2)]), axis=0)
+    second = jnp.sum(jnp.stack([squares_ref[t] for t in range(1, LINE * CORES, 2)]), axis=0)
+    pieces = jnp.where(swapped, second, first) + swap_lines(
+        jnp.where(swapped, first, second), factor_ref.shape[0]
+    )
     squares = jnp.concatenate([pieces[i : i + 1] for i in range(height // 128)], axis=1)
     squares = jnp.broadcast_to(squares, (8, height))
     place, part, low = split_row(lax.broadcasted_iota(jnp.int32, (8, height), 1), share)
@@ -295,10 +328,17 @@
         out_ref[:, h * half : (h + 1) * half] = (
             scale * direction[h * rows : (h + 1) * rows]
         ).astype(jnp.bfloat16)
-    mine = (device_of(place) == lax.axis_index("fsdp")) & (part == 0)
-    mine = mine & (low == lax.broadcasted_iota(jnp.int32, (8, height), 0))
+    own_share, device = factor_ref.shape[0], lax.axis_index("fsdp")
+    mine = device_of(place * (share // own_share) + low // own_share, swapped) == device
+    row = lax.broadcasted_iota(jnp.int32, (8, height), 0)
+    mine = mine & (part == 0) & (low % own_share == row)
     own_inverse = jnp.sum(jnp.where(mine, inverse, 0.0), axis=1, keepdims=True)
-    factor_ref[...] = own_ref[...] * own_inverse[0:share]
+    own_line = jnp.where(swapped, lax.div(device, SIDE), lax.rem(device, SIDE))
+    own = jnp.zeros(factor_ref.shape, jnp.float32)
+    for block in range(share // own_share):
+        rows_of_block = sums_ref[block * own_share : (block + 1) * own_share, :]
+        own = jnp.where(lax.div(own_line, 2) == block, rows_of_block, own)
+    factor_ref[...] = own * own_inverse[0:own_share]
 
 
 def body(momentum, gradient, right_factor):
@@ -345,16 +385,18 @@
         ).astype(jnp.bfloat16)
         partial = exchange(partial.reshape(4, tiles * share, cols), NEAR)
         partial = add_up(partial).astype(jnp.bfloat16)
-        partial = exchange(partial.reshape(tiles, share, cols), STRIDED)
-        own = add_up(partial)
-        projection = spread(spread(halves(own.astype(jnp.bfloat16)), STRIDED), NEAR)
-        projection = projection.reshape(2 * rank, cols // 2)
+        lines = SIDE // 2
+        partial = exchange(partial.reshape(lines, lines * share, cols), SPARSE_FIRST)
+        partial = spread(add_up(partial).astype(jnp.bfloat16), SPARSE_SECOND)
+        sums = add_up(partial)
+        strided = spread(halves(sums.astype(jnp.bfloat16)), SPARSE_FIRST)
+        projection = spread(strided, NEAR).reshape(2 * rank, cols // 2)
     with jax.named_scope("norms"):
         copies = local_call(squares_kernel, "squares", shaped(columns, 8, 128), projection)
         squares = exchange(copies, COLUMNS)
     with jax.named_scope("outputs"):
         momentum_next, left = local_call(
-            functools.partial(momentum_kernel, share=share),
+            functools.partial(momentum_kernel, share=lines * share),
             "momentum_next",
             (shaped(rows, cols, dtype=jnp.bfloat16), shaped(2 * rows, 2 * rank, dtype=jnp.bfloat16)),
             ortho_basis, projection, blended,
@@ -362,10 +404,10 @@
         )
         scale = math.sqrt(rows * groups * cols * columns / rank)
         update, factor_next = local_call(
-            functools.partial(update_kernel, share=share, scale=scale),
+            functools.partial(update_kernel, share=lines * share, scale=scale),
             "update",
             (shaped(rows, cols, dtype=jnp.bfloat16), shaped(share, cols)),
-            left, projection, squares, own,
+            left, projection, squares, sums,
             flops=8 * rows * cols * rank,
         )
     return (momentum_next, factor_next, update)

time: 206 us -> 204 us (level)
  blocking collectives: 179 us -> 174 us
  starting transfers between devices: 5.63 us -> 7.79 us
    all_to_all x10 -> x11, blocking collectives: 179 us -> 174 us  [exchange(): lax.all_to_all(blocks, AXES, 0, 0, axis_index_groups=groups, tiled=True)]
    all_to_all x1, starting transfers between devices: 3.29 us -> 5.45 us  [exchange(): lax.all_to_all(blocks, AXES, 0, 0, axis_index_groups=groups, tiled=True)]
where the time goes in v8:
time: 204 us
  blocking collectives  174 us (85%)
  Pallas kernels  14.4 us (7%)
  starting transfers between devices  7.79 us (4%)
  waiting for transfers between devices  4.03 us (2%)
    all_to_all x11, blocking collectives, exchange(): lax.all_to_all(blocks, AXES, 0, 0, axis_index_groups=groups, tiled=True)  174 us
    pallas_call x8, Pallas kernels, local_call(): pl.pallas_call(kernel, out_shape=shapes, in_specs=[VMEM] * len(operands),...  14.4 us
    all_to_all x1, starting transfers between devices, exchange(): lax.all_to_all(blocks, AXES, 0, 0, axis_index_groups=groups, tiled=True)  5.45 us
  transfers between devices with their start and end apart: 2, of which 2 were waited for; matrix products, arithmetic and copies ran while one was open for 0% of the time, Pallas kernels for 1%

profile of v8, /device:TPU:1, one launch (start us, length us, event | category | flops | bytes accessed | tf_op | source)
XLA Modules:
  0.0 203.6 jit_solution(11931073568435597383)
XLA Ops:
  0.6 0.7 fusion.3
  1.4 32.5 %all_to_all.60 = bf16[16,8,1664]{2,1,0:T(8,128)(2,1)S(1)} all-to-all(bf16[16,8,1664]{2,1,0:T(8,128)(2,1)S(1)} %broadcast_in_dim.14), channel_id=1, replica_groups={{0,16,32,48,128,144,160,176,256,272,288,304,384,400,416,432},{1,17,33,4..., dimensions={0} | all-to-all | bytes 851968 | tf_op jit(solution)/shard_map/factor_gather/all_to_all | solution.py:195
  33.9 0.1 broadcast_in_dim.15
  34.0 0.0 copy-start
  34.0 0.0 copy-start.1
  34.1 17.9 %all_to_all.61 = bf16[4,16,8,1664]{3,2,1,0:T(8,128)(2,1)S(1)} all-to-all(bf16[4,16,8,1664]{3,2,1,0:T(8,128)(2,1)S(1)} %broadcast_in_dim.15), channel_id=1, replica_groups={{0,8,64,72},{1,57,449,505},{2,10,66,74},{3,59,451,507},{4,12,68,76},{5,..., dimensions={0} | all-to-all | bytes 3407872 | tf_op jit(solution)/shard_map/factor_gather/all_to_all | solution.py:195
  52.0 0.0 copy-done
  52.0 0.0 copy-done.1
  52.0 1.2 basis_part.1
  53.1 2.3 %collective-permute-start = (f32[128,256]{1,0:T(8,128)S(1)}, f32[128,256]{1,0:T(8,128)S(1)}, u32[]{:S(2)}, u32[]{:S(2)}) collective-permute-start(f32[128,256]{1,0:T(8,128)S(1)} %get-tuple-element.11), channel_id=1, source_target_pairs={{0,1},{1,0},{2,3},{3,2},{4,5},{5,4},{6,7},{7,6},{8,9},{9,8},{10,11... | collective-permute-start | bytes 393224 | tf_op jit(solution)/shard_map/basis/ppermute | solution.py:361
  55.5 1.0 collective-permute-done
  56.5 12.4 %all_to_all.62.parts_ref = f32[4,128,256]{2,1,0:T(8,128)S(1)} all-to-all(f32[4,128,256]{2,1,0:T(8,128)S(1)} %broadcast_in_dim.16), channel_id=1, replica_groups={{0,2,4,6},{1,3,5,7},{8,10,12,14},{9,11,13,15},{16,18,20,22},{17,19,21,2..., dimensions={0} | all-to-all | bytes 1048576 | tf_op jit(solution)/shard_map/basis/all_to_all | solution.py:195
  68.9 0.4 gram_part.1
  69.3 12.8 %all_to_all.63.parts_ref = f32[8,48,128]{2,1,0:T(8,128)S(1)} all-to-all(f32[8,48,128]{2,1,0:T(8,128)S(1)} %get-tuple-element.12), channel_id=1, replica_groups={{0,64,128,192,256,320,384,448},{1,9,17,25,33,41,49,57},{2,66,130,194,25..., dimensions={0} | all-to-all | bytes 393216 | tf_op jit(solution)/shard_map/gram/all_to_all | solution.py:195
  82.1 13.5 %all_to_all.64.parts_ref = f32[8,48,128]{2,1,0:T(8,128)S(1)} all-to-all(f32[8,48,128]{2,1,0:T(8,128)S(1)} %gram_first.1), channel_id=1, replica_groups={{0,8,16,24,32,40,48,56},{1,65,129,193,257,321,385,449},{2,10,18,26,34,4..., dimensions={0} | all-to-all | bytes 393216 | tf_op jit(solution)/shard_map/gram/all_to_all | solution.py:195
  95.6 12.4 %all_to_all.65.blocks_ref = f32[8,48,128]{2,1,0:T(8,128)S(1)} all-to-all(f32[8,48,128]{2,1,0:T(8,128)S(1)} %gram_second.1), channel_id=1, replica_groups={{0,1,2,3,4,5,6,7},{8,9,10,11,12,13,14,15},{16,17,18,19,20,21,22,23},{24..., dimensions={0} | all-to-all | bytes 393216 | tf_op jit(solution)/shard_map/gram/all_to_all | solution.py:195
  108.1 8.4 %ortho_basis.1.ortho_ref = bf16[128,256]{1,0:T(8,128)(2,1)S(1)} custom-call(f32[8,48,128]{2,1,0:T(8,128)S(1)} %all_to_all.65.blocks_ref, f32[128,256]{1,0:T(8,128)S(1)} %get-tuple-element.13.basis_ref), custom_call_target="tpu_custom_call" | custom-call | flops 1000000000 | bytes 655360 | tf_op jit(solution)/shard_map/solve/ortho_basis/pallas_call | solution.py:178
  116.5 0.6 convolution_convert_fusion
  117.1 17.2 %all_to_all.66 = bf16[4,64,3328]{2,1,0:T(8,128)(2,1)S(1)} all-to-all(bf16[4,64,3328]{2,1,0:T(8,128)(2,1)S(1)} %bitcast.15), channel_id=1, replica_groups={{0,8,64,72},{1,57,449,505},{2,10,66,74},{3,59,451,507},{4,12,68,76},{5,..., dimensions={0} | all-to-all | bytes 3407872 | tf_op jit(solution)/shard_map/projection/all_to_all | solution.py:195
  134.3 0.2 add_convert_fusion
  134.5 12.6 %all_to_all.67 = bf16[4,16,3328]{2,1,0:T(8,128)(2,1)S(1)} all-to-all(bf16[4,16,3328]{2,1,0:T(8,128)(2,1)S(1)} %bitcast.16), channel_id=1, replica_groups={{0,128,256,384},{1,17,33,49},{2,130,258,386},{3,19,35,51},{4,132,260,38..., dimensions={0} | all-to-all | bytes 851968 | tf_op jit(solution)/shard_map/projection/all_to_all | solution.py:195
  147.1 0.1 fusion
  147.2 13.1 %all_to_all.68 = bf16[4,16,3328]{2,1,0:T(8,128)(2,1)S(1)} all-to-all(bf16[4,16,3328]{2,1,0:T(8,128)(2,1)S(1)} %broadcast_in_dim.18), channel_id=1, replica_groups={{0,16,32,48},{1,129,257,385},{2,18,34,50},{3,131,259,387},{4,20,36,52},..., dimensions={0} | all-to-all | bytes 851968 | tf_op jit(solution)/shard_map/projection/all_to_all | solution.py:195
  160.4 0.1 fusion.1
  160.5 12.8 %all_to_all.69 = bf16[4,32,1664]{2,1,0:T(8,128)(2,1)S(1)} all-to-all(bf16[4,32,1664]{2,1,0:T(8,128)(2,1)S(1)} %broadcast_in_dim.19), channel_id=1, replica_groups={{0,128,256,384},{1,17,33,49},{2,130,258,386},{3,19,35,51},{4,132,260,38..., dimensions={0} | all-to-all | bytes 851968 | tf_op jit(solution)/shard_map/projection/all_to_all | solution.py:195
  173.3 0.2 broadcast_in_dim.20
  173.5 17.2 %all_to_all.70 = bf16[4,4,32,1664]{3,2,1,0:T(8,128)(2,1)S(1)} all-to-all(bf16[4,4,32,1664]{3,2,1,0:T(8,128)(2,1)S(1)} %broadcast_in_dim.20), channel_id=1, replica_groups={{0,8,64,72},{1,57,449,505},{2,10,66,74},{3,59,451,507},{4,12,68,76},{5,..., dimensions={0} | all-to-all | bytes 3407872 | tf_op jit(solution)/shard_map/projection/all_to_all | solution.py:195
  190.7 1.0 squares.1
  191.7 5.4 %all-to-all-start.11 = ((f32[8,8,128]{2,1,0:T(8,128)}), f32[8,8,128]{2,1,0:T(8,128)S(1)}, u32[]{:S(2)}, u32[]{:S(2)}) async-start(f32[8,8,128]{2,1,0:T(8,128)} %squares.1), calls=%async_computation.11 | async-start | bytes 65536 | tf_op jit(solution)/shard_map/norms/all_to_all | solution.py:195
  197.1 1.7 momentum_next.1
  198.8 3.1 %all-to-all-done.11.squares_ref = f32[8,8,128]{2,1,0:T(8,128)S(1)} async-done(((f32[8,8,128]{2,1,0:T(8,128)}), f32[8,8,128]{2,1,0:T(8,128)S(1)}, u32[]{:S(2)}, u32[]{:S(2)}) %all-to-all-start.11) | async-done | bytes 32800 | tf_op jit(solution)/shard_map/norms/all_to_all | solution.py:195
  201.9 1.7 update.1
  (10 shorter events, 0.2 us)
Async XLA Ops:
  34.0 17.9 %copy-start = (bf16[128,3328]{1,0:T(8,128)(2,1)S(1)}, bf16[128,3328]{1,0:T(8,128)(2,1)}, u32[]{:S(2)}) copy-start(bf16[128,3328]{1,0:T(8,128)(2,1)} %momentum_ref.1) | copy-start | bytes 2555908
  34.0 17.9 %copy-start.1 = (bf16[128,3328]{1,0:T(8,128)(2,1)S(1)}, bf16[128,3328]{1,0:T(8,128)(2,1)}, u32[]{:S(2)}) copy-start(bf16[128,3328]{1,0:T(8,128)(2,1)} %gradient_ref.1) | copy-start | bytes 2555908
  53.1 3.3 %collective-permute-start = (f32[128,256]{1,0:T(8,128)S(1)}, f32[128,256]{1,0:T(8,128)S(1)}, u32[]{:S(2)}, u32[]{:S(2)}) collective-permute-start(f32[128,256]{1,0:T(8,128)S(1)} %get-tuple-element.11), channel_id=1, source_target_pairs={{0,1},{1,0},{2,3},{3,2},{4,5},{5,4},{6,7},{7,6},{8,9},{9,8},{10,11... | collective-permute-start | bytes 393224 | tf_op jit(solution)/shard_map/basis/ppermute | solution.py:361
  191.7 10.2 %all-to-all-start.11 = ((f32[8,8,128]{2,1,0:T(8,128)}), f32[8,8,128]{2,1,0:T(8,128)S(1)}, u32[]{:S(2)}, u32[]{:S(2)}) async-start(f32[8,8,128]{2,1,0:T(8,128)} %squares.1), calls=%async_computation.11 | async-start | bytes 65536 | tf_op jit(solution)/shard_map/norms/all_to_all | solution.py:195

commit v9 on v8

--- a/solution.py
+++ b/solution.py
@@ -237,8 +237,10 @@
     rest = a - high.astype(jnp.float32)
     middle = rest.astype(jnp.bfloat16)
     low = (rest - middle.astype(jnp.float32)).astype(jnp.bfloat16)
-    dot = functools.partial(jnp.dot, preferred_element_type=jnp.float32)
-    return dot(high, selection) + (dot(middle, selection) + dot(low, selection))
+    stacked = jnp.concatenate([high, middle, low], axis=0)
+    product = jnp.dot(stacked, selection, preferred_element_type=jnp.float32)
+    rows = a.shape[0]
+    return product[:rows] + (product[rows : 2 * rows] + product[2 * rows :])
 
 
 def basis_kernel(momentum_ref, gradient_ref, factor_ref, blended_ref, basis_ref, *, share):
@@ -280,10 +282,14 @@
 
 def squares_kernel(projection_ref, copies_ref):
     height, half = projection_ref.shape
-    sums = jnp.zeros((height, 128), jnp.float32)
-    for column in range(0, half, 128):
-        piece = projection_ref[:, column : column + 128].astype(jnp.float32)
-        sums = sums + piece * piece
+    blocks = []
+    for first in range(0, height, 64):
+        block = jnp.zeros((64, 128), jnp.float32)
+        for column in range(0, half, 128):
+            piece = projection_ref[first : first + 64, column : column + 128].astype(jnp.float32)
+            block = block + piece * piece
+        blocks.append(block)
+    sums = jnp.concatenate(blocks, axis=0)
     totals = jnp.sum(sums.T, axis=0, keepdims=True)
     copies_ref[...] = jnp.zeros(copies_ref.shape, jnp.float32)
     for copy in range(copies_ref.shape[0]):

time: 204 us -> 204 us (level)
  no operation moved by 1% of the time
where the time goes in v9:
time: 204 us; the launch traced here: 203 us
  blocking collectives  174 us (85%)
  Pallas kernels  14.2 us (7%)
  starting transfers between devices  7.79 us (4%)
  waiting for transfers between devices  4.03 us (2%)
    all_to_all x11, blocking collectives, exchange(): lax.all_to_all(blocks, AXES, 0, 0, axis_index_groups=groups, tiled=True)  174 us
    pallas_call x8, Pallas kernels, local_call(): pl.pallas_call(kernel, out_shape=shapes, in_specs=[VMEM] * len(operands),...  14.2 us
    all_to_all x1, starting transfers between devices, exchange(): lax.all_to_all(blocks, AXES, 0, 0, axis_index_groups=groups, tiled=True)  5.45 us
  transfers between devices with their start and end apart: 2, of which 2 were waited for; matrix products, arithmetic and copies ran while one was open for 0% of the time, Pallas kernels for 1%

profile of v9, /device:TPU:1, one launch (start us, length us, event | category | flops | bytes accessed | tf_op | source)
XLA Modules:
  0.0 203.4 jit_solution(3140605801067197963)
XLA Ops:
  0.6 0.7 fusion.3
  1.4 32.5 %all_to_all.60 = bf16[16,8,1664]{2,1,0:T(8,128)(2,1)S(1)} all-to-all(bf16[16,8,1664]{2,1,0:T(8,128)(2,1)S(1)} %broadcast_in_dim.14), channel_id=1, replica_groups={{0,16,32,48,128,144,160,176,256,272,288,304,384,400,416,432},{1,17,33,4..., dimensions={0} | all-to-all | bytes 851968 | tf_op jit(solution)/shard_map/factor_gather/all_to_all | solution.py:195
  33.9 0.1 broadcast_in_dim.15
  34.0 0.0 copy-start
  34.0 0.0 copy-start.1
  34.1 17.9 %all_to_all.61 = bf16[4,16,8,1664]{3,2,1,0:T(8,128)(2,1)S(1)} all-to-all(bf16[4,16,8,1664]{3,2,1,0:T(8,128)(2,1)S(1)} %broadcast_in_dim.15), channel_id=1, replica_groups={{0,8,64,72},{1,57,449,505},{2,10,66,74},{3,59,451,507},{4,12,68,76},{5,..., dimensions={0} | all-to-all | bytes 3407872 | tf_op jit(solution)/shard_map/factor_gather/all_to_all | solution.py:195
  52.0 0.0 copy-done
  52.0 0.0 copy-done.1
  52.0 1.0 basis_part.1
  53.0 2.3 %collective-permute-start = (f32[128,256]{1,0:T(8,128)S(1)}, f32[128,256]{1,0:T(8,128)S(1)}, u32[]{:S(2)}, u32[]{:S(2)}) collective-permute-start(f32[128,256]{1,0:T(8,128)S(1)} %get-tuple-element.11), channel_id=1, source_target_pairs={{0,1},{1,0},{2,3},{3,2},{4,5},{5,4},{6,7},{7,6},{8,9},{9,8},{10,11... | collective-permute-start | bytes 393224 | tf_op jit(solution)/shard_map/basis/ppermute | solution.py:367
  55.3 1.0 collective-permute-done
  56.3 12.4 %all_to_all.62.parts_ref = f32[4,128,256]{2,1,0:T(8,128)S(1)} all-to-all(f32[4,128,256]{2,1,0:T(8,128)S(1)} %broadcast_in_dim.16), channel_id=1, replica_groups={{0,2,4,6},{1,3,5,7},{8,10,12,14},{9,11,13,15},{16,18,20,22},{17,19,21,2..., dimensions={0} | all-to-all | bytes 1048576 | tf_op jit(solution)/shard_map/basis/all_to_all | solution.py:195
  68.8 0.4 gram_part.1
  69.2 12.8 %all_to_all.63.parts_ref = f32[8,48,128]{2,1,0:T(8,128)S(1)} all-to-all(f32[8,48,128]{2,1,0:T(8,128)S(1)} %get-tuple-element.12), channel_id=1, replica_groups={{0,64,128,192,256,320,384,448},{1,9,17,25,33,41,49,57},{2,66,130,194,25..., dimensions={0} | all-to-all | bytes 393216 | tf_op jit(solution)/shard_map/gram/all_to_all | solution.py:195
  82.0 13.5 %all_to_all.64.parts_ref = f32[8,48,128]{2,1,0:T(8,128)S(1)} all-to-all(f32[8,48,128]{2,1,0:T(8,128)S(1)} %gram_first.1), channel_id=1, replica_groups={{0,8,16,24,32,40,48,56},{1,65,129,193,257,321,385,449},{2,10,18,26,34,4..., dimensions={0} | all-to-all | bytes 393216 | tf_op jit(solution)/shard_map/gram/all_to_all | solution.py:195
  95.5 12.4 %all_to_all.65.blocks_ref = f32[8,48,128]{2,1,0:T(8,128)S(1)} all-to-all(f32[8,48,128]{2,1,0:T(8,128)S(1)} %gram_second.1), channel_id=1, replica_groups={{0,1,2,3,4,5,6,7},{8,9,10,11,12,13,14,15},{16,17,18,19,20,21,22,23},{24..., dimensions={0} | all-to-all | bytes 393216 | tf_op jit(solution)/shard_map/gram/all_to_all | solution.py:195
  107.9 8.4 %ortho_basis.1.ortho_ref = bf16[128,256]{1,0:T(8,128)(2,1)S(1)} custom-call(f32[8,48,128]{2,1,0:T(8,128)S(1)} %all_to_all.65.blocks_ref, f32[128,256]{1,0:T(8,128)S(1)} %get-tuple-element.13.basis_ref), custom_call_target="tpu_custom_call" | custom-call | flops 1000000000 | bytes 655360 | tf_op jit(solution)/shard_map/solve/ortho_basis/pallas_call | solution.py:178
  116.3 0.6 convolution_convert_fusion
  117.0 17.2 %all_to_all.66 = bf16[4,64,3328]{2,1,0:T(8,128)(2,1)S(1)} all-to-all(bf16[4,64,3328]{2,1,0:T(8,128)(2,1)S(1)} %bitcast.15), channel_id=1, replica_groups={{0,8,64,72},{1,57,449,505},{2,10,66,74},{3,59,451,507},{4,12,68,76},{5,..., dimensions={0} | all-to-all | bytes 3407872 | tf_op jit(solution)/shard_map/projection/all_to_all | solution.py:195
  134.1 0.2 add_convert_fusion
  134.3 12.6 %all_to_all.67 = bf16[4,16,3328]{2,1,0:T(8,128)(2,1)S(1)} all-to-all(bf16[4,16,3328]{2,1,0:T(8,128)(2,1)S(1)} %bitcast.16), channel_id=1, replica_groups={{0,128,256,384},{1,17,33,49},{2,130,258,386},{3,19,35,51},{4,132,260,38..., dimensions={0} | all-to-all | bytes 851968 | tf_op jit(solution)/shard_map/projection/all_to_all | solution.py:195
  147.0 0.1 fusion
  147.1 13.1 %all_to_all.68 = bf16[4,16,3328]{2,1,0:T(8,128)(2,1)S(1)} all-to-all(bf16[4,16,3328]{2,1,0:T(8,128)(2,1)S(1)} %broadcast_in_dim.18), channel_id=1, replica_groups={{0,16,32,48},{1,129,257,385},{2,18,34,50},{3,131,259,387},{4,20,36,52},..., dimensions={0} | all-to-all | bytes 851968 | tf_op jit(solution)/shard_map/projection/all_to_all | solution.py:195
  160.2 0.1 fusion.1
  160.4 12.8 %all_to_all.69 = bf16[4,32,1664]{2,1,0:T(8,128)(2,1)S(1)} all-to-all(bf16[4,32,1664]{2,1,0:T(8,128)(2,1)S(1)} %broadcast_in_dim.19), channel_id=1, replica_groups={{0,128,256,384},{1,17,33,49},{2,130,258,386},{3,19,35,51},{4,132,260,38..., dimensions={0} | all-to-all | bytes 851968 | tf_op jit(solution)/shard_map/projection/all_to_all | solution.py:195
  173.2 0.2 broadcast_in_dim.20
  173.3 17.2 %all_to_all.70 = bf16[4,4,32,1664]{3,2,1,0:T(8,128)(2,1)S(1)} all-to-all(bf16[4,4,32,1664]{3,2,1,0:T(8,128)(2,1)S(1)} %broadcast_in_dim.20), channel_id=1, replica_groups={{0,8,64,72},{1,57,449,505},{2,10,66,74},{3,59,451,507},{4,12,68,76},{5,..., dimensions={0} | all-to-all | bytes 3407872 | tf_op jit(solution)/shard_map/projection/all_to_all | solution.py:195
  190.5 1.0 squares.1
  191.5 5.4 %all-to-all-start.11 = ((f32[8,8,128]{2,1,0:T(8,128)}), f32[8,8,128]{2,1,0:T(8,128)S(1)}, u32[]{:S(2)}, u32[]{:S(2)}) async-start(f32[8,8,128]{2,1,0:T(8,128)} %squares.1), calls=%async_computation.11 | async-start | bytes 65536 | tf_op jit(solution)/shard_map/norms/all_to_all | solution.py:195
  197.0 1.7 momentum_next.1
  198.7 3.1 %all-to-all-done.11.squares_ref = f32[8,8,128]{2,1,0:T(8,128)S(1)} async-done(((f32[8,8,128]{2,1,0:T(8,128)}), f32[8,8,128]{2,1,0:T(8,128)S(1)}, u32[]{:S(2)}, u32[]{:S(2)}) %all-to-all-start.11) | async-done | bytes 32800 | tf_op jit(solution)/shard_map/norms/all_to_all | solution.py:195
  201.7 1.7 update.1
  (10 shorter events, 0.2 us)
Async XLA Ops:
  34.0 17.9 %copy-start = (bf16[128,3328]{1,0:T(8,128)(2,1)S(1)}, bf16[128,3328]{1,0:T(8,128)(2,1)}, u32[]{:S(2)}) copy-start(bf16[128,3328]{1,0:T(8,128)(2,1)} %momentum_ref.1) | copy-start | bytes 2555908
  34.0 17.9 %copy-start.1 = (bf16[128,3328]{1,0:T(8,128)(2,1)S(1)}, bf16[128,3328]{1,0:T(8,128)(2,1)}, u32[]{:S(2)}) copy-start(bf16[128,3328]{1,0:T(8,128)(2,1)} %gradient_ref.1) | copy-start | bytes 2555908
  53.0 3.3 %collective-permute-start = (f32[128,256]{1,0:T(8,128)S(1)}, f32[128,256]{1,0:T(8,128)S(1)}, u32[]{:S(2)}, u32[]{:S(2)}) collective-permute-start(f32[128,256]{1,0:T(8,128)S(1)} %get-tuple-element.11), channel_id=1, source_target_pairs={{0,1},{1,0},{2,3},{3,2},{4,5},{5,4},{6,7},{7,6},{8,9},{9,8},{10,11... | collective-permute-start | bytes 393224 | tf_op jit(solution)/shard_map/basis/ppermute | solution.py:367
  191.5 10.2 %all-to-all-start.11 = ((f32[8,8,128]{2,1,0:T(8,128)}), f32[8,8,128]{2,1,0:T(8,128)S(1)}, u32[]{:S(2)}, u32[]{:S(2)}) async-start(f32[8,8,128]{2,1,0:T(8,128)} %squares.1), calls=%async_computation.11 | async-start | bytes 65536 | tf_op jit(solution)/shard_map/norms/all_to_all | solution.py:195

commit v10 on v9

--- a/solution.py
+++ b/solution.py
@@ -46,10 +46,10 @@
     lambda z, y, x, core: z if core else y,
 )
 FIRST_LINE = groups_of(
-    lambda z, y, x, core: (z if core else y, x, core), lambda z, y, x, core: y if core else z
+    lambda z, y, x, core: (y, x, core), lambda z, y, x, core: z
 )
 SECOND_LINE = groups_of(
-    lambda z, y, x, core: (y if core else z, x, core), lambda z, y, x, core: z if core else y
+    lambda z, y, x, core: (z, x, core), lambda z, y, x, core: y
 )
 COLUMNS = groups_of(lambda z, y, x, core: (z, y), lambda z, y, x, core: (x, core))
 ROW = groups_of(lambda z, y, x, core: (z, y, core), lambda z, y, x, core: x)

time: 204 us -> 204 us (level)
  no operation moved by 1% of the time
where the time goes in v10:
time: 204 us
  blocking collectives  175 us (86%)
  Pallas kernels  14.2 us (7%)
  starting transfers between devices  7.79 us (4%)
  waiting for transfers between devices  4.03 us (2%)
    all_to_all x11, blocking collectives, exchange(): lax.all_to_all(blocks, AXES, 0, 0, axis_index_groups=groups, tiled=True)  175 us
    pallas_call x8, Pallas kernels, local_call(): pl.pallas_call(kernel, out_shape=shapes, in_specs=[VMEM] * len(operands),...  14.2 us
    all_to_all x1, starting transfers between devices, exchange(): lax.all_to_all(blocks, AXES, 0, 0, axis_index_groups=groups, tiled=True)  5.45 us
  transfers between devices with their start and end apart: 2, of which 2 were waited for; matrix products, arithmetic and copies ran while one was open for 0% of the time, Pallas kernels for 1%

profile of v10, /device:TPU:1, one launch (start us, length us, event | category | flops | bytes accessed | tf_op | source)
XLA Modules:
  0.0 203.5 jit_solution(15658388858120460703)
XLA Ops:
  0.6 0.7 fusion.3
  1.4 32.5 %all_to_all.60 = bf16[16,8,1664]{2,1,0:T(8,128)(2,1)S(1)} all-to-all(bf16[16,8,1664]{2,1,0:T(8,128)(2,1)S(1)} %broadcast_in_dim.14), channel_id=1, replica_groups={{0,16,32,48,128,144,160,176,256,272,288,304,384,400,416,432},{1,17,33,4..., dimensions={0} | all-to-all | bytes 851968 | tf_op jit(solution)/shard_map/factor_gather/all_to_all | solution.py:195
  33.9 0.1 broadcast_in_dim.15
  34.0 0.0 copy-start
  34.0 0.0 copy-start.1
  34.1 17.9 %all_to_all.61 = bf16[4,16,8,1664]{3,2,1,0:T(8,128)(2,1)S(1)} all-to-all(bf16[4,16,8,1664]{3,2,1,0:T(8,128)(2,1)S(1)} %broadcast_in_dim.15), channel_id=1, replica_groups={{0,8,64,72},{1,57,449,505},{2,10,66,74},{3,59,451,507},{4,12,68,76},{5,..., dimensions={0} | all-to-all | bytes 3407872 | tf_op jit(solution)/shard_map/factor_gather/all_to_all | solution.py:195
  52.0 0.0 copy-done
  52.0 0.0 copy-done.1
  52.0 1.0 basis_part.1
  53.0 2.3 %collective-permute-start = (f32[128,256]{1,0:T(8,128)S(1)}, f32[128,256]{1,0:T(8,128)S(1)}, u32[]{:S(2)}, u32[]{:S(2)}) collective-permute-start(f32[128,256]{1,0:T(8,128)S(1)} %get-tuple-element.11), channel_id=1, source_target_pairs={{0,1},{1,0},{2,3},{3,2},{4,5},{5,4},{6,7},{7,6},{8,9},{9,8},{10,11... | collective-permute-start | bytes 393224 | tf_op jit(solution)/shard_map/basis/ppermute | solution.py:367
  55.3 1.0 collective-permute-done
  56.3 12.4 %all_to_all.62.parts_ref = f32[4,128,256]{2,1,0:T(8,128)S(1)} all-to-all(f32[4,128,256]{2,1,0:T(8,128)S(1)} %broadcast_in_dim.16), channel_id=1, replica_groups={{0,2,4,6},{1,3,5,7},{8,10,12,14},{9,11,13,15},{16,18,20,22},{17,19,21,2..., dimensions={0} | all-to-all | bytes 1048576 | tf_op jit(solution)/shard_map/basis/all_to_all | solution.py:195
  68.8 0.4 gram_part.1
  69.2 11.9 %all_to_all.63.parts_ref = f32[8,48,128]{2,1,0:T(8,128)S(1)} all-to-all(f32[8,48,128]{2,1,0:T(8,128)S(1)} %get-tuple-element.12), channel_id=1, replica_groups={{0,64,128,192,256,320,384,448},{1,65,129,193,257,321,385,449},{2,66,130..., dimensions={0} | all-to-all | bytes 393216 | tf_op jit(solution)/shard_map/gram/all_to_all | solution.py:195
  81.1 14.3 %all_to_all.64.parts_ref = f32[8,48,128]{2,1,0:T(8,128)S(1)} all-to-all(f32[8,48,128]{2,1,0:T(8,128)S(1)} %gram_first.1), channel_id=1, replica_groups={{0,8,16,24,32,40,48,56},{1,9,17,25,33,41,49,57},{2,10,18,26,34,42,50,58..., dimensions={0} | all-to-all | bytes 393216 | tf_op jit(solution)/shard_map/gram/all_to_all | solution.py:195
  95.3 12.7 %all_to_all.65.blocks_ref = f32[8,48,128]{2,1,0:T(8,128)S(1)} all-to-all(f32[8,48,128]{2,1,0:T(8,128)S(1)} %gram_second.1), channel_id=1, replica_groups={{0,1,2,3,4,5,6,7},{8,9,10,11,12,13,14,15},{16,17,18,19,20,21,22,23},{24..., dimensions={0} | all-to-all | bytes 393216 | tf_op jit(solution)/shard_map/gram/all_to_all | solution.py:195
  108.0 8.4 %ortho_basis.1.ortho_ref = bf16[128,256]{1,0:T(8,128)(2,1)S(1)} custom-call(f32[8,48,128]{2,1,0:T(8,128)S(1)} %all_to_all.65.blocks_ref, f32[128,256]{1,0:T(8,128)S(1)} %get-tuple-element.13.basis_ref), custom_call_target="tpu_custom_call" | custom-call | flops 1000000000 | bytes 655360 | tf_op jit(solution)/shard_map/solve/ortho_basis/pallas_call | solution.py:178
  116.4 0.6 convolution_convert_fusion
  117.0 17.2 %all_to_all.66 = bf16[4,64,3328]{2,1,0:T(8,128)(2,1)S(1)} all-to-all(bf16[4,64,3328]{2,1,0:T(8,128)(2,1)S(1)} %bitcast.15), channel_id=1, replica_groups={{0,8,64,72},{1,57,449,505},{2,10,66,74},{3,59,451,507},{4,12,68,76},{5,..., dimensions={0} | all-to-all | bytes 3407872 | tf_op jit(solution)/shard_map/projection/all_to_all | solution.py:195
  134.2 0.2 add_convert_fusion
  134.4 12.6 %all_to_all.67 = bf16[4,16,3328]{2,1,0:T(8,128)(2,1)S(1)} all-to-all(bf16[4,16,3328]{2,1,0:T(8,128)(2,1)S(1)} %bitcast.16), channel_id=1, replica_groups={{0,128,256,384},{1,17,33,49},{2,130,258,386},{3,19,35,51},{4,132,260,38..., dimensions={0} | all-to-all | bytes 851968 | tf_op jit(solution)/shard_map/projection/all_to_all | solution.py:195
  147.1 0.1 fusion
  147.2 12.6 %all_to_all.68 = bf16[4,16,3328]{2,1,0:T(8,128)(2,1)S(1)} all-to-all(bf16[4,16,3328]{2,1,0:T(8,128)(2,1)S(1)} %broadcast_in_dim.18), channel_id=1, replica_groups={{0,16,32,48},{1,129,257,385},{2,18,34,50},{3,131,259,387},{4,20,36,52},..., dimensions={0} | all-to-all | bytes 851968 | tf_op jit(solution)/shard_map/projection/all_to_all | solution.py:195
  159.8 0.1 fusion.1
  159.9 13.3 %all_to_all.69 = bf16[4,32,1664]{2,1,0:T(8,128)(2,1)S(1)} all-to-all(bf16[4,32,1664]{2,1,0:T(8,128)(2,1)S(1)} %broadcast_in_dim.19), channel_id=1, replica_groups={{0,128,256,384},{1,17,33,49},{2,130,258,386},{3,19,35,51},{4,132,260,38..., dimensions={0} | all-to-all | bytes 851968 | tf_op jit(solution)/shard_map/projection/all_to_all | solution.py:195
  173.3 0.2 broadcast_in_dim.20
  173.4 17.2 %all_to_all.70 = bf16[4,4,32,1664]{3,2,1,0:T(8,128)(2,1)S(1)} all-to-all(bf16[4,4,32,1664]{3,2,1,0:T(8,128)(2,1)S(1)} %broadcast_in_dim.20), channel_id=1, replica_groups={{0,8,64,72},{1,57,449,505},{2,10,66,74},{3,59,451,507},{4,12,68,76},{5,..., dimensions={0} | all-to-all | bytes 3407872 | tf_op jit(solution)/shard_map/projection/all_to_all | solution.py:195
  190.6 1.0 squares.1
  191.6 5.5 %all-to-all-start.11 = ((f32[8,8,128]{2,1,0:T(8,128)}), f32[8,8,128]{2,1,0:T(8,128)S(1)}, u32[]{:S(2)}, u32[]{:S(2)}) async-start(f32[8,8,128]{2,1,0:T(8,128)} %squares.1), calls=%async_computation.11 | async-start | bytes 65536 | tf_op jit(solution)/shard_map/norms/all_to_all | solution.py:195
  197.1 1.7 momentum_next.1
  198.7 3.1 %all-to-all-done.11.squares_ref = f32[8,8,128]{2,1,0:T(8,128)S(1)} async-done(((f32[8,8,128]{2,1,0:T(8,128)}), f32[8,8,128]{2,1,0:T(8,128)S(1)}, u32[]{:S(2)}, u32[]{:S(2)}) %all-to-all-start.11) | async-done | bytes 32800 | tf_op jit(solution)/shard_map/norms/all_to_all | solution.py:195
  201.8 1.7 update.1
  (10 shorter events, 0.2 us)
Async XLA Ops:
  34.0 17.9 %copy-start = (bf16[128,3328]{1,0:T(8,128)(2,1)S(1)}, bf16[128,3328]{1,0:T(8,128)(2,1)}, u32[]{:S(2)}) copy-start(bf16[128,3328]{1,0:T(8,128)(2,1)} %momentum_ref.1) | copy-start | bytes 2555908
  34.0 17.9 %copy-start.1 = (bf16[128,3328]{1,0:T(8,128)(2,1)S(1)}, bf16[128,3328]{1,0:T(8,128)(2,1)}, u32[]{:S(2)}) copy-start(bf16[128,3328]{1,0:T(8,128)(2,1)} %gradient_ref.1) | copy-start | bytes 2555908
  53.0 3.3 %collective-permute-start = (f32[128,256]{1,0:T(8,128)S(1)}, f32[128,256]{1,0:T(8,128)S(1)}, u32[]{:S(2)}, u32[]{:S(2)}) collective-permute-start(f32[128,256]{1,0:T(8,128)S(1)} %get-tuple-element.11), channel_id=1, source_target_pairs={{0,1},{1,0},{2,3},{3,2},{4,5},{5,4},{6,7},{7,6},{8,9},{9,8},{10,11... | collective-permute-start | bytes 393224 | tf_op jit(solution)/shard_map/basis/ppermute | solution.py:367
  191.6 10.2 %all-to-all-start.11 = ((f32[8,8,128]{2,1,0:T(8,128)}), f32[8,8,128]{2,1,0:T(8,128)S(1)}, u32[]{:S(2)}, u32[]{:S(2)}) async-start(f32[8,8,128]{2,1,0:T(8,128)} %squares.1), calls=%async_computation.11 | async-start | bytes 65536 | tf_op jit(solution)/shard_map/norms/all_to_all | solution.py:195
